TPU v7x, 256 devices: a whole 4x4x8 slice. The times are simulated.
256 devices in a mesh: dp: 32 (over x, y, core), mp: 8 (over z).
Axes of the slice: x: 4, y: 4, z: 8, core: 2. Of those that a mesh axis runs over, the one named last changes fastest.
Arguments:
- layer_input: bfloat16 [1024, 8192], P('dp'), may hold values from -12 to 12
- output_grad: bfloat16 [1024, 8192], P('dp'), may hold values from -24 to 24
- gate_pre: bfloat16 [1024, 32768], P('dp', 'mp'), may hold values from -4 to 4
- up_pre: bfloat16 [1024, 32768], P('dp', 'mp'), may hold values from -10 to 10
- hidden_grad: bfloat16 [1024, 32768], P('dp', 'mp'), may hold values from -22 to 22
- row_gate: float32 [8192], P('dp'), may hold values from 0.01 to 0.3
- col_gate: float32 [32768], P('mp'), may hold values from 0.01 to 0.3
- row_up: float32 [8192], P('dp'), may hold values from 0.01 to 0.3
- col_up: float32 [32768], P('mp'), may hold values from 0.01 to 0.3
- row_down: float32 [32768], P('mp'), may hold values from 0.01 to 0.3
- col_down: float32 [8192], P('dp'), may hold values from 0.01 to 0.3
Outputs:
- step_gate: bfloat16 [8192, 32768], P('dp', 'mp')
- step_up: bfloat16 [8192, 32768], P('dp', 'mp')
- step_down: bfloat16 [32768, 8192], P('mp', 'dp')
- new_row_gate: float32 [8192], P('dp')
- new_col_gate: float32 [32768], P('mp')
- new_row_up: float32 [8192], P('dp')
- new_col_up: float32 [32768], P('mp')
- new_row_down: float32 [32768], P('mp')
- new_col_down: float32 [8192], P('dp')
All inputs are finite; a program needn't handle non-finite values.
Results may differ from a plain program's by a relative error of at most 0.0053.
Values may be sent and summed in bfloat16 or wider, within the bound.
No kernel may reach another device: no remote copies, remote signals or barrier semaphores. Data moves between devices by JAX's collectives and lax.ppermute only.
A program may use at most 128 MiB of HBM per device.

v0:
```python
import math

import jax
import jax.numpy as jnp
from jax import lax
from jax.sharding import PartitionSpec as P

D = 8192
FF = 32768
STEP = 8


eps_square = 1e-30


def derive(gate_pre, up_pre, hidden_grad):
    first = gate_pre.astype(jnp.float32)
    second = up_pre.astype(jnp.float32)
    cotangent = hidden_grad.astype(jnp.float32)
    sigma = jax.nn.sigmoid(first)
    gate_cot = (cotangent * second * sigma * (1.0 + first * (1.0 - sigma))).astype(jnp.bfloat16)
    up_cot = (cotangent * first * sigma).astype(jnp.bfloat16)
    hidden = (first * sigma * second).astype(jnp.bfloat16)
    return (gate_cot, up_cot, hidden)


def contract(left, right):
    return lax.dot_general(
        left, right, (((0,), (0,)), ((), ())), preferred_element_type=jnp.float32
    )


def refresh(old, total, count):
    beta = 1.0 - float(STEP) ** (-0.8)
    return beta * old + (1.0 - beta) * (total / count + eps_square)


def normalize(grad, new_row, new_col):
    return grad * lax.rsqrt(new_row)[:, None] * lax.rsqrt(new_col)[None, :]


def finish(normed, squares):
    spread = jnp.sqrt(squares / (D * FF))
    return (normed / jnp.maximum(1.0, spread)).astype(jnp.bfloat16)


def local(
    layer_input,
    output_grad,
    gate_pre,
    up_pre,
    hidden_grad,
    row_gate,
    col_gate,
    row_up,
    col_up,
    row_down,
    col_down,
):
    input_cols, outgrad_cols = (
        lax.all_to_all(layer_input, "dp", split_axis=1, concat_axis=0, tiled=True),
        lax.all_to_all(output_grad, "dp", split_axis=1, concat_axis=0, tiled=True),
    )
    total = input_cols.shape[0]
    factor = 1.0 / math.sqrt(total)
    local_gate, local_up, local_hidden = derive(gate_pre, up_pre, hidden_grad)
    sum_gate = contract(input_cols, lax.all_gather(local_gate, "dp", axis=0, tiled=True))
    sum_up = contract(input_cols, lax.all_gather(local_up, "dp", axis=0, tiled=True))
    sum_down = contract(lax.all_gather(local_hidden, "dp", axis=0, tiled=True), outgrad_cols)
    grad_gate = sum_gate * factor
    grad_up = sum_up * factor
    grad_down = sum_down * factor
    square_gate = grad_gate * grad_gate
    square_up = grad_up * grad_up
    square_down = grad_down * grad_down
    width_gate, width_up, width_down = lax.psum(
        (jnp.sum(square_gate, axis=1), jnp.sum(square_up, axis=1), jnp.sum(square_down, axis=0)),
        "mp",
    )
    new_row_gate = refresh(row_gate, width_gate, FF)
    new_row_up = refresh(row_up, width_up, FF)
    new_col_down = refresh(col_down, width_down, FF)
    span_gate, span_up, span_down = lax.psum(
        (jnp.sum(square_gate, axis=0), jnp.sum(square_up, axis=0), jnp.sum(square_down, axis=1)),
        "dp",
    )
    new_col_gate = refresh(col_gate, span_gate, D)
    new_col_up = refresh(col_up, span_up, D)
    new_row_down = refresh(row_down, span_down, D)
    normed_gate = normalize(grad_gate, new_row_gate, new_col_gate)
    normed_up = normalize(grad_up, new_row_up, new_col_up)
    normed_down = normalize(grad_down, new_row_down, new_col_down)
    squares_gate, squares_up, squares_down = lax.psum(
        (
            jnp.sum(normed_gate * normed_gate),
            jnp.sum(normed_up * normed_up),
            jnp.sum(normed_down * normed_down),
        ),
        ("dp", "mp"),
    )
    step_gate = finish(normed_gate, squares_gate)
    step_up = finish(normed_up, squares_up)
    step_down = finish(normed_down, squares_down)
    return (
        step_gate,
        step_up,
        step_down,
        new_row_gate,
        new_col_gate,
        new_row_up,
        new_col_up,
        new_row_down,
        new_col_down,
    )


def solution(mesh):
    return jax.shard_map(
        local,
        mesh=mesh,
        in_specs=(
            P("dp", None),
            P("dp", None),
            P("dp", "mp"),
            P("dp", "mp"),
            P("dp", "mp"),
            P("dp"),
            P("mp"),
            P("dp"),
            P("mp"),
            P("mp"),
            P("dp"),
        ),
        out_specs=(
            P("dp", "mp"),
            P("dp", "mp"),
            P("mp", "dp"),
            P("dp"),
            P("mp"),
            P("dp"),
            P("mp"),
            P("mp"),
            P("dp"),
        ),
        check_vma=False,
    )
```

profile of v0, /device:TPU:1, one launch (start us, length us, event | category | flops | bytes accessed | tf_op | source)
XLA Modules:
  0.0 449.0 jit_solution(11502092146266429168)
XLA Ops:
  7.2 2.3 fusion.11
  11.1 1.9 copy.37
  13.0 8.6 %all-to-all-start = ((bf16[32,32,256]{2,0,1:T(8,128)(2,1)}), bf16[32,32,256]{2,0,1:T(8,128)(2,1)S(1)}, u32[]{:S(2)}, u32[]{:S(2)}) async-start(bf16[32,32,256]{2,0,1:T(8,128)(2,1)} %bitcast.23), calls=%async_computation | async-start | bytes 1048576 | tf_op jit(solution)/shard_map/all_to_all | solution.py:61
  21.6 0.9 copy.36
  22.4 10.8 %all-to-all-done = bf16[32,32,256]{2,0,1:T(8,128)(2,1)S(1)} async-done(((bf16[32,32,256]{2,0,1:T(8,128)(2,1)}), bf16[32,32,256]{2,0,1:T(8,128)(2,1)S(1)}, u32[]{:S(2)}, u32[]{:S(2)}) %all-to-all-start) | async-done | bytes 524320 | tf_op jit(solution)/shard_map/all_to_all | solution.py:61
  33.2 3.7 all-to-all-start.1
  36.9 37.3 %all-gather.4.cloned.1.call-done = bf16[1024,4096]{1,0:T(8,128)(2,1)} async-done(((bf16[32,4096]{1,0:T(8,128)(2,1)}), bf16[1024,4096]{1,0:T(8,128)(2,1)}) %all-gather.4.cloned.1.call-update) | async-done | bytes 8388624 | tf_op jit(solution)/shard_map/all_gather | solution.py:67
  74.2 8.2 %fusion.1 = (f32[256]{0:T(256)S(1)}, f32[4096]{0:T(1024)S(1)}, f32[4096,256]{1,0:T(8,128)}) fusion(bf16[1024,4096]{1,0:T(8,128)(2,1)} %all-gather.4.cloned.1.call-done, bf16[1024,256]{1,0:T(8,128)(2,1)S(1)} %bitcast.27), kind=kOutput, calls=%fused_computation.13 | convolution fusion | flops 2151673600 | bytes 13124608 | tf_op jit(solution)/shard_map/dot_general | solution.py:28
  82.4 52.0 %all-gather.6.cloned.1.call-done = bf16[1024,4096]{1,0:T(8,128)(2,1)} async-done(((bf16[32,4096]{1,0:T(8,128)(2,1)}), bf16[1024,4096]{1,0:T(8,128)(2,1)}) %all-gather.6.cloned.1.call-update) | async-done | bytes 8388624 | tf_op jit(solution)/shard_map/all_gather | solution.py:68
  134.3 8.1 %fusion.3 = (f32[256]{0:T(256)S(1)}, f32[4096]{0:T(1024)S(1)}, f32[4096,256]{1,0:T(8,128)}) fusion(bf16[1024,4096]{1,0:T(8,128)(2,1)} %all-gather.6.cloned.1.call-done, bf16[1024,256]{1,0:T(8,128)(2,1)S(1)} %bitcast.28), kind=kOutput, calls=%fused_computation.15 | convolution fusion | flops 2151673600 | bytes 13124608 | tf_op jit(solution)/shard_map/dot_general | solution.py:28
  142.5 52.6 %all-gather.8.cloned.1.call-done = bf16[1024,4096]{1,0:T(8,128)(2,1)} async-done(((bf16[32,4096]{1,0:T(8,128)(2,1)}), bf16[1024,4096]{1,0:T(8,128)(2,1)}) %all-gather.8.cloned.1.call-update) | async-done | bytes 8388624 | tf_op jit(solution)/shard_map/all_gather | solution.py:69
  195.1 8.2 %fusion.5 = (f32[4096]{0:T(1024)S(1)}, f32[256]{0:T(256)S(1)}, f32[4096,256]{1,0:T(8,128)}) fusion(bf16[1024,4096]{1,0:T(8,128)(2,1)} %all-gather.8.cloned.1.call-done, bf16[1024,256]{1,0:T(8,128)(2,1)S(1)} %bitcast.26), kind=kOutput, calls=%fused_computation.17 | convolution fusion | flops 2151673600 | bytes 13124608 | tf_op jit(solution)/shard_map/dot_general | solution.py:28
  203.3 14.0 %all-reduce.2 = (f32[256]{0:T(256)S(1)}, f32[256]{0:T(256)S(1)}, f32[256]{0:T(256)S(1)}) all-reduce(f32[256]{0:T(256)S(1)} %get-tuple-element.49, f32[256]{0:T(256)S(1)} %get-tuple-element.47, f32[256]{0:T(256)S(1)} %get-tuple-element.46), channel_id=1, replica_groups=mesh['dp'=32,'mp'=8] {'mp'}, use_global_device_ids=true, to_apply=%region_1.0 | all-reduce | flops 768 | bytes 6144 | tf_op jit(solution)/shard_map/psum | solution.py:76
  217.9 122.2 %all-reduce.1 = (f32[4096]{0:T(1024)S(1)}, f32[4096]{0:T(1024)S(1)}, f32[4096]{0:T(1024)S(1)}) all-reduce(f32[4096]{0:T(1024)S(1)} %get-tuple-element.50, f32[4096]{0:T(1024)S(1)} %get-tuple-element.48, f32[4096]{0:T(1024)S(1)} %get-tuple-element.45), channel_id=1, replica_groups=mesh['dp'=32,'mp'=8] {'dp'}, use_global_device_ids=true, to_apply=%region_3.0 | all-reduce | flops 12288 | bytes 98304 | tf_op jit(solution)/shard_map/psum | solution.py:83
  341.2 3.6 multiply_reduce_fusion.2
  345.4 1.9 multiply_reduce_fusion.1
  347.3 1.8 multiply_reduce_fusion
  349.2 76.3 %all-reduce = (f32[]{:T(128)}, f32[]{:T(128)}, f32[]{:T(128)}) all-reduce(f32[]{:T(128)} %multiply_reduce_fusion.2, f32[]{:T(128)} %multiply_reduce_fusion.1, f32[]{:T(128)} %multiply_reduce_fusion), channel_id=1, replica_groups=mesh['dp'=32,'mp'=8] {'dp','mp'}, use_global_device_ids=true, to_apply=%region_5.0 | all-reduce | flops 3 | bytes 24 | tf_op jit(solution)/shard_map/psum | solution.py:93
  427.5 2.7 fusion.6
  430.9 1.7 fusion.7
  432.6 1.3 copy-done.3
  433.9 1.7 divide_convert_fusion
  435.6 4.1 copy.31
  439.6 2.8 copy.30
  (32 shorter events, 4.6 us)
Async XLA Ops:
  7.2 14.4 %copy-start.4 = (bf16[32,8192]{1,0:T(8,128)(2,1)S(1)}, bf16[32,8192]{1,0:T(8,128)(2,1)}, u32[]{:S(2)}) copy-start(bf16[32,8192]{1,0:T(8,128)(2,1)} %param.12) | copy-start | bytes 1572868
  7.2 67.0 %all-gather.4.cloned.1.call-start = ((), (), s32[]{:S(2)}) async-start(), calls=%async_computation.2 | async-start | bytes 8650752 | tf_op jit(solution)/shard_map/all_gather | solution.py:67
  9.6 124.7 %all-gather.6.cloned.1.call-start = ((), (), s32[]{:S(2)}) async-start(), calls=%async_computation.3 | async-start | bytes 8650752 | tf_op jit(solution)/shard_map/all_gather | solution.py:68
  10.3 184.7 %all-gather.8.cloned.1.call-start = ((), (), s32[]{:S(2)}) async-start(), calls=%async_computation.4 | async-start | bytes 8650752 | tf_op jit(solution)/shard_map/all_gather | solution.py:69
  13.0 20.2 %all-to-all-start = ((bf16[32,32,256]{2,0,1:T(8,128)(2,1)}), bf16[32,32,256]{2,0,1:T(8,128)(2,1)S(1)}, u32[]{:S(2)}, u32[]{:S(2)}) async-start(bf16[32,32,256]{2,0,1:T(8,128)(2,1)} %bitcast.23), calls=%async_computation | async-start | bytes 1048576 | tf_op jit(solution)/shard_map/all_to_all | solution.py:61
  33.2 109.3 %all-to-all-start.1 = ((bf16[32,32,256]{2,0,1:T(8,128)(2,1)}), bf16[32,32,256]{2,0,1:T(8,128)(2,1)S(1)}, u32[]{:S(2)}, u32[]{:S(2)}) async-start(bf16[32,32,256]{2,0,1:T(8,128)(2,1)} %bitcast.22), calls=%async_computation.1 | async-start | bytes 1048576 | tf_op jit(solution)/shard_map/all_to_all | solution.py:62
  195.1 22.2 %copy-start.8 = (f32[256]{0:T(256)S(1)}, f32[256]{0:T(256)}, u32[]{:S(2)}) copy-start(f32[256]{0:T(256)} %param.21) | copy-start | bytes 3076
  195.1 145.0 %copy-start.5 = (f32[4096]{0:T(1024)S(1)}, f32[4096]{0:T(1024)}, u32[]{:S(2)}) copy-start(f32[4096]{0:T(1024)} %param.17) | copy-start | bytes 49156
  195.1 145.6 %copy-start.9 = (f32[256]{0:T(256)S(1)}, f32[256]{0:T(256)}, u32[]{:S(2)}) copy-start(f32[256]{0:T(256)} %param.18) | copy-start | bytes 3076
  195.1 145.6 %copy-start.10 = (f32[256]{0:T(256)S(1)}, f32[256]{0:T(256)}, u32[]{:S(2)}) copy-start(f32[256]{0:T(256)} %param.16) | copy-start | bytes 3076
  203.3 141.5 %copy-start.6 = (f32[4096]{0:T(1024)S(1)}, f32[4096]{0:T(1024)}, u32[]{:S(2)}) copy-start(f32[4096]{0:T(1024)} %param.20) | copy-start | bytes 49156
  203.3 141.5 %copy-start.7 = (f32[4096]{0:T(1024)S(1)}, f32[4096]{0:T(1024)}, u32[]{:S(2)}) copy-start(f32[4096]{0:T(1024)} %param.19) | copy-start | bytes 49156
  340.0 5.4 %copy-start = (f32[4096,256]{1,0:T(8,128)S(1)}, f32[4096,256]{1,0:T(8,128)}, u32[]{:S(2)}) copy-start(f32[4096,256]{1,0:T(8,128)} %get-tuple-element.76) | copy-start | bytes 12582916
  341.2 6.1 %copy-start.2 = (f32[4096,256]{1,0:T(8,128)S(1)}, f32[4096,256]{1,0:T(8,128)}, u32[]{:S(2)}) copy-start(f32[4096,256]{1,0:T(8,128)} %get-tuple-element.77) | copy-start | bytes 12582916
  427.5 3.5 copy-start.1
  430.9 2.9 copy-start.3
Sparse Core Ops, SparseCore 0:
  10.6 63.5 all-gather.3
  76.7 57.5 all-gather.5
  137.5 57.5 all-gather.7
where the time goes:
time: 450 us; the launch traced here: 449 us
  blocking collectives  212 us (47%)
  waiting for transfers between devices  154 us (34%)
  matrix products  24.6 us (5%)
  other arithmetic  18.1 us (4%)
  between operations  15.9 us (4%)
  starting transfers between devices  12.4 us (3%)
  local copies, waits for them, and re-layouts  11.7 us (3%)
    psum x1, blocking collectives, local(): lax.psum((jnp.sum(square_gate, axis=0), jnp.sum(square_up, axis=0), jnp.s...  122 us
    psum x1, blocking collectives, local(): lax.psum((jnp.sum(normed_gate * normed_gate), jnp.sum(normed_up * normed_...  76.3 us
    all_gather x1, waiting for transfers between devices, local(): lax.all_gather(local_hidden, 'dp', axis=0, tiled=True)  52.6 us
    all_gather x1, waiting for transfers between devices, local(): lax.all_gather(local_up, 'dp', axis=0, tiled=True)  52 us
    all_gather x1, waiting for transfers between devices, local(): lax.all_gather(local_gate, 'dp', axis=0, tiled=True)  37.3 us
    dot_general x3, matrix products, contract(): lax.dot_general(left, right, (((0,), (0,)), ((), ())), preferred_element_...  24.6 us
    psum x1, blocking collectives, local(): lax.psum((jnp.sum(square_gate, axis=1), jnp.sum(square_up, axis=1), jnp.s...  14 us
    all_to_all x1, waiting for transfers between devices, local(): lax.all_to_all(layer_input, 'dp', split_axis=1, concat_axis=0, tiled=True)  10.8 us
  transfers between devices with their start and end apart: 5, of which 4 were waited for; matrix products, arithmetic and copies ran while one was open for 4% of the time, Pallas kernels for 0%

commit v1 on v0

v1 whole, which is shorter than its diff:
```python
import jax
import jax.numpy as jnp
from jax import lax
from jax.experimental import pallas as pl
from jax.experimental.pallas import tpu as pltpu
from jax.sharding import Mesh, PartitionSpec as P

D = 8192
FF = 32768
STEP = 8
TOKENS = 1024

EPS = 1e-30
BETA = 1.0 - float(STEP) ** (-0.8)
XN, YN, CN, ZN = 4, 4, 2, 8
ROWS = D // (XN * YN * CN)
COLS = FF // ZN
HALF = COLS // 2
QUART = HALF // 2
LOCAL = TOKENS // (XN * YN * CN)
VMEM = 12 * 1024 * 1024
SCALE = 1.0 / TOKENS
ORDER = (0, 3, 1, 2)


def derive(gate_pre, up_pre, hidden_grad):
    first = gate_pre.astype(jnp.float32)
    second = up_pre.astype(jnp.float32)
    cotangent = hidden_grad.astype(jnp.float32)
    sigma = jax.nn.sigmoid(first)
    gate_cot = (cotangent * second * sigma * (1.0 + first * (1.0 - sigma))).astype(jnp.bfloat16)
    up_cot = (cotangent * first * sigma).astype(jnp.bfloat16)
    hidden = (first * sigma * second).astype(jnp.bfloat16)
    return jnp.stack((gate_cot, up_cot, hidden))


def shift(value, axis, size, step):
    return lax.ppermute(value, axis, [(i, (i + step) % size) for i in range(size)])


def swap(value):
    return shift(value, "c", CN, 1)


def neighbours(value, axis):
    return shift(value, axis, 4, 1), shift(value, axis, 4, 3)


def here(*values):
    return [pltpu.with_memory_space_constraint(v, pltpu.VMEM) for v in values]


def whole(kernel, name, outs, operands, flops=0, scratch=()):
    size = sum(v.size * v.dtype.itemsize for v in operands)
    spec = pl.BlockSpec(memory_space=pltpu.VMEM)
    return pl.pallas_call(
        kernel,
        in_specs=[spec] * len(operands),
        out_specs=[spec] * len(outs),
        out_shape=[pltpu.VMEM(shape, dtype) for shape, dtype in outs],
        scratch_shapes=list(scratch),
        compiler_params=pltpu.CompilerParams(vmem_limit_bytes=VMEM),
        cost_estimate=pl.CostEstimate(flops=flops, bytes_accessed=size, transcendentals=0),
        name=name,
    )(*here(*operands))


def halve_kernel(*refs):
    for i in range(4):
        half = refs[4 + i].shape[0]
        refs[4 + i][...] = refs[i][i % 2 * half : (i % 2 + 1) * half]


def relay(pairs, axes):
    arrived = [v for pair in pairs for v in pair]
    outs = [((v.shape[0] // 2,) + v.shape[1:], v.dtype) for v in arrived]
    halves = whole(halve_kernel, "halve", outs, arrived)
    return [(shift(halves[2 * r], axis, 4, 1), shift(halves[2 * r + 1], axis, 4, 3)) for r, axis in enumerate(axes)]


def spread(value, axes, count):
    sent = jnp.broadcast_to(value[None], (count,) + value.shape)
    return lax.all_to_all(sent, axes, split_axis=0, concat_axis=0, tiled=True)


def join_kernel(*refs):
    for route in range(2):
        own, left, right, low, high = refs[5 * route : 5 * route + 5]
        line = refs[10 + route]
        for block, ref in enumerate((own, left, right)):
            line[block] = ref[...]
        line[3, 0] = low[0]
        line[3, 1] = high[0]


def join(blocks):
    return whole(join_kernel, "join", [((4, CN, 3, LOCAL, QUART), jnp.bfloat16)] * 2, blocks)


def pick_kernel(z_ref, first_ref, second_ref, out_ref):
    z = z_ref[0]
    for array, ref in enumerate((first_ref, second_ref)):

        @pl.when(z // 4 == array)
        def _():
            for chip in range(XN * YN):
                start = pl.multiple_of(chip * 2 * ROWS + lax.rem(z, 4) * 128, 128)
                out_ref[chip] = ref[:, pl.ds(start, 128)]


def pick(z, first, second):
    spec = pl.BlockSpec(memory_space=pltpu.VMEM)
    return pl.pallas_call(
        pick_kernel,
        in_specs=[pl.BlockSpec(memory_space=pltpu.SMEM), spec, spec],
        out_specs=spec,
        out_shape=jax.ShapeDtypeStruct((XN * YN, LOCAL, 128), jnp.bfloat16),
        compiler_params=pltpu.CompilerParams(vmem_limit_bytes=VMEM),
        cost_estimate=pl.CostEstimate(flops=0, bytes_accessed=1 << 20, transcendentals=0),
        name="pick",
    )(z, *here(first, second))


def start_kernel(*refs):
    features, parts, total_ref, line = refs[:4], refs[4:10], refs[10], refs[11]
    depth = line.shape[1]
    tile = line.shape[2]
    for m in range(3):
        for step in range(QUART // tile):
            units = slice(step * tile, (step + 1) * tile)
            for route in range(2):
                x_ref = features[m // 2 * 2 + route]
                size = depth // 3
                for i, ref in enumerate(parts[3 * route : 3 * route + 3]):
                    line[route, i * size : (i + 1) * size] = ref[:, :, m, :, units].reshape(size, tile)
                for i in range(2):
                    rows = slice(i * ROWS, (i + 1) * ROWS)
                    total_ref[m, route, rows, units] = jnp.dot(
                        x_ref[rows, :depth], line[route], preferred_element_type=jnp.float32
                    )


def start(features, parts):
    outs = [((3, 2, 2 * ROWS, QUART), jnp.float32)]
    depth = TOKENS * 3 // 4
    scratch = [pltpu.VMEM((2, depth, QUART // 2), jnp.bfloat16)]
    return whole(start_kernel, "start", outs, (*features, *parts), 3 * 4 * ROWS * HALF * depth, scratch)[0]


def multiply_kernel(*refs):
    features, total_ref, parts = refs[:4], refs[4], refs[5:9]
    keep_ref, send_ref, rows_ref, cols_ref, line = refs[9:]
    depth = line.shape[1]
    tile = line.shape[2]
    for m in range(3):
        across = [jnp.zeros((ROWS, 128), jnp.float32) for _ in range(2)]
        for step in range(QUART // tile):
            units = slice(step * tile, (step + 1) * tile)
            for route in range(2):
                x_ref = features[m // 2 * 2 + route]
                size = depth // 2
                for i, ref in enumerate(parts[2 * route : 2 * route + 2]):
                    line[route, i * size : (i + 1) * size] = ref[:, :, m, :, units].reshape(size, tile)
                down = jnp.zeros((1, tile), jnp.float32)
                for i, out_ref in enumerate((keep_ref, send_ref)):
                    rows = slice(i * ROWS, (i + 1) * ROWS)
                    last = jnp.dot(x_ref[rows, TOKENS - depth :], line[route], preferred_element_type=jnp.float32)
                    grad = total_ref[m, route, rows, units] + last
                    out_ref[m, route, :, units] = grad.astype(jnp.bfloat16)
                    square = grad * grad
                    down += jnp.sum(square, axis=0, keepdims=True)
                    for k in range(tile // 128):
                        across[i] += square[:, k * 128 : (k + 1) * 128]
                for k in range(tile // 128):
                    row = step * (tile // 128) + k
                    cols_ref[m, route, row : row + 1, :] = down[:, k * 128 : (k + 1) * 128] * SCALE
        for i, total in enumerate(across):
            rows_ref[m, i : i + 1] = jnp.sum(total.T, axis=0, keepdims=True) * SCALE


def multiply(features, total, parts):
    outs = [
        ((3, 2, ROWS, QUART), jnp.bfloat16),
        ((3, 2, ROWS, QUART), jnp.bfloat16),
        ((3, 2, ROWS), jnp.float32),
        ((3, 2, 8, 128), jnp.float32),
    ]
    depth = TOKENS // 4
    scratch = [pltpu.VMEM((2, depth, QUART // 2), jnp.bfloat16)]
    return whole(multiply_kernel, "multiply", outs, (*features, total, *parts), 3 * 4 * ROWS * HALF * depth, scratch)


def weigh_kernel(mine_ref, other_ref, keep_ref, got_ref, out_ref):
    for m in range(3):
        total = jnp.zeros((ROWS, 128), jnp.float32)
        for ref, inverse_ref in ((keep_ref, mine_ref), (got_ref, other_ref)):
            for route in range(2):
                for k in range(8):
                    at = (m * 2 + route) * 8 + k
                    grad = ref[m, route, :, k * 128 : (k + 1) * 128].astype(jnp.float32)
                    total += grad * grad * inverse_ref[at : at + 1]
        out_ref[m : m + 1] = jnp.sum(total.T, axis=0, keepdims=True) * SCALE


def weigh(*operands):
    return whole(weigh_kernel, "weigh", [((3, ROWS), jnp.float32)], operands, 12 * ROWS * COLS)[0]


def finish_kernel(core_ref, width_ref, mine_ref, other_ref, keep_ref, got_ref, *refs):
    outs, bufs, sem = refs[:3], refs[3:6], refs[6]
    core = core_ref[0]
    copies = []
    for m in range(3):
        width = jnp.broadcast_to(width_ref[m : m + 1], (128, ROWS)).T
        for ref, unit_ref, at in ((keep_ref, mine_ref, core), (got_ref, other_ref, 1 - core)):
            for route in range(2):
                first = at * HALF + route * QUART
                for k in range(8):
                    row = (m * 2 + route) * 8 + k
                    grad = ref[m, route, :, k * 128 : (k + 1) * 128].astype(jnp.float32)
                    normed = (grad * width * unit_ref[row : row + 1]).astype(jnp.bfloat16)
                    place = pl.ds(pl.multiple_of(first + k * 128, 128), 128)
                    if m < 2:
                        bufs[m][:, place] = normed
                    else:
                        bufs[m][place, :] = normed.T
                part = pl.ds(pl.multiple_of(first, QUART), QUART)
                ends = [v.at[:, part] if m < 2 else v.at[part] for v in (bufs[m], outs[m])]
                copies.append(pltpu.make_async_copy(*ends, sem.at[len(copies)]))
                copies[-1].start()
    for copy in copies:
        copy.wait()


def finish(core, *operands):
    spec = pl.BlockSpec(memory_space=pltpu.VMEM)
    wide, tall = (ROWS, COLS), (COLS, ROWS)
    operands = here(*operands)
    return pl.pallas_call(
        finish_kernel,
        in_specs=[pl.BlockSpec(memory_space=pltpu.SMEM)] + [spec] * len(operands),
        out_specs=[pl.BlockSpec(memory_space=pl.ANY)] * 3,
        out_shape=[jax.ShapeDtypeStruct(shape, jnp.bfloat16) for shape in (wide, wide, tall)],
        scratch_shapes=[pltpu.VMEM(shape, jnp.bfloat16) for shape in (wide, wide, tall)]
        + [pltpu.SemaphoreType.DMA((12,))],
        compiler_params=pltpu.CompilerParams(vmem_limit_bytes=2 * VMEM),
        cost_estimate=pl.CostEstimate(flops=12 * ROWS * COLS, bytes_accessed=12 << 20, transcendentals=0),
        name="finish",
    )(core, *operands)


def arrange_kernel(place_ref, mine_ref, other_ref, *outs):
    x, y, core = place_ref[0], place_ref[1], place_ref[2]
    for array in range(2):
        for part in range(4):
            column = array * 4 + lax.rem(core + part // 2, 2) * 2 + part % 2
            rows = slice(part * 128, (part + 1) * 128)
            for route in range(2):
                for outer in range(4):
                    blocks = []
                    for inner in range(4):
                        dx, dy = (ORDER[outer], ORDER[inner]) if route else (ORDER[inner], ORDER[outer])
                        source = lax.rem(x + dx, XN) * YN + lax.rem(y + dy, YN)
                        blocks += [mine_ref[column, source], other_ref[column, source]]
                    tokens = slice(outer * 256, (outer + 1) * 256)
                    outs[array * 2 + route][rows, tokens] = jnp.concatenate(blocks).T


def arrange(place, mine, other):
    spec = pl.BlockSpec(memory_space=pltpu.VMEM)
    return pl.pallas_call(
        arrange_kernel,
        in_specs=[pl.BlockSpec(memory_space=pltpu.SMEM), spec, spec],
        out_specs=[spec] * 4,
        out_shape=[pltpu.VMEM((2 * ROWS, TOKENS), jnp.bfloat16)] * 4,
        compiler_params=pltpu.CompilerParams(vmem_limit_bytes=VMEM),
        cost_estimate=pl.CostEstimate(flops=0, bytes_accessed=6 << 20, transcendentals=0),
        name="arrange",
    )(place, *here(mine, other))


def local(
    layer_input,
    output_grad,
    gate_pre,
    up_pre,
    hidden_grad,
    row_gate,
    col_gate,
    row_up,
    col_up,
    row_down,
    col_down,
):
    x, y, c, z = (lax.axis_index(name) for name in ("x", "y", "c", "z"))
    core = c.astype(jnp.int32).reshape(1)
    place = jnp.stack((x, y, c)).astype(jnp.int32)

    def halves(at):
        return derive(*(lax.dynamic_slice_in_dim(v, at * HALF, HALF, 1) for v in (gate_pre, up_pre, hidden_grad)))

    got = swap(halves(1 - c))
    own = jnp.stack((halves(c), got))
    own_a, own_b = own[..., :QUART], own[..., QUART:]
    near = [neighbours(own_a, "x"), neighbours(own_b, "y")]

    chosen = pick(z.astype(jnp.int32).reshape(1), layer_input, output_grad)
    chosen = lax.all_to_all(chosen, ("x", "y"), split_axis=0, concat_axis=0, tiled=True)
    near, chosen = lax.optimization_barrier((near, chosen))
    far = relay(near, ("x", "y"))
    chosen = lax.all_gather(chosen, "z")
    lines = join([own_a, *near[0], *far[0], own_b, *near[1], *far[1]])

    near = [neighbours(line, axis) for line, axis in zip(lines, ("y", "x"))]
    far = relay(near, ("y", "x"))
    features = arrange(place, chosen, swap(chosen))
    parts = [lines[0], *near[0], lines[1], *near[1]]
    keep, send, rows, cols = multiply(features, start(features, parts), [*far[0], *far[1]])

    rows = rows[:, 0] + swap(rows[:, 1])
    cols = cols.reshape(48, 128)
    got = swap(send)

    span = jnp.sum(spread(cols, ("x", "y"), XN * YN), axis=0)
    old = jnp.stack((col_gate, col_up, row_down)).reshape(3, CN, 16, 128)
    old = lax.dynamic_index_in_dim(old, c, 1, keepdims=False).reshape(48, 128)
    new_span = BETA * old + (1.0 - BETA) * (span / D + EPS)
    other_span = swap(new_span)

    weighted = weigh(1.0 / new_span, 1.0 / other_span, keep, got)
    both = jnp.sum(spread(jnp.concatenate((rows, weighted)), ("z",), ZN), axis=0)
    new_width = BETA * jnp.stack((row_gate, row_up, col_down)) + (1.0 - BETA) * (both[:3] / FF + EPS)
    squares = jnp.sum(both[3:] / new_width, axis=1, keepdims=True)
    squares = jnp.sum(spread(jnp.broadcast_to(squares, (3, 128)), ("x", "y", "c"), XN * YN * CN), axis=0)[:, :1]
    scale = (1.0 / 32.0) / jnp.maximum(1.0, jnp.sqrt(squares / (D * FF)))
    width = lax.rsqrt(new_width) * scale
    step_gate, step_up, step_down = finish(
        core,
        width,
        lax.rsqrt(new_span),
        lax.rsqrt(other_span),
        keep,
        got,
    )
    mine, other = new_span.reshape(3, HALF), other_span.reshape(3, HALF)
    columns = jnp.where(c == 0, jnp.concatenate((mine, other), 1), jnp.concatenate((other, mine), 1))
    return (
        step_gate,
        step_up,
        step_down,
        new_width[0],
        columns[0],
        new_width[1],
        columns[1],
        columns[2],
        new_width[2],
    )


def solution(mesh):
    grid = Mesh(mesh.devices.reshape(XN, YN, CN, ZN), ("x", "y", "c", "z"))
    dp = ("x", "y", "c")
    return jax.shard_map(
        local,
        mesh=grid,
        in_specs=(
            P(dp, None),
            P(dp, None),
            P(dp, "z"),
            P(dp, "z"),
            P(dp, "z"),
            P(dp),
            P("z"),
            P(dp),
            P("z"),
            P("z"),
            P(dp),
        ),
        out_specs=(
            P(dp, "z"),
            P(dp, "z"),
            P("z", dp),
            P(dp),
            P("z"),
            P(dp),
            P("z"),
            P("z"),
            P(dp),
        ),
        check_vma=False,
    )
```

time: 450 us -> 173 us (0.38)
  blocking collectives: 212 us -> 9.96 us
  waiting for transfers between devices: 154 us -> 53.2 us
  starting transfers between devices: 12.4 us -> 56 us
  Pallas kernels: 0 us -> 31.1 us
  matrix products: 24.6 us -> 0 us
  other arithmetic: 18.1 us -> 3.34 us
  local copies, waits for them, and re-layouts: 11.7 us -> 4.65 us
    psum x3 -> x0, blocking collectives: 212 us -> none  [the longest x1 122 us: local(): lax.psum((jnp.sum(square_gate, axis=0), jnp.sum(square_up, axis=0), jnp.s...]
    all_gather x3 -> x1, waiting for transfers between devices: 142 us -> 19.7 us  [local(): chosen = lax.all_gather(chosen, 'z')]
    ppermute x0 -> x21, starting transfers between devices: none -> 38.9 us  [shift(): lax.ppermute(value, axis, [(i, (i + step) % size) for i in range(size)])]
    pallas_call x0 -> x9, Pallas kernels: none -> 31.1 us  [the longest x6 23.1 us: whole(): pl.pallas_call(kernel, in_specs=[spec] * len(operands), out_specs=[spec]...]
    dot_general x3 -> x0, matrix products: 24.6 us -> none  [contract(): lax.dot_general(left, right, (((0,), (0,)), ((), ())), preferred_element_...]
    ppermute x0 -> x21, waiting for transfers between devices: none -> 12.3 us  [shift(): lax.ppermute(value, axis, [(i, (i + step) % size) for i in range(size)])]
    all_to_all x2 -> x3, waiting for transfers between devices: 10.8 us -> 21.3 us  [spread(): return lax.all_to_all(sent, axes, split_axis=0, concat_axis=0, tiled=True)]
    all_to_all x0 -> x1, blocking collectives: none -> 9.96 us  [local(): lax.all_to_all(chosen, ('x', 'y'), split_axis=0, concat_axis=0, tiled=True)]
  transfers between devices with their start and end apart: 5 -> 25, of which waited for: 4 -> 12; matrix products, arithmetic and copies ran while one was open for 4% -> 2% of each run, Pallas kernels for 0% -> 9%
where the time goes in v1:
time: 173 us
  starting transfers between devices  56 us (32%)
  waiting for transfers between devices  53.2 us (31%)
  Pallas kernels  31.1 us (18%)
  between operations  14.4 us (8%)
  blocking collectives  9.96 us (6%)
  local copies, waits for them, and re-layouts  4.65 us (3%)
  other arithmetic  3.34 us (2%)
    ppermute x21, starting transfers between devices, shift(): lax.ppermute(value, axis, [(i, (i + step) % size) for i in range(size)])  38.9 us
    pallas_call x6, Pallas kernels, whole(): pl.pallas_call(kernel, in_specs=[spec] * len(operands), out_specs=[spec]...  23.1 us
    all_to_all x3, waiting for transfers between devices, spread(): return lax.all_to_all(sent, axes, split_axis=0, concat_axis=0, tiled=True)  21.3 us
    all_gather x1, waiting for transfers between devices, local(): chosen = lax.all_gather(chosen, 'z')  19.7 us
    all_to_all x3, starting transfers between devices, spread(): return lax.all_to_all(sent, axes, split_axis=0, concat_axis=0, tiled=True)  17 us
    ppermute x21, waiting for transfers between devices, shift(): lax.ppermute(value, axis, [(i, (i + step) % size) for i in range(size)])  12.3 us
    all_to_all x1, blocking collectives, local(): lax.all_to_all(chosen, ('x', 'y'), split_axis=0, concat_axis=0, tiled=True)  9.96 us
    pallas_call x1, Pallas kernels, finish(): pl.pallas_call(finish_kernel, in_specs=[pl.BlockSpec(memory_space=pltpu.S...  5.54 us
  transfers between devices with their start and end apart: 25, of which 12 were waited for; matrix products, arithmetic and copies ran while one was open for 2% of the time, Pallas kernels for 9%

profile of v1, /device:TPU:1, one launch (start us, length us, event | category | flops | bytes accessed | tf_op | source)
XLA Modules:
  0.0 172.5 jit_solution(13785763999296581732)
XLA Ops:
  8.9 3.3 %collective-permute-start = (bf16[3,32,2048]{2,1,0:T(8,128)(2,1)S(1)}, bf16[3,32,2048]{2,1,0:T(8,128)(2,1)S(1)}, u32[]{:S(2)}, u32[]{:S(2)}) collective-permute-start(bf16[3,32,2048]{2,1,0:T(8,128)(2,1)S(1)} %pad_maximum_fusion.1), channel_id=1, source_target_pairs={{0,8},{8,0},{1,9},{9,1},{2,10},{10,2},{3,11},{11,3},{4,12},{12,4},... | collective-permute-start | bytes 1179656 | tf_op jit(solution)/shard_map/ppermute | solution.py:38
  13.8 2.7 %collective-permute-start.2 = (bf16[2,3,32,1024]{3,2,1,0:T(8,128)(2,1)S(1)}, bf16[2,3,32,1024]{3,2,1,0:T(8,128)(2,1)S(1)}, u32[]{:S(2)}, u32[]{:S(2)}) collective-permute-start(bf16[2,3,32,1024]{3,2,1,0:T(8,128)(2,1)S(1)} %get-tuple-element.66.refs_0_), channel_id=1, source_target_pairs={{0,192},{64,0},{128,64},{192,128},{1,193},{65,1},{129,65},{193,129... | collective-permute-start | bytes 1179656 | tf_op jit(solution)/shard_map/ppermute | solution.py:38
  16.4 2.7 %collective-permute-start.4 = (bf16[2,3,32,1024]{3,2,1,0:T(8,128)(2,1)S(1)}, bf16[2,3,32,1024]{3,2,1,0:T(8,128)(2,1)S(1)}, u32[]{:S(2)}, u32[]{:S(2)}) collective-permute-start(bf16[2,3,32,1024]{3,2,1,0:T(8,128)(2,1)S(1)} %get-tuple-element.65.refs_5_), channel_id=1, source_target_pairs={{0,48},{16,0},{32,16},{48,32},{1,49},{17,1},{33,17},{49,33},{2,50}... | collective-permute-start | bytes 1179656 | tf_op jit(solution)/shard_map/ppermute | solution.py:38
  19.2 10.0 %all_to_all.20 = bf16[16,32,128]{2,1,0:T(8,128)(2,1)} all-to-all(bf16[16,32,128]{2,1,0:T(8,128)(2,1)S(1)} %pick.1), channel_id=1, replica_groups=mesh['x'=4,'y'=4,'c'=2,'z'=8] {'x','y'}, dimensions={0} | all-to-all | bytes 262144 | tf_op jit(solution)/shard_map/all_to_all | solution.py:308
  35.0 3.0 %collective-permute-done.8.refs_8_ = bf16[1,3,32,1024]{3,2,1,0:T(8,128)(2,1)S(1)} collective-permute-done((bf16[1,3,32,1024]{3,2,1,0:T(8,128)(2,1)S(1)}, bf16[1,3,32,1024]{3,2,1,0:T(8,128)(2,1)S(1)}, u32[]{:S(2)}, u32[]{:S(2)}) %collective-permute-start.8) | collective-permute-done | bytes 196640 | tf_op jit(solution)/shard_map/ppermute | solution.py:38
  39.9 2.7 %collective-permute-start.11 = (bf16[4,2,3,32,1024]{4,3,2,1,0:T(8,128)(2,1)}, bf16[4,2,3,32,1024]{4,3,2,1,0:T(8,128)(2,1)S(1)}, u32[]{:S(2)}, u32[]{:S(2)}) collective-permute-start(bf16[4,2,3,32,1024]{4,3,2,1,0:T(8,128)(2,1)} %get-tuple-element.48.refs_4_), channel_id=1, source_target_pairs={{0,48},{16,0},{32,16},{48,32},{1,49},{17,1},{33,17},{49,33},{2,50}... | collective-permute-start | bytes 4718600 | tf_op jit(solution)/shard_map/ppermute | solution.py:38
  42.5 2.7 %collective-permute-start.13 = (bf16[4,2,3,32,1024]{4,3,2,1,0:T(8,128)(2,1)}, bf16[4,2,3,32,1024]{4,3,2,1,0:T(8,128)(2,1)}, u32[]{:S(2)}, u32[]{:S(2)}) collective-permute-start(bf16[4,2,3,32,1024]{4,3,2,1,0:T(8,128)(2,1)} %get-tuple-element.49.refs_7_), channel_id=1, source_target_pairs={{0,192},{64,0},{128,64},{192,128},{1,193},{65,1},{129,65},{193,129... | collective-permute-start | bytes 4718600 | tf_op jit(solution)/shard_map/ppermute | solution.py:38
  45.2 19.7 %all-gather.3.cloned.1.call-done = bf16[128,32,128]{2,1,0:T(8,128)(2,1)} async-done(((bf16[16,32,128]{2,1,0:T(8,128)(2,1)}), bf16[128,32,128]{2,1,0:T(8,128)(2,1)}) %all-gather.3.cloned.1.call-update) | async-done | bytes 1048592 | tf_op jit(solution)/shard_map/all_gather | solution.py:311
  64.9 4.8 %collective-permute-start.5 = (bf16[8,16,32,128]{3,2,1,0:T(8,128)(2,1)}, bf16[8,16,32,128]{3,2,1,0:T(8,128)(2,1)}, u32[]{:S(2)}, u32[]{:S(2)}) collective-permute-start(bf16[8,16,32,128]{3,2,1,0:T(8,128)(2,1)} %bitcast.47), channel_id=1, source_target_pairs={{0,8},{8,0},{1,9},{9,1},{2,10},{10,2},{3,11},{11,3},{4,12},{12,4},... | collective-permute-start | bytes 3145736 | tf_op jit(solution)/shard_map/ppermute | solution.py:38
  69.7 3.5 %collective-permute-done.10.refs_5_.refs_0_ = bf16[4,2,3,32,1024]{4,3,2,1,0:T(8,128)(2,1)S(1)} collective-permute-done((bf16[4,2,3,32,1024]{4,3,2,1,0:T(8,128)(2,1)}, bf16[4,2,3,32,1024]{4,3,2,1,0:T(8,128)(2,1)S(1)}, u32[]{:S(2)}, u32[]{:S(2)}) %collective-permute-start.10) | collective-permute-done | bytes 1572896 | tf_op jit(solution)/shard_map/ppermute | solution.py:38
  75.4 3.6 %halve.3 = (bf16[2,2,3,32,1024]{4,3,2,1,0:T(8,128)(2,1)}, bf16[2,2,3,32,1024]{4,3,2,1,0:T(8,128)(2,1)}, bf16[2,2,3,32,1024]{4,3,2,1,0:T(8,128)(2,1)}, bf16[2,2,3,32,1024]{4,3,2,1,0:T(8,128)(2,1)}) custom-call(bf16[4,2,3,32,1024]{4,3,2,1,0:T(8,128)(2,1)S(1)} %collective-permute-done.10.refs_5_.refs_0_, ...), custom_call_target="tpu_custom_call" | custom-call | bytes 6291456 | tf_op jit(solution)/shard_map/halve/pallas_call | solution.py:56
  79.0 2.7 %collective-permute-start.15 = (bf16[2,2,3,32,1024]{4,3,2,1,0:T(8,128)(2,1)}, bf16[2,2,3,32,1024]{4,3,2,1,0:T(8,128)(2,1)}, u32[]{:S(2)}, u32[]{:S(2)}) collective-permute-start(bf16[2,2,3,32,1024]{4,3,2,1,0:T(8,128)(2,1)} %get-tuple-element.51), channel_id=1, source_target_pairs={{0,48},{16,0},{32,16},{48,32},{1,49},{17,1},{33,17},{49,33},{2,50}... | collective-permute-start | bytes 2359304 | tf_op jit(solution)/shard_map/ppermute | solution.py:38
  81.7 2.7 %collective-permute-start.17 = (bf16[2,2,3,32,1024]{4,3,2,1,0:T(8,128)(2,1)}, bf16[2,2,3,32,1024]{4,3,2,1,0:T(8,128)(2,1)}, u32[]{:S(2)}, u32[]{:S(2)}) collective-permute-start(bf16[2,2,3,32,1024]{4,3,2,1,0:T(8,128)(2,1)} %get-tuple-element.53), channel_id=1, source_target_pairs={{0,192},{64,0},{128,64},{192,128},{1,193},{65,1},{129,65},{193,129... | collective-permute-start | bytes 2359304 | tf_op jit(solution)/shard_map/ppermute | solution.py:38
  88.1 7.9 %start.1.refs_4_ = f32[3,2,512,1024]{3,2,1,0:T(8,128)S(1)} custom-call(bf16[512,1024]{1,0:T(8,128)(2,1)S(1)} %get-tuple-element.36.refs_0_, bf16[512,1024]{1,0:T(8,128)(2,1)S(1)} %get-tuple-element.37.refs_1_, bf16[512,1024]{1,0:T(8,128)(2,1)S(1)} %get-tuple-element.38.refs_2_, bf16[512,1024]{1,0:T(8,128)(2,1)S(1)} %get-tuple-element.39.refs_3_, ...), custom_call_target="tpu_custom_call" | custom-call | flops 4831838208 | bytes 13631488 | tf_op jit(solution)/shard_map/start/pallas_call | solution.py:56
  96.2 6.1 %multiply.6 = (bf16[3,2,256,1024]{3,2,1,0:T(8,128)(2,1)S(1)}, bf16[3,2,256,1024]{3,2,1,0:T(8,128)(2,1)}, f32[3,2,256]{2,1,0:T(2,128)S(1)}, f32[3,2,8,128]{3,2,1,0:T(8,128)S(1)}) custom-call(bf16[512,1024]{1,0:T(8,128)(2,1)S(1)} %get-tuple-element.36.refs_0_, bf16[512,1024]{1,0:T(8,128)(2,1)S(1)} %get-tuple-element.37.refs_1_, ...), custom_call_target="tpu_custom_call" | custom-call | flops 1610612736 | bytes 19922944 | tf_op jit(solution)/shard_map/multiply/pallas_call | solution.py:56
  102.3 7.0 %collective-permute-start.20 = (bf16[3,2,256,1024]{3,2,1,0:T(8,128)(2,1)}, bf16[3,2,256,1024]{3,2,1,0:T(8,128)(2,1)}, u32[]{:S(2)}, u32[]{:S(2)}) collective-permute-start(bf16[3,2,256,1024]{3,2,1,0:T(8,128)(2,1)} %get-tuple-element.57), channel_id=1, source_target_pairs={{0,8},{8,0},{1,9},{9,1},{2,10},{10,2},{3,11},{11,3},{4,12},{12,4},... | collective-permute-start | bytes 9437192 | tf_op jit(solution)/shard_map/ppermute | solution.py:38
  110.0 4.2 %all-to-all-start.1 = ((f32[16,48,128]{2,1,0:T(8,128)}), f32[16,48,128]{2,1,0:T(8,128)}, u32[]{:S(2)}, u32[]{:S(2)}) async-start(f32[16,48,128]{2,1,0:T(8,128)} %broadcast_in_dim.7), calls=%async_computation.1 | async-start | bytes 786432 | tf_op jit(solution)/shard_map/all_to_all | solution.py:83
  115.5 7.9 %all-to-all-done.1 = f32[16,48,128]{2,1,0:T(8,128)} async-done(((f32[16,48,128]{2,1,0:T(8,128)}), f32[16,48,128]{2,1,0:T(8,128)}, u32[]{:S(2)}, u32[]{:S(2)}) %all-to-all-start.1) | async-done | bytes 393248 | tf_op jit(solution)/shard_map/all_to_all | solution.py:83
  127.3 3.6 %weigh.1 = f32[3,256]{1,0:T(4,128)S(1)} custom-call(f32[48,128]{1,0:T(8,128)S(1)} %broadcast_divide_fusion.1.mine_ref, f32[48,128]{1,0:T(8,128)S(1)} %get-tuple-element.78.other_ref, bf16[3,2,256,1024]{3,2,1,0:T(8,128)(2,1)S(1)} %get-tuple-element.56.keep_ref, bf16[3,2,256,1024]{3,2,1,0:T(8,128)(2,1)} %collective-permute-done.20.got_ref), custom_call_target="tpu_custom_call" | custom-call | flops 12582912 | bytes 6340608 | tf_op jit(solution)/shard_map/weigh/pallas_call | solution.py:56
  131.6 7.3 %all-to-all-start.2 = ((f32[8,6,256]{2,1,0:T(8,128)}), f32[8,6,256]{2,1,0:T(8,128)S(1)}, u32[]{:S(2)}, u32[]{:S(2)}) async-start(f32[8,6,256]{2,1,0:T(8,128)} %broadcast_in_dim.16), calls=%async_computation.2 | async-start | bytes 131072 | tf_op jit(solution)/shard_map/all_to_all | solution.py:83
  139.5 6.6 %all-to-all-done.2 = f32[8,6,256]{2,1,0:T(8,128)S(1)} async-done(((f32[8,6,256]{2,1,0:T(8,128)}), f32[8,6,256]{2,1,0:T(8,128)S(1)}, u32[]{:S(2)}, u32[]{:S(2)}) %all-to-all-start.2) | async-done | bytes 49184 | tf_op jit(solution)/shard_map/all_to_all | solution.py:83
  147.0 5.6 %all-to-all-start.3 = ((f32[32,3,128]{2,1,0:T(4,128)}), f32[32,3,128]{2,1,0:T(4,128)S(1)}, u32[]{:S(2)}, u32[]{:S(2)}) async-start(f32[32,3,128]{2,1,0:T(4,128)} %broadcast_in_dim_broadcast_in_dim_broadcast_in_dim.2), calls=%async_computation.3 | async-start | bytes 131072 | tf_op jit(solution)/shard_map/all_to_all | solution.py:83
  153.1 6.8 %all-to-all-done.3 = f32[32,3,128]{2,1,0:T(4,128)S(1)} async-done(((f32[32,3,128]{2,1,0:T(4,128)}), f32[32,3,128]{2,1,0:T(4,128)S(1)}, u32[]{:S(2)}, u32[]{:S(2)}) %all-to-all-start.3) | async-done | bytes 49184 | tf_op jit(solution)/shard_map/all_to_all | solution.py:83
  160.1 5.5 %finish.1 = (bf16[256,4096]{1,0:T(8,128)(2,1)}, bf16[256,4096]{1,0:T(8,128)(2,1)}, bf16[4096,256]{1,0:T(8,128)(2,1)}) custom-call(s32[1]{0:T(128)} %bitcast.core_ref, f32[3,256]{1,0:T(4,128)S(1)} %rsqrt_multiply_fusion.width_ref, f32[48,128]{1,0:T(8,128)S(1)} %get-tuple-element.61.mine_ref, f32[48,128]{1,0:T(8,128)S(1)} %get-tuple-element.77.other_ref, ...), custom_call_target="tpu_custom_call" | custom-call | flops 12582912 | bytes 12582912 | tf_op jit(solution)/shard_map/finish/pallas_call | solution.py:239
  (83 shorter events, 25.8 us)
Async XLA Ops:
  7.2 57.7 %all-gather.3.cloned.1.call-start = ((), (), s32[]{:S(2)}) async-start(), calls=%async_computation.4 | async-start | bytes 1179648 | tf_op jit(solution)/shard_map/all_gather | solution.py:311
  8.9 4.7 %collective-permute-start = (bf16[3,32,2048]{2,1,0:T(8,128)(2,1)S(1)}, bf16[3,32,2048]{2,1,0:T(8,128)(2,1)S(1)}, u32[]{:S(2)}, u32[]{:S(2)}) collective-permute-start(bf16[3,32,2048]{2,1,0:T(8,128)(2,1)S(1)} %pad_maximum_fusion.1), channel_id=1, source_target_pairs={{0,8},{8,0},{1,9},{9,1},{2,10},{10,2},{3,11},{11,3},{4,12},{12,4},... | collective-permute-start | bytes 1179656 | tf_op jit(solution)/shard_map/ppermute | solution.py:38
  13.7 15.4 %collective-permute-start.1 = (bf16[2,3,32,1024]{3,2,1,0:T(8,128)(2,1)S(1)}, bf16[2,3,32,1024]{3,2,1,0:T(8,128)(2,1)S(1)}, u32[]{:S(2)}, u32[]{:S(2)}) collective-permute-start(bf16[2,3,32,1024]{3,2,1,0:T(8,128)(2,1)S(1)} %get-tuple-element.66.refs_0_), channel_id=1, source_target_pairs={{0,64},{64,128},{128,192},{192,0},{1,65},{65,129},{129,193},{193,1... | collective-permute-start | bytes 1179656 | tf_op jit(solution)/shard_map/ppermute | solution.py:38
  13.8 15.4 %collective-permute-start.2 = (bf16[2,3,32,1024]{3,2,1,0:T(8,128)(2,1)S(1)}, bf16[2,3,32,1024]{3,2,1,0:T(8,128)(2,1)S(1)}, u32[]{:S(2)}, u32[]{:S(2)}) collective-permute-start(bf16[2,3,32,1024]{3,2,1,0:T(8,128)(2,1)S(1)} %get-tuple-element.66.refs_0_), channel_id=1, source_target_pairs={{0,192},{64,0},{128,64},{192,128},{1,193},{65,1},{129,65},{193,129... | collective-permute-start | bytes 1179656 | tf_op jit(solution)/shard_map/ppermute | solution.py:38
  16.4 12.7 %collective-permute-start.3 = (bf16[2,3,32,1024]{3,2,1,0:T(8,128)(2,1)S(1)}, bf16[2,3,32,1024]{3,2,1,0:T(8,128)(2,1)S(1)}, u32[]{:S(2)}, u32[]{:S(2)}) collective-permute-start(bf16[2,3,32,1024]{3,2,1,0:T(8,128)(2,1)S(1)} %get-tuple-element.65.refs_5_), channel_id=1, source_target_pairs={{0,16},{16,32},{32,48},{48,0},{1,17},{17,33},{33,49},{49,1},{2,18}... | collective-permute-start | bytes 1179656 | tf_op jit(solution)/shard_map/ppermute | solution.py:38
  16.4 12.7 %collective-permute-start.4 = (bf16[2,3,32,1024]{3,2,1,0:T(8,128)(2,1)S(1)}, bf16[2,3,32,1024]{3,2,1,0:T(8,128)(2,1)S(1)}, u32[]{:S(2)}, u32[]{:S(2)}) collective-permute-start(bf16[2,3,32,1024]{3,2,1,0:T(8,128)(2,1)S(1)} %get-tuple-element.65.refs_5_), channel_id=1, source_target_pairs={{0,48},{16,0},{32,16},{48,32},{1,49},{17,1},{33,17},{49,33},{2,50}... | collective-permute-start | bytes 1179656 | tf_op jit(solution)/shard_map/ppermute | solution.py:38
  29.2 5.8 %collective-permute-start.6 = (bf16[1,3,32,1024]{3,2,1,0:T(8,128)(2,1)S(1)}, bf16[1,3,32,1024]{3,2,1,0:T(8,128)(2,1)S(1)}, u32[]{:S(2)}, u32[]{:S(2)}) collective-permute-start(bf16[1,3,32,1024]{3,2,1,0:T(8,128)(2,1)S(1)} %get-tuple-element.44), channel_id=1, source_target_pairs={{0,64},{64,128},{128,192},{192,0},{1,65},{65,129},{129,193},{193,1... | collective-permute-start | bytes 589832 | tf_op jit(solution)/shard_map/ppermute | solution.py:38
  29.5 5.5 %collective-permute-start.7 = (bf16[1,3,32,1024]{3,2,1,0:T(8,128)(2,1)S(1)}, bf16[1,3,32,1024]{3,2,1,0:T(8,128)(2,1)S(1)}, u32[]{:S(2)}, u32[]{:S(2)}) collective-permute-start(bf16[1,3,32,1024]{3,2,1,0:T(8,128)(2,1)S(1)} %get-tuple-element.45), channel_id=1, source_target_pairs={{0,192},{64,0},{128,64},{192,128},{1,193},{65,1},{129,65},{193,129... | collective-permute-start | bytes 589832 | tf_op jit(solution)/shard_map/ppermute | solution.py:38
  32.0 6.0 %collective-permute-start.8 = (bf16[1,3,32,1024]{3,2,1,0:T(8,128)(2,1)S(1)}, bf16[1,3,32,1024]{3,2,1,0:T(8,128)(2,1)S(1)}, u32[]{:S(2)}, u32[]{:S(2)}) collective-permute-start(bf16[1,3,32,1024]{3,2,1,0:T(8,128)(2,1)S(1)} %get-tuple-element.46), channel_id=1, source_target_pairs={{0,16},{16,32},{32,48},{48,0},{1,17},{17,33},{33,49},{49,1},{2,18}... | collective-permute-start | bytes 589832 | tf_op jit(solution)/shard_map/ppermute | solution.py:38
  32.3 5.8 %collective-permute-start.9 = (bf16[1,3,32,1024]{3,2,1,0:T(8,128)(2,1)S(1)}, bf16[1,3,32,1024]{3,2,1,0:T(8,128)(2,1)S(1)}, u32[]{:S(2)}, u32[]{:S(2)}) collective-permute-start(bf16[1,3,32,1024]{3,2,1,0:T(8,128)(2,1)S(1)} %get-tuple-element.47), channel_id=1, source_target_pairs={{0,48},{16,0},{32,16},{48,32},{1,49},{17,1},{33,17},{49,33},{2,50}... | collective-permute-start | bytes 589832 | tf_op jit(solution)/shard_map/ppermute | solution.py:38
  39.9 33.4 %collective-permute-start.10 = (bf16[4,2,3,32,1024]{4,3,2,1,0:T(8,128)(2,1)}, bf16[4,2,3,32,1024]{4,3,2,1,0:T(8,128)(2,1)S(1)}, u32[]{:S(2)}, u32[]{:S(2)}) collective-permute-start(bf16[4,2,3,32,1024]{4,3,2,1,0:T(8,128)(2,1)} %get-tuple-element.48.refs_4_), channel_id=1, source_target_pairs={{0,16},{16,32},{32,48},{48,0},{1,17},{17,33},{33,49},{49,1},{2,18}... | collective-permute-start | bytes 4718600 | tf_op jit(solution)/shard_map/ppermute | solution.py:38
  39.9 33.4 %collective-permute-start.11 = (bf16[4,2,3,32,1024]{4,3,2,1,0:T(8,128)(2,1)}, bf16[4,2,3,32,1024]{4,3,2,1,0:T(8,128)(2,1)S(1)}, u32[]{:S(2)}, u32[]{:S(2)}) collective-permute-start(bf16[4,2,3,32,1024]{4,3,2,1,0:T(8,128)(2,1)} %get-tuple-element.48.refs_4_), channel_id=1, source_target_pairs={{0,48},{16,0},{32,16},{48,32},{1,49},{17,1},{33,17},{49,33},{2,50}... | collective-permute-start | bytes 4718600 | tf_op jit(solution)/shard_map/ppermute | solution.py:38
  42.5 32.8 %collective-permute-start.12 = (bf16[4,2,3,32,1024]{4,3,2,1,0:T(8,128)(2,1)}, bf16[4,2,3,32,1024]{4,3,2,1,0:T(8,128)(2,1)}, u32[]{:S(2)}, u32[]{:S(2)}) collective-permute-start(bf16[4,2,3,32,1024]{4,3,2,1,0:T(8,128)(2,1)} %get-tuple-element.49.refs_7_), channel_id=1, source_target_pairs={{0,64},{64,128},{128,192},{192,0},{1,65},{65,129},{129,193},{193,1... | collective-permute-start | bytes 4718600 | tf_op jit(solution)/shard_map/ppermute | solution.py:38
  42.5 32.8 %collective-permute-start.13 = (bf16[4,2,3,32,1024]{4,3,2,1,0:T(8,128)(2,1)}, bf16[4,2,3,32,1024]{4,3,2,1,0:T(8,128)(2,1)}, u32[]{:S(2)}, u32[]{:S(2)}) collective-permute-start(bf16[4,2,3,32,1024]{4,3,2,1,0:T(8,128)(2,1)} %get-tuple-element.49.refs_7_), channel_id=1, source_target_pairs={{0,192},{64,0},{128,64},{192,128},{1,193},{65,1},{129,65},{193,129... | collective-permute-start | bytes 4718600 | tf_op jit(solution)/shard_map/ppermute | solution.py:38
  64.9 19.6 %collective-permute-start.5 = (bf16[8,16,32,128]{3,2,1,0:T(8,128)(2,1)}, bf16[8,16,32,128]{3,2,1,0:T(8,128)(2,1)}, u32[]{:S(2)}, u32[]{:S(2)}) collective-permute-start(bf16[8,16,32,128]{3,2,1,0:T(8,128)(2,1)} %bitcast.47), channel_id=1, source_target_pairs={{0,8},{8,0},{1,9},{9,1},{2,10},{10,2},{3,11},{11,3},{4,12},{12,4},... | collective-permute-start | bytes 3145736 | tf_op jit(solution)/shard_map/ppermute | solution.py:38
  79.0 17.0 %collective-permute-start.14 = (bf16[2,2,3,32,1024]{4,3,2,1,0:T(8,128)(2,1)}, bf16[2,2,3,32,1024]{4,3,2,1,0:T(8,128)(2,1)}, u32[]{:S(2)}, u32[]{:S(2)}) collective-permute-start(bf16[2,2,3,32,1024]{4,3,2,1,0:T(8,128)(2,1)} %get-tuple-element.50), channel_id=1, source_target_pairs={{0,16},{16,32},{32,48},{48,0},{1,17},{17,33},{33,49},{49,1},{2,18}... | collective-permute-start | bytes 2359304 | tf_op jit(solution)/shard_map/ppermute | solution.py:38
  79.0 17.0 %collective-permute-start.15 = (bf16[2,2,3,32,1024]{4,3,2,1,0:T(8,128)(2,1)}, bf16[2,2,3,32,1024]{4,3,2,1,0:T(8,128)(2,1)}, u32[]{:S(2)}, u32[]{:S(2)}) collective-permute-start(bf16[2,2,3,32,1024]{4,3,2,1,0:T(8,128)(2,1)} %get-tuple-element.51), channel_id=1, source_target_pairs={{0,48},{16,0},{32,16},{48,32},{1,49},{17,1},{33,17},{49,33},{2,50}... | collective-permute-start | bytes 2359304 | tf_op jit(solution)/shard_map/ppermute | solution.py:38
  81.7 14.5 %collective-permute-start.16 = (bf16[2,2,3,32,1024]{4,3,2,1,0:T(8,128)(2,1)}, bf16[2,2,3,32,1024]{4,3,2,1,0:T(8,128)(2,1)}, u32[]{:S(2)}, u32[]{:S(2)}) collective-permute-start(bf16[2,2,3,32,1024]{4,3,2,1,0:T(8,128)(2,1)} %get-tuple-element.52), channel_id=1, source_target_pairs={{0,64},{64,128},{128,192},{192,0},{1,65},{65,129},{129,193},{193,1... | collective-permute-start | bytes 2359304 | tf_op jit(solution)/shard_map/ppermute | solution.py:38
  81.7 14.5 %collective-permute-start.17 = (bf16[2,2,3,32,1024]{4,3,2,1,0:T(8,128)(2,1)}, bf16[2,2,3,32,1024]{4,3,2,1,0:T(8,128)(2,1)}, u32[]{:S(2)}, u32[]{:S(2)}) collective-permute-start(bf16[2,2,3,32,1024]{4,3,2,1,0:T(8,128)(2,1)} %get-tuple-element.53), channel_id=1, source_target_pairs={{0,192},{64,0},{128,64},{192,128},{1,193},{65,1},{129,65},{193,129... | collective-permute-start | bytes 2359304 | tf_op jit(solution)/shard_map/ppermute | solution.py:38
  102.3 25.0 %collective-permute-start.20 = (bf16[3,2,256,1024]{3,2,1,0:T(8,128)(2,1)}, bf16[3,2,256,1024]{3,2,1,0:T(8,128)(2,1)}, u32[]{:S(2)}, u32[]{:S(2)}) collective-permute-start(bf16[3,2,256,1024]{3,2,1,0:T(8,128)(2,1)} %get-tuple-element.57), channel_id=1, source_target_pairs={{0,8},{8,0},{1,9},{9,1},{2,10},{10,2},{3,11},{11,3},{4,12},{12,4},... | collective-permute-start | bytes 9437192 | tf_op jit(solution)/shard_map/ppermute | solution.py:38
  110.0 13.4 %all-to-all-start.1 = ((f32[16,48,128]{2,1,0:T(8,128)}), f32[16,48,128]{2,1,0:T(8,128)}, u32[]{:S(2)}, u32[]{:S(2)}) async-start(f32[16,48,128]{2,1,0:T(8,128)} %broadcast_in_dim.7), calls=%async_computation.1 | async-start | bytes 786432 | tf_op jit(solution)/shard_map/all_to_all | solution.py:83
  124.5 2.8 %collective-permute-start.19 = (f32[48,128]{1,0:T(8,128)S(1)}, f32[48,128]{1,0:T(8,128)S(1)}, u32[]{:S(2)}, u32[]{:S(2)}) collective-permute-start(f32[48,128]{1,0:T(8,128)S(1)} %get-tuple-element.62), channel_id=1, source_target_pairs={{0,8},{8,0},{1,9},{9,1},{2,10},{10,2},{3,11},{11,3},{4,12},{12,4},... | collective-permute-start | bytes 73736 | tf_op jit(solution)/shard_map/ppermute | solution.py:38
  131.6 14.5 %all-to-all-start.2 = ((f32[8,6,256]{2,1,0:T(8,128)}), f32[8,6,256]{2,1,0:T(8,128)S(1)}, u32[]{:S(2)}, u32[]{:S(2)}) async-start(f32[8,6,256]{2,1,0:T(8,128)} %broadcast_in_dim.16), calls=%async_computation.2 | async-start | bytes 131072 | tf_op jit(solution)/shard_map/all_to_all | solution.py:83
  147.0 12.9 %all-to-all-start.3 = ((f32[32,3,128]{2,1,0:T(4,128)}), f32[32,3,128]{2,1,0:T(4,128)S(1)}, u32[]{:S(2)}, u32[]{:S(2)}) async-start(f32[32,3,128]{2,1,0:T(4,128)} %broadcast_in_dim_broadcast_in_dim_broadcast_in_dim.2), calls=%async_computation.3 | async-start | bytes 131072 | tf_op jit(solution)/shard_map/all_to_all | solution.py:83
  (10 other events, 138.3 us)
Sparse Core Ops, SparseCore 0:
  29.3 35.5 all-gather.2

commit v2 on v1

--- a/solution.py
+++ b/solution.py
@@ -78,9 +78,8 @@
     return [(shift(halves[2 * r], axis, 4, 1), shift(halves[2 * r + 1], axis, 4, 3)) for r, axis in enumerate(axes)]
 
 
-def spread(value, axes, count):
-    sent = jnp.broadcast_to(value[None], (count,) + value.shape)
-    return lax.all_to_all(sent, axes, split_axis=0, concat_axis=0, tiled=True)
+def collect(copies, axes):
+    return lax.all_to_all(copies, axes, split_axis=0, concat_axis=0, tiled=True)
 
 
 def join_kernel(*refs):
@@ -173,52 +172,82 @@
                         across[i] += square[:, k * 128 : (k + 1) * 128]
                 for k in range(tile // 128):
                     row = step * (tile // 128) + k
-                    cols_ref[m, route, row : row + 1, :] = down[:, k * 128 : (k + 1) * 128] * SCALE
+                    row += (m * 2 + route) * 8
+                    cols_ref[0, row : row + 1] = down[:, k * 128 : (k + 1) * 128] * SCALE
         for i, total in enumerate(across):
-            rows_ref[m, i : i + 1] = jnp.sum(total.T, axis=0, keepdims=True) * SCALE
+            rows_ref[i, m : m + 1] = jnp.sum(total.T, axis=0, keepdims=True) * SCALE
+    for i in range(1, XN * YN):
+        cols_ref[i] = cols_ref[0]
 
 
 def multiply(features, total, parts):
     outs = [
         ((3, 2, ROWS, QUART), jnp.bfloat16),
         ((3, 2, ROWS, QUART), jnp.bfloat16),
-        ((3, 2, ROWS), jnp.float32),
-        ((3, 2, 8, 128), jnp.float32),
+        ((2, 3, ROWS), jnp.float32),
+        ((XN * YN, 48, 128), jnp.float32),
     ]
     depth = TOKENS // 4
     scratch = [pltpu.VMEM((2, depth, QUART // 2), jnp.bfloat16)]
     return whole(multiply_kernel, "multiply", outs, (*features, total, *parts), 3 * 4 * ROWS * HALF * depth, scratch)
 
 
-def weigh_kernel(mine_ref, other_ref, keep_ref, got_ref, out_ref):
+def span_kernel(parts_ref, old_ref, out_ref):
+    total = parts_ref[0]
+    for i in range(1, XN * YN):
+        total += parts_ref[i]
+    out_ref[...] = BETA * old_ref[...] + (1.0 - BETA) * (total * (1.0 / D) + EPS)
+
+
+def weigh_kernel(rows_ref, mine_ref, other_ref, keep_ref, got_ref, out_ref):
+    out_ref[0, 0:3] = rows_ref[...]
     for m in range(3):
         total = jnp.zeros((ROWS, 128), jnp.float32)
-        for ref, inverse_ref in ((keep_ref, mine_ref), (got_ref, other_ref)):
+        for ref, span_ref in ((keep_ref, mine_ref), (got_ref, other_ref)):
             for route in range(2):
+                at = (m * 2 + route) * 8
+                inverse = 1.0 / span_ref[at : at + 8]
                 for k in range(8):
-                    at = (m * 2 + route) * 8 + k
                     grad = ref[m, route, :, k * 128 : (k + 1) * 128].astype(jnp.float32)
-                    total += grad * grad * inverse_ref[at : at + 1]
-        out_ref[m : m + 1] = jnp.sum(total.T, axis=0, keepdims=True) * SCALE
-
-
-def weigh(*operands):
-    return whole(weigh_kernel, "weigh", [((3, ROWS), jnp.float32)], operands, 12 * ROWS * COLS)[0]
-
-
-def finish_kernel(core_ref, width_ref, mine_ref, other_ref, keep_ref, got_ref, *refs):
-    outs, bufs, sem = refs[:3], refs[3:6], refs[6]
+                    total += grad * grad * inverse[k : k + 1]
+        out_ref[0, 3 + m : 4 + m] = jnp.sum(total.T, axis=0, keepdims=True) * SCALE
+    for i in range(1, ZN):
+        out_ref[i] = out_ref[0]
+
+
+def width_kernel(parts_ref, old_ref, width_ref, out_ref):
+    total = parts_ref[0]
+    for i in range(1, ZN):
+        total += parts_ref[i]
+    width = BETA * old_ref[...] + (1.0 - BETA) * (total[0:3] * (1.0 / FF) + EPS)
+    width_ref[...] = width
+    squares = total[3:6] / width
+    squares = squares[:, :128] + squares[:, 128:]
+    for i in range(XN * YN * CN):
+        out_ref[i] = squares
+
+
+def finish_kernel(core_ref, parts_ref, width_ref, mine_ref, other_ref, keep_ref, got_ref, *refs):
+    outs, widths, spans, bufs, sem = refs[:3], refs[3:6], refs[6:9], refs[9:12], refs[12]
     core = core_ref[0]
+    squares = parts_ref[0]
+    for i in range(1, XN * YN * CN):
+        squares += parts_ref[i]
+    rms = jnp.sqrt(jnp.sum(squares, axis=1, keepdims=True) * (1.0 / (D * FF)))
+    scaled = lax.rsqrt(width_ref[...]) * ((1.0 / 32.0) / jnp.maximum(1.0, rms))
     copies = []
     for m in range(3):
-        width = jnp.broadcast_to(width_ref[m : m + 1], (128, ROWS)).T
-        for ref, unit_ref, at in ((keep_ref, mine_ref, core), (got_ref, other_ref, 1 - core)):
+        widths[m][...] = width_ref[m : m + 1]
+        width = jnp.broadcast_to(scaled[m : m + 1], (128, ROWS)).T
+        for ref, span_ref, at in ((keep_ref, mine_ref, core), (got_ref, other_ref, 1 - core)):
+            spans[m][pl.ds(pl.multiple_of(at * 16, 16), 16)] = span_ref[m * 16 : (m + 1) * 16]
             for route in range(2):
                 first = at * HALF + route * QUART
+                row = (m * 2 + route) * 8
+                unit = lax.rsqrt(span_ref[row : row + 8])
                 for k in range(8):
-                    row = (m * 2 + route) * 8 + k
                     grad = ref[m, route, :, k * 128 : (k + 1) * 128].astype(jnp.float32)
-                    normed = (grad * width * unit_ref[row : row + 1]).astype(jnp.bfloat16)
+                    normed = (grad * width * unit[k : k + 1]).astype(jnp.bfloat16)
                     place = pl.ds(pl.multiple_of(first + k * 128, 128), 128)
                     if m < 2:
                         bufs[m][:, place] = normed
@@ -234,15 +263,16 @@
 
 def finish(core, *operands):
     spec = pl.BlockSpec(memory_space=pltpu.VMEM)
-    wide, tall = (ROWS, COLS), (COLS, ROWS)
+    steps = [(ROWS, COLS), (ROWS, COLS), (COLS, ROWS)]
     operands = here(*operands)
     return pl.pallas_call(
         finish_kernel,
         in_specs=[pl.BlockSpec(memory_space=pltpu.SMEM)] + [spec] * len(operands),
-        out_specs=[pl.BlockSpec(memory_space=pl.ANY)] * 3,
-        out_shape=[jax.ShapeDtypeStruct(shape, jnp.bfloat16) for shape in (wide, wide, tall)],
-        scratch_shapes=[pltpu.VMEM(shape, jnp.bfloat16) for shape in (wide, wide, tall)]
-        + [pltpu.SemaphoreType.DMA((12,))],
+        out_specs=[pl.BlockSpec(memory_space=pl.ANY)] * 3 + [spec] * 6,
+        out_shape=[jax.ShapeDtypeStruct(shape, jnp.bfloat16) for shape in steps]
+        + [jax.ShapeDtypeStruct((1, ROWS), jnp.float32)] * 3
+        + [jax.ShapeDtypeStruct((COLS // 128, 128), jnp.float32)] * 3,
+        scratch_shapes=[pltpu.VMEM(shape, jnp.bfloat16) for shape in steps] + [pltpu.SemaphoreType.DMA((12,))],
         compiler_params=pltpu.CompilerParams(vmem_limit_bytes=2 * VMEM),
         cost_estimate=pl.CostEstimate(flops=12 * ROWS * COLS, bytes_accessed=12 << 20, transcendentals=0),
         name="finish",
@@ -294,7 +324,13 @@
 ):
     x, y, c, z = (lax.axis_index(name) for name in ("x", "y", "c", "z"))
     core = c.astype(jnp.int32).reshape(1)
+    level = z.astype(jnp.int32).reshape(1)
     place = jnp.stack((x, y, c)).astype(jnp.int32)
+    known = (core, level, place, c == 0, gate_pre, up_pre, hidden_grad)
+    core, level, place, first, gate_pre, up_pre, hidden_grad = lax.optimization_barrier(known)
+    old_span = jnp.stack((col_gate, col_up, row_down)).reshape(3, CN, 16, 128)
+    old_span = jnp.where(first, old_span[:, 0], old_span[:, 1]).reshape(48, 128)
+    old_width = jnp.stack((row_gate, row_up, col_down))
 
     def halves(at):
         return derive(*(lax.dynamic_slice_in_dim(v, at * HALF, HALF, 1) for v in (gate_pre, up_pre, hidden_grad)))
@@ -304,9 +340,9 @@
     own_a, own_b = own[..., :QUART], own[..., QUART:]
     near = [neighbours(own_a, "x"), neighbours(own_b, "y")]
 
-    chosen = pick(z.astype(jnp.int32).reshape(1), layer_input, output_grad)
+    chosen = pick(level, layer_input, output_grad)
     chosen = lax.all_to_all(chosen, ("x", "y"), split_axis=0, concat_axis=0, tiled=True)
-    near, chosen = lax.optimization_barrier((near, chosen))
+    near, chosen, old_span, old_width = lax.optimization_barrier((near, chosen, old_span, old_width))
     far = relay(near, ("x", "y"))
     chosen = lax.all_gather(chosen, "z")
     lines = join([own_a, *near[0], *far[0], own_b, *near[1], *far[1]])
@@ -317,44 +353,22 @@
     parts = [lines[0], *near[0], lines[1], *near[1]]
     keep, send, rows, cols = multiply(features, start(features, parts), [*far[0], *far[1]])
 
-    rows = rows[:, 0] + swap(rows[:, 1])
-    cols = cols.reshape(48, 128)
+    rows = rows[0] + swap(rows[1])
+    rows, cols, send = lax.optimization_barrier((rows, cols, send))
     got = swap(send)
 
-    span = jnp.sum(spread(cols, ("x", "y"), XN * YN), axis=0)
-    old = jnp.stack((col_gate, col_up, row_down)).reshape(3, CN, 16, 128)
-    old = lax.dynamic_index_in_dim(old, c, 1, keepdims=False).reshape(48, 128)
-    new_span = BETA * old + (1.0 - BETA) * (span / D + EPS)
-    other_span = swap(new_span)
-
-    weighted = weigh(1.0 / new_span, 1.0 / other_span, keep, got)
-    both = jnp.sum(spread(jnp.concatenate((rows, weighted)), ("z",), ZN), axis=0)
-    new_width = BETA * jnp.stack((row_gate, row_up, col_down)) + (1.0 - BETA) * (both[:3] / FF + EPS)
-    squares = jnp.sum(both[3:] / new_width, axis=1, keepdims=True)
-    squares = jnp.sum(spread(jnp.broadcast_to(squares, (3, 128)), ("x", "y", "c"), XN * YN * CN), axis=0)[:, :1]
-    scale = (1.0 / 32.0) / jnp.maximum(1.0, jnp.sqrt(squares / (D * FF)))
-    width = lax.rsqrt(new_width) * scale
-    step_gate, step_up, step_down = finish(
-        core,
-        width,
-        lax.rsqrt(new_span),
-        lax.rsqrt(other_span),
-        keep,
-        got,
-    )
-    mine, other = new_span.reshape(3, HALF), other_span.reshape(3, HALF)
-    columns = jnp.where(c == 0, jnp.concatenate((mine, other), 1), jnp.concatenate((other, mine), 1))
-    return (
-        step_gate,
-        step_up,
-        step_down,
-        new_width[0],
-        columns[0],
-        new_width[1],
-        columns[1],
-        columns[2],
-        new_width[2],
-    )
+    parts = collect(cols, ("x", "y"))
+    span = whole(span_kernel, "span", [((48, 128), jnp.float32)], (parts, old_span))[0]
+    other = swap(span)
+    sums = whole(weigh_kernel, "weigh", [((ZN, 6, ROWS), jnp.float32)], (rows, span, other, keep, got))[0]
+    parts = collect(sums, ("z",))
+    outs = [((3, ROWS), jnp.float32), ((XN * YN * CN, 3, 128), jnp.float32)]
+    width, squares = whole(width_kernel, "width", outs, (parts, old_width))
+    parts = collect(squares, ("x", "y", "c"))
+    outs = finish(core, parts, width, span, other, keep, got)
+    widths = [v.reshape(ROWS) for v in outs[3:6]]
+    spans = [v.reshape(COLS) for v in outs[6:9]]
+    return (*outs[:3], widths[0], spans[0], widths[1], spans[1], spans[2], widths[2])
 
 
 def solution(mesh):

time: 173 us -> 167 us (0.965)
  blocking collectives: 9.96 us -> 41.1 us
  starting transfers between devices: 56 us -> 42.9 us
  waiting for transfers between devices: 53.2 us -> 43.7 us
  Pallas kernels: 31.1 us -> 23.2 us
  local copies, waits for them, and re-layouts: 4.65 us -> 0.06 us
    all_to_all x1 -> x3, blocking collectives: 9.96 us -> 41.1 us  [collect(): return lax.all_to_all(copies, axes, split_axis=0, concat_axis=0, tiled=True)]
    all_to_all x3 -> x1, waiting for transfers between devices: 21.3 us -> 1.08 us  [local(): lax.all_to_all(chosen, ('x', 'y'), split_axis=0, concat_axis=0, tiled=True)]
    all_to_all x3 -> x1, starting transfers between devices: 17 us -> 5.02 us  [local(): lax.all_to_all(chosen, ('x', 'y'), split_axis=0, concat_axis=0, tiled=True)]
    ppermute x21, waiting for transfers between devices: 12.3 us -> 22 us  [shift(): lax.ppermute(value, axis, [(i, (i + step) % size) for i in range(size)])]
    pallas_call x6 -> x8, Pallas kernels: 23.1 us -> 16.4 us  [whole(): pl.pallas_call(kernel, in_specs=[spec] * len(operands), out_specs=[spec]...]
  transfers between devices with their start and end apart: 25 -> 23, of which waited for: 12 -> 12; matrix products, arithmetic and copies ran while one was open for 2% -> 0% of each run, Pallas kernels for 9% -> 9%
where the time goes in v2:
time: 167 us
  waiting for transfers between devices  43.7 us (26%)
  starting transfers between devices  42.9 us (26%)
  blocking collectives  41.1 us (25%)
  Pallas kernels  23.2 us (14%)
  between operations  14.3 us (9%)
  other arithmetic  1.85 us (1%)
    all_to_all x3, blocking collectives, collect(): return lax.all_to_all(copies, axes, split_axis=0, concat_axis=0, tiled=True)  41.1 us
    ppermute x21, starting transfers between devices, shift(): lax.ppermute(value, axis, [(i, (i + step) % size) for i in range(size)])  37.8 us
    ppermute x21, waiting for transfers between devices, shift(): lax.ppermute(value, axis, [(i, (i + step) % size) for i in range(size)])  22 us
    all_gather x1, waiting for transfers between devices, local(): chosen = lax.all_gather(chosen, 'z')  20.6 us
    pallas_call x8, Pallas kernels, whole(): pl.pallas_call(kernel, in_specs=[spec] * len(operands), out_specs=[spec]...  16.4 us
    all_to_all x1, starting transfers between devices, local(): lax.all_to_all(chosen, ('x', 'y'), split_axis=0, concat_axis=0, tiled=True)  5.02 us
    pallas_call x1, Pallas kernels, finish(): pl.pallas_call(finish_kernel, in_specs=[pl.BlockSpec(memory_space=pltpu.S...  4.41 us
  transfers between devices with their start and end apart: 23, of which 12 were waited for; matrix products, arithmetic and copies ran while one was open for 0% of the time, Pallas kernels for 9%

profile of v2, /device:TPU:1, one launch (start us, length us, event | category | flops | bytes accessed | tf_op | source)
XLA Modules:
  0.0 167.0 jit_solution(3051911724523081602)
XLA Ops:
  9.0 3.3 %collective-permute-start = (bf16[3,32,2048]{2,1,0:T(8,128)(2,1)S(1)}, bf16[3,32,2048]{2,1,0:T(8,128)(2,1)S(1)}, u32[]{:S(2)}, u32[]{:S(2)}) collective-permute-start(bf16[3,32,2048]{2,1,0:T(8,128)(2,1)S(1)} %pad_maximum_fusion.1), channel_id=1, source_target_pairs={{0,8},{8,0},{1,9},{9,1},{2,10},{10,2},{3,11},{11,3},{4,12},{12,4},... | collective-permute-start | bytes 1179656 | tf_op jit(solution)/shard_map/ppermute | solution.py:38
  13.0 5.0 %all-to-all-start = ((bf16[16,32,128]{2,1,0:T(8,128)(2,1)}), bf16[16,32,128]{2,1,0:T(8,128)(2,1)S(1)}, u32[]{:S(2)}, u32[]{:S(2)}) async-start(bf16[16,32,128]{2,1,0:T(8,128)(2,1)} %pick.1), calls=%async_computation | async-start | bytes 262144 | tf_op jit(solution)/shard_map/all_to_all | solution.py:344
  24.8 6.5 %collective-permute-done.1.refs_0_.refs_1_ = bf16[2,3,32,1024]{3,2,1,0:T(8,128)(2,1)S(1)} collective-permute-done((bf16[2,3,32,1024]{3,2,1,0:T(8,128)(2,1)S(1)}, bf16[2,3,32,1024]{3,2,1,0:T(8,128)(2,1)S(1)}, u32[]{:S(2)}, u32[]{:S(2)}) %collective-permute-start.1) | collective-permute-done | bytes 393248 | tf_op jit(solution)/shard_map/ppermute | solution.py:38
  33.2 2.7 %collective-permute-start.7 = (bf16[1,3,32,1024]{3,2,1,0:T(8,128)(2,1)S(1)}, bf16[1,3,32,1024]{3,2,1,0:T(8,128)(2,1)S(1)}, u32[]{:S(2)}, u32[]{:S(2)}) collective-permute-start(bf16[1,3,32,1024]{3,2,1,0:T(8,128)(2,1)S(1)} %get-tuple-element.72), channel_id=1, source_target_pairs={{0,192},{64,0},{128,64},{192,128},{1,193},{65,1},{129,65},{193,129... | collective-permute-start | bytes 589832 | tf_op jit(solution)/shard_map/ppermute | solution.py:38
  35.9 2.7 %collective-permute-start.9 = (bf16[1,3,32,1024]{3,2,1,0:T(8,128)(2,1)S(1)}, bf16[1,3,32,1024]{3,2,1,0:T(8,128)(2,1)S(1)}, u32[]{:S(2)}, u32[]{:S(2)}) collective-permute-start(bf16[1,3,32,1024]{3,2,1,0:T(8,128)(2,1)S(1)} %get-tuple-element.74), channel_id=1, source_target_pairs={{0,48},{16,0},{32,16},{48,32},{1,49},{17,1},{33,17},{49,33},{2,50}... | collective-permute-start | bytes 589832 | tf_op jit(solution)/shard_map/ppermute | solution.py:38
  39.6 2.0 %collective-permute-done.8.refs_8_ = bf16[1,3,32,1024]{3,2,1,0:T(8,128)(2,1)S(1)} collective-permute-done((bf16[1,3,32,1024]{3,2,1,0:T(8,128)(2,1)S(1)}, bf16[1,3,32,1024]{3,2,1,0:T(8,128)(2,1)S(1)}, u32[]{:S(2)}, u32[]{:S(2)}) %collective-permute-start.8) | collective-permute-done | bytes 196640 | tf_op jit(solution)/shard_map/ppermute | solution.py:38
  41.6 1.9 %join.1 = (bf16[4,2,3,32,1024]{4,3,2,1,0:T(8,128)(2,1)}, bf16[4,2,3,32,1024]{4,3,2,1,0:T(8,128)(2,1)}) custom-call(bf16[2,3,32,1024]{3,2,1,0:T(8,128)(2,1)S(1)} %get-tuple-element.102.refs_0_, bf16[2,3,32,1024]{3,2,1,0:T(8,128)(2,1)S(1)} %collective-permute-done.1.refs_0_.refs_1_, bf16[2,3,32,1024]{3,2,1,0:T(8,128)(2,1)S(1)} %collective-permute-done.2.refs_1_.refs_2_, ...), custom_call_target="tpu_custom_call" | custom-call | bytes 3145728 | tf_op jit(solution)/shard_map/join/pallas_call | solution.py:56
  43.5 2.7 %collective-permute-start.11 = (bf16[4,2,3,32,1024]{4,3,2,1,0:T(8,128)(2,1)}, bf16[4,2,3,32,1024]{4,3,2,1,0:T(8,128)(2,1)S(1)}, u32[]{:S(2)}, u32[]{:S(2)}) collective-permute-start(bf16[4,2,3,32,1024]{4,3,2,1,0:T(8,128)(2,1)} %get-tuple-element.75.refs_4_), channel_id=1, source_target_pairs={{0,48},{16,0},{32,16},{48,32},{1,49},{17,1},{33,17},{49,33},{2,50}... | collective-permute-start | bytes 4718600 | tf_op jit(solution)/shard_map/ppermute | solution.py:38
  46.2 2.7 %collective-permute-start.13 = (bf16[4,2,3,32,1024]{4,3,2,1,0:T(8,128)(2,1)}, bf16[4,2,3,32,1024]{4,3,2,1,0:T(8,128)(2,1)}, u32[]{:S(2)}, u32[]{:S(2)}) collective-permute-start(bf16[4,2,3,32,1024]{4,3,2,1,0:T(8,128)(2,1)} %get-tuple-element.76.refs_7_), channel_id=1, source_target_pairs={{0,192},{64,0},{128,64},{192,128},{1,193},{65,1},{129,65},{193,129... | collective-permute-start | bytes 4718600 | tf_op jit(solution)/shard_map/ppermute | solution.py:38
  48.8 20.6 %all-gather.3.cloned.1.call-done = bf16[128,32,128]{2,1,0:T(8,128)(2,1)} async-done(((bf16[16,32,128]{2,1,0:T(8,128)(2,1)}), bf16[128,32,128]{2,1,0:T(8,128)(2,1)}) %all-gather.3.cloned.1.call-update) | async-done | bytes 1048592 | tf_op jit(solution)/shard_map/all_gather | solution.py:347
  69.5 4.6 %collective-permute-start.5 = (bf16[8,16,32,128]{3,2,1,0:T(8,128)(2,1)}, bf16[8,16,32,128]{3,2,1,0:T(8,128)(2,1)S(1)}, u32[]{:S(2)}, u32[]{:S(2)}) collective-permute-start(bf16[8,16,32,128]{3,2,1,0:T(8,128)(2,1)} %bitcast.37), channel_id=1, source_target_pairs={{0,8},{8,0},{1,9},{9,1},{2,10},{10,2},{3,11},{11,3},{4,12},{12,4},... | collective-permute-start | bytes 3145736 | tf_op jit(solution)/shard_map/ppermute | solution.py:38
  74.0 3.9 %collective-permute-done.10.refs_5_.refs_0_ = bf16[4,2,3,32,1024]{4,3,2,1,0:T(8,128)(2,1)S(1)} collective-permute-done((bf16[4,2,3,32,1024]{4,3,2,1,0:T(8,128)(2,1)}, bf16[4,2,3,32,1024]{4,3,2,1,0:T(8,128)(2,1)S(1)}, u32[]{:S(2)}, u32[]{:S(2)}) %collective-permute-start.10) | collective-permute-done | bytes 1572896 | tf_op jit(solution)/shard_map/ppermute | solution.py:38
  78.0 2.1 %collective-permute-done.12.refs_8_.refs_2_ = bf16[4,2,3,32,1024]{4,3,2,1,0:T(8,128)(2,1)} collective-permute-done((bf16[4,2,3,32,1024]{4,3,2,1,0:T(8,128)(2,1)}, bf16[4,2,3,32,1024]{4,3,2,1,0:T(8,128)(2,1)}, u32[]{:S(2)}, u32[]{:S(2)}) %collective-permute-start.12) | collective-permute-done | bytes 1572896 | tf_op jit(solution)/shard_map/ppermute | solution.py:38
  80.1 2.1 %halve.3 = (bf16[2,2,3,32,1024]{4,3,2,1,0:T(8,128)(2,1)S(1)}, bf16[2,2,3,32,1024]{4,3,2,1,0:T(8,128)(2,1)S(1)}, bf16[2,2,3,32,1024]{4,3,2,1,0:T(8,128)(2,1)S(1)}, bf16[2,2,3,32,1024]{4,3,2,1,0:T(8,128)(2,1)S(1)}) custom-call(bf16[4,2,3,32,1024]{4,3,2,1,0:T(8,128)(2,1)S(1)} %collective-permute-done.10.refs_5_.refs_0_, ...), custom_call_target="tpu_custom_call" | custom-call | bytes 6291456 | tf_op jit(solution)/shard_map/halve/pallas_call | solution.py:56
  82.4 2.7 %collective-permute-start.15 = (bf16[2,2,3,32,1024]{4,3,2,1,0:T(8,128)(2,1)S(1)}, bf16[2,2,3,32,1024]{4,3,2,1,0:T(8,128)(2,1)S(1)}, u32[]{:S(2)}, u32[]{:S(2)}) collective-permute-start(bf16[2,2,3,32,1024]{4,3,2,1,0:T(8,128)(2,1)S(1)} %get-tuple-element.78), channel_id=1, source_target_pairs={{0,48},{16,0},{32,16},{48,32},{1,49},{17,1},{33,17},{49,33},{2,50}... | collective-permute-start | bytes 2359304 | tf_op jit(solution)/shard_map/ppermute | solution.py:38
  85.1 2.7 %collective-permute-start.17 = (bf16[2,2,3,32,1024]{4,3,2,1,0:T(8,128)(2,1)S(1)}, bf16[2,2,3,32,1024]{4,3,2,1,0:T(8,128)(2,1)S(1)}, u32[]{:S(2)}, u32[]{:S(2)}) collective-permute-start(bf16[2,2,3,32,1024]{4,3,2,1,0:T(8,128)(2,1)S(1)} %get-tuple-element.80), channel_id=1, source_target_pairs={{0,192},{64,0},{128,64},{192,128},{1,193},{65,1},{129,65},{193,129... | collective-permute-start | bytes 2359304 | tf_op jit(solution)/shard_map/ppermute | solution.py:38
  89.5 7.9 %start.1.refs_4_ = f32[3,2,512,1024]{3,2,1,0:T(8,128)S(1)} custom-call(bf16[512,1024]{1,0:T(8,128)(2,1)S(1)} %get-tuple-element.63.refs_0_, bf16[512,1024]{1,0:T(8,128)(2,1)S(1)} %get-tuple-element.64.refs_1_, bf16[512,1024]{1,0:T(8,128)(2,1)S(1)} %get-tuple-element.65.refs_2_, bf16[512,1024]{1,0:T(8,128)(2,1)S(1)} %get-tuple-element.66.refs_3_, ...), custom_call_target="tpu_custom_call" | custom-call | flops 4831838208 | bytes 13631488 | tf_op jit(solution)/shard_map/start/pallas_call | solution.py:56
  98.2 2.1 %collective-permute-done.16.refs_7_ = bf16[2,2,3,32,1024]{4,3,2,1,0:T(8,128)(2,1)S(1)} collective-permute-done((bf16[2,2,3,32,1024]{4,3,2,1,0:T(8,128)(2,1)S(1)}, bf16[2,2,3,32,1024]{4,3,2,1,0:T(8,128)(2,1)S(1)}, u32[]{:S(2)}, u32[]{:S(2)}) %collective-permute-start.16) | collective-permute-done | bytes 786464 | tf_op jit(solution)/shard_map/ppermute | solution.py:38
  100.3 2.7 %multiply.1 = (bf16[3,2,256,1024]{3,2,1,0:T(8,128)(2,1)S(1)}, bf16[3,2,256,1024]{3,2,1,0:T(8,128)(2,1)S(1)}, f32[2,3,256]{2,1,0:T(4,128)S(1)}, f32[16,48,128]{2,1,0:T(8,128)S(1)}) custom-call(bf16[512,1024]{1,0:T(8,128)(2,1)S(1)} %get-tuple-element.63.refs_0_, bf16[512,1024]{1,0:T(8,128)(2,1)S(1)} %get-tuple-element.64.refs_1_, ...), custom_call_target="tpu_custom_call" | custom-call | flops 1610612736 | bytes 19922944 | tf_op jit(solution)/shard_map/multiply/pallas_call | solution.py:56
  103.1 6.0 %collective-permute-start.18 = (f32[3,256]{1,0:T(4,128)S(1)}, f32[3,256]{1,0:T(4,128)S(1)}, u32[]{:S(2)}, u32[]{:S(2)}) collective-permute-start(f32[3,256]{1,0:T(4,128)S(1)} %slice_bitcast_fusion), channel_id=1, source_target_pairs={{0,8},{8,0},{1,9},{9,1},{2,10},{10,2},{3,11},{11,3},{4,12},{12,4},... | collective-permute-start | bytes 9224 | tf_op jit(solution)/shard_map/ppermute | solution.py:38
  110.3 13.2 %all_to_all.20.parts_ref = f32[16,48,128]{2,1,0:T(8,128)S(1)} all-to-all(f32[16,48,128]{2,1,0:T(8,128)S(1)} %get-tuple-element.85), channel_id=1, replica_groups=mesh['x'=4,'y'=4,'c'=2,'z'=8] {'x','y'}, dimensions={0} | all-to-all | bytes 786432 | tf_op jit(solution)/shard_map/all_to_all | solution.py:82
  127.8 15.2 %all_to_all.21.parts_ref = f32[8,6,256]{2,1,0:T(8,128)S(1)} all-to-all(f32[8,6,256]{2,1,0:T(8,128)S(1)} %weigh.1), channel_id=1, replica_groups=mesh['x'=4,'y'=4,'c'=2,'z'=8] {'z'}, dimensions={0} | all-to-all | bytes 98304 | tf_op jit(solution)/shard_map/all_to_all | solution.py:82
  143.1 12.7 %all_to_all.22.parts_ref = f32[32,3,128]{2,1,0:T(4,128)S(1)} all-to-all(f32[32,3,128]{2,1,0:T(4,128)S(1)} %get-tuple-element.90), channel_id=1, replica_groups=mesh['x'=4,'y'=4,'c'=2,'z'=8] {'x','y','c'}, dimensions={0} | all-to-all | bytes 98304 | tf_op jit(solution)/shard_map/all_to_all | solution.py:82
  155.8 4.4 %finish.1 = (bf16[256,4096]{1,0:T(8,128)(2,1)}, bf16[256,4096]{1,0:T(8,128)(2,1)}, bf16[4096,256]{1,0:T(8,128)(2,1)}, f32[1,256]{1,0:T(1,128)}, f32[1,256]{1,0:T...) custom-call(s32[1]{0:T(128)} %bitcast.core_ref, ...), custom_call_target="tpu_custom_call" | custom-call | flops 12582912 | bytes 12582912 | tf_op jit(solution)/shard_map/finish/pallas_call | solution.py:268
  (67 shorter events, 20.4 us)
Async XLA Ops:
  9.0 9.2 %collective-permute-start = (bf16[3,32,2048]{2,1,0:T(8,128)(2,1)S(1)}, bf16[3,32,2048]{2,1,0:T(8,128)(2,1)S(1)}, u32[]{:S(2)}, u32[]{:S(2)}) collective-permute-start(bf16[3,32,2048]{2,1,0:T(8,128)(2,1)S(1)} %pad_maximum_fusion.1), channel_id=1, source_target_pairs={{0,8},{8,0},{1,9},{9,1},{2,10},{10,2},{3,11},{11,3},{4,12},{12,4},... | collective-permute-start | bytes 1179656 | tf_op jit(solution)/shard_map/ppermute | solution.py:38
  13.0 11.8 %all-to-all-start = ((bf16[16,32,128]{2,1,0:T(8,128)(2,1)}), bf16[16,32,128]{2,1,0:T(8,128)(2,1)S(1)}, u32[]{:S(2)}, u32[]{:S(2)}) async-start(bf16[16,32,128]{2,1,0:T(8,128)(2,1)} %pick.1), calls=%async_computation | async-start | bytes 262144 | tf_op jit(solution)/shard_map/all_to_all | solution.py:344
  18.1 51.4 %all-gather.3.cloned.1.call-start = ((), (), s32[]{:S(2)}) async-start(), calls=%async_computation.4 | async-start | bytes 1179648 | tf_op jit(solution)/shard_map/all_gather | solution.py:347
  18.2 13.1 %collective-permute-start.1 = (bf16[2,3,32,1024]{3,2,1,0:T(8,128)(2,1)S(1)}, bf16[2,3,32,1024]{3,2,1,0:T(8,128)(2,1)S(1)}, u32[]{:S(2)}, u32[]{:S(2)}) collective-permute-start(bf16[2,3,32,1024]{3,2,1,0:T(8,128)(2,1)S(1)} %get-tuple-element.102.refs_0_), channel_id=1, source_target_pairs={{0,64},{64,128},{128,192},{192,0},{1,65},{65,129},{129,193},{193,1... | collective-permute-start | bytes 1179656 | tf_op jit(solution)/shard_map/ppermute | solution.py:38
  19.7 11.7 %collective-permute-start.2 = (bf16[2,3,32,1024]{3,2,1,0:T(8,128)(2,1)S(1)}, bf16[2,3,32,1024]{3,2,1,0:T(8,128)(2,1)S(1)}, u32[]{:S(2)}, u32[]{:S(2)}) collective-permute-start(bf16[2,3,32,1024]{3,2,1,0:T(8,128)(2,1)S(1)} %get-tuple-element.102.refs_0_), channel_id=1, source_target_pairs={{0,192},{64,0},{128,64},{192,128},{1,193},{65,1},{129,65},{193,129... | collective-permute-start | bytes 1179656 | tf_op jit(solution)/shard_map/ppermute | solution.py:38
  21.0 12.0 %collective-permute-start.3 = (bf16[2,3,32,1024]{3,2,1,0:T(8,128)(2,1)S(1)}, bf16[2,3,32,1024]{3,2,1,0:T(8,128)(2,1)S(1)}, u32[]{:S(2)}, u32[]{:S(2)}) collective-permute-start(bf16[2,3,32,1024]{3,2,1,0:T(8,128)(2,1)S(1)} %get-tuple-element.101.refs_5_), channel_id=1, source_target_pairs={{0,16},{16,32},{32,48},{48,0},{1,17},{17,33},{33,49},{49,1},{2,18}... | collective-permute-start | bytes 1179656 | tf_op jit(solution)/shard_map/ppermute | solution.py:38
  22.4 10.7 %collective-permute-start.4 = (bf16[2,3,32,1024]{3,2,1,0:T(8,128)(2,1)S(1)}, bf16[2,3,32,1024]{3,2,1,0:T(8,128)(2,1)S(1)}, u32[]{:S(2)}, u32[]{:S(2)}) collective-permute-start(bf16[2,3,32,1024]{3,2,1,0:T(8,128)(2,1)S(1)} %get-tuple-element.101.refs_5_), channel_id=1, source_target_pairs={{0,48},{16,0},{32,16},{48,32},{1,49},{17,1},{33,17},{49,33},{2,50}... | collective-permute-start | bytes 1179656 | tf_op jit(solution)/shard_map/ppermute | solution.py:38
  33.1 6.4 %collective-permute-start.6 = (bf16[1,3,32,1024]{3,2,1,0:T(8,128)(2,1)S(1)}, bf16[1,3,32,1024]{3,2,1,0:T(8,128)(2,1)S(1)}, u32[]{:S(2)}, u32[]{:S(2)}) collective-permute-start(bf16[1,3,32,1024]{3,2,1,0:T(8,128)(2,1)S(1)} %get-tuple-element.71), channel_id=1, source_target_pairs={{0,64},{64,128},{128,192},{192,0},{1,65},{65,129},{129,193},{193,1... | collective-permute-start | bytes 589832 | tf_op jit(solution)/shard_map/ppermute | solution.py:38
  33.2 6.3 %collective-permute-start.7 = (bf16[1,3,32,1024]{3,2,1,0:T(8,128)(2,1)S(1)}, bf16[1,3,32,1024]{3,2,1,0:T(8,128)(2,1)S(1)}, u32[]{:S(2)}, u32[]{:S(2)}) collective-permute-start(bf16[1,3,32,1024]{3,2,1,0:T(8,128)(2,1)S(1)} %get-tuple-element.72), channel_id=1, source_target_pairs={{0,192},{64,0},{128,64},{192,128},{1,193},{65,1},{129,65},{193,129... | collective-permute-start | bytes 589832 | tf_op jit(solution)/shard_map/ppermute | solution.py:38
  35.9 5.7 %collective-permute-start.8 = (bf16[1,3,32,1024]{3,2,1,0:T(8,128)(2,1)S(1)}, bf16[1,3,32,1024]{3,2,1,0:T(8,128)(2,1)S(1)}, u32[]{:S(2)}, u32[]{:S(2)}) collective-permute-start(bf16[1,3,32,1024]{3,2,1,0:T(8,128)(2,1)S(1)} %get-tuple-element.73), channel_id=1, source_target_pairs={{0,16},{16,32},{32,48},{48,0},{1,17},{17,33},{33,49},{49,1},{2,18}... | collective-permute-start | bytes 589832 | tf_op jit(solution)/shard_map/ppermute | solution.py:38
  35.9 5.7 %collective-permute-start.9 = (bf16[1,3,32,1024]{3,2,1,0:T(8,128)(2,1)S(1)}, bf16[1,3,32,1024]{3,2,1,0:T(8,128)(2,1)S(1)}, u32[]{:S(2)}, u32[]{:S(2)}) collective-permute-start(bf16[1,3,32,1024]{3,2,1,0:T(8,128)(2,1)S(1)} %get-tuple-element.74), channel_id=1, source_target_pairs={{0,48},{16,0},{32,16},{48,32},{1,49},{17,1},{33,17},{49,33},{2,50}... | collective-permute-start | bytes 589832 | tf_op jit(solution)/shard_map/ppermute | solution.py:38
  43.5 34.5 %collective-permute-start.10 = (bf16[4,2,3,32,1024]{4,3,2,1,0:T(8,128)(2,1)}, bf16[4,2,3,32,1024]{4,3,2,1,0:T(8,128)(2,1)S(1)}, u32[]{:S(2)}, u32[]{:S(2)}) collective-permute-start(bf16[4,2,3,32,1024]{4,3,2,1,0:T(8,128)(2,1)} %get-tuple-element.75.refs_4_), channel_id=1, source_target_pairs={{0,16},{16,32},{32,48},{48,0},{1,17},{17,33},{33,49},{49,1},{2,18}... | collective-permute-start | bytes 4718600 | tf_op jit(solution)/shard_map/ppermute | solution.py:38
  43.5 34.5 %collective-permute-start.11 = (bf16[4,2,3,32,1024]{4,3,2,1,0:T(8,128)(2,1)}, bf16[4,2,3,32,1024]{4,3,2,1,0:T(8,128)(2,1)S(1)}, u32[]{:S(2)}, u32[]{:S(2)}) collective-permute-start(bf16[4,2,3,32,1024]{4,3,2,1,0:T(8,128)(2,1)} %get-tuple-element.75.refs_4_), channel_id=1, source_target_pairs={{0,48},{16,0},{32,16},{48,32},{1,49},{17,1},{33,17},{49,33},{2,50}... | collective-permute-start | bytes 4718600 | tf_op jit(solution)/shard_map/ppermute | solution.py:38
  46.2 33.9 %collective-permute-start.12 = (bf16[4,2,3,32,1024]{4,3,2,1,0:T(8,128)(2,1)}, bf16[4,2,3,32,1024]{4,3,2,1,0:T(8,128)(2,1)}, u32[]{:S(2)}, u32[]{:S(2)}) collective-permute-start(bf16[4,2,3,32,1024]{4,3,2,1,0:T(8,128)(2,1)} %get-tuple-element.76.refs_7_), channel_id=1, source_target_pairs={{0,64},{64,128},{128,192},{192,0},{1,65},{65,129},{129,193},{193,1... | collective-permute-start | bytes 4718600 | tf_op jit(solution)/shard_map/ppermute | solution.py:38
  46.2 33.9 %collective-permute-start.13 = (bf16[4,2,3,32,1024]{4,3,2,1,0:T(8,128)(2,1)}, bf16[4,2,3,32,1024]{4,3,2,1,0:T(8,128)(2,1)}, u32[]{:S(2)}, u32[]{:S(2)}) collective-permute-start(bf16[4,2,3,32,1024]{4,3,2,1,0:T(8,128)(2,1)} %get-tuple-element.76.refs_7_), channel_id=1, source_target_pairs={{0,192},{64,0},{128,64},{192,128},{1,193},{65,1},{129,65},{193,129... | collective-permute-start | bytes 4718600 | tf_op jit(solution)/shard_map/ppermute | solution.py:38
  69.5 18.3 %copy-start = (bf16[128,32,128]{2,1,0:T(8,128)(2,1)S(1)}, bf16[128,32,128]{2,1,0:T(8,128)(2,1)}, u32[]{:S(2)}) copy-start(bf16[128,32,128]{2,1,0:T(8,128)(2,1)} %all-gather.3.cloned.1.call-done) | copy-start | bytes 3145732
  69.5 18.3 %collective-permute-start.5 = (bf16[8,16,32,128]{3,2,1,0:T(8,128)(2,1)}, bf16[8,16,32,128]{3,2,1,0:T(8,128)(2,1)S(1)}, u32[]{:S(2)}, u32[]{:S(2)}) collective-permute-start(bf16[8,16,32,128]{3,2,1,0:T(8,128)(2,1)} %bitcast.37), channel_id=1, source_target_pairs={{0,8},{8,0},{1,9},{9,1},{2,10},{10,2},{3,11},{11,3},{4,12},{12,4},... | collective-permute-start | bytes 3145736 | tf_op jit(solution)/shard_map/ppermute | solution.py:38
  82.2 16.1 %collective-permute-start.14 = (bf16[2,2,3,32,1024]{4,3,2,1,0:T(8,128)(2,1)S(1)}, bf16[2,2,3,32,1024]{4,3,2,1,0:T(8,128)(2,1)S(1)}, u32[]{:S(2)}, u32[]{:S(2)}) collective-permute-start(bf16[2,2,3,32,1024]{4,3,2,1,0:T(8,128)(2,1)S(1)} %get-tuple-element.77), channel_id=1, source_target_pairs={{0,16},{16,32},{32,48},{48,0},{1,17},{17,33},{33,49},{49,1},{2,18}... | collective-permute-start | bytes 2359304 | tf_op jit(solution)/shard_map/ppermute | solution.py:38
  82.4 15.8 %collective-permute-start.15 = (bf16[2,2,3,32,1024]{4,3,2,1,0:T(8,128)(2,1)S(1)}, bf16[2,2,3,32,1024]{4,3,2,1,0:T(8,128)(2,1)S(1)}, u32[]{:S(2)}, u32[]{:S(2)}) collective-permute-start(bf16[2,2,3,32,1024]{4,3,2,1,0:T(8,128)(2,1)S(1)} %get-tuple-element.78), channel_id=1, source_target_pairs={{0,48},{16,0},{32,16},{48,32},{1,49},{17,1},{33,17},{49,33},{2,50}... | collective-permute-start | bytes 2359304 | tf_op jit(solution)/shard_map/ppermute | solution.py:38
  85.1 15.2 %collective-permute-start.16 = (bf16[2,2,3,32,1024]{4,3,2,1,0:T(8,128)(2,1)S(1)}, bf16[2,2,3,32,1024]{4,3,2,1,0:T(8,128)(2,1)S(1)}, u32[]{:S(2)}, u32[]{:S(2)}) collective-permute-start(bf16[2,2,3,32,1024]{4,3,2,1,0:T(8,128)(2,1)S(1)} %get-tuple-element.79), channel_id=1, source_target_pairs={{0,64},{64,128},{128,192},{192,0},{1,65},{65,129},{129,193},{193,1... | collective-permute-start | bytes 2359304 | tf_op jit(solution)/shard_map/ppermute | solution.py:38
  85.1 15.2 %collective-permute-start.17 = (bf16[2,2,3,32,1024]{4,3,2,1,0:T(8,128)(2,1)S(1)}, bf16[2,2,3,32,1024]{4,3,2,1,0:T(8,128)(2,1)S(1)}, u32[]{:S(2)}, u32[]{:S(2)}) collective-permute-start(bf16[2,2,3,32,1024]{4,3,2,1,0:T(8,128)(2,1)S(1)} %get-tuple-element.80), channel_id=1, source_target_pairs={{0,192},{64,0},{128,64},{192,128},{1,193},{65,1},{129,65},{193,129... | collective-permute-start | bytes 2359304 | tf_op jit(solution)/shard_map/ppermute | solution.py:38
  103.1 6.8 %collective-permute-start.18 = (f32[3,256]{1,0:T(4,128)S(1)}, f32[3,256]{1,0:T(4,128)S(1)}, u32[]{:S(2)}, u32[]{:S(2)}) collective-permute-start(f32[3,256]{1,0:T(4,128)S(1)} %slice_bitcast_fusion), channel_id=1, source_target_pairs={{0,8},{8,0},{1,9},{9,1},{2,10},{10,2},{3,11},{11,3},{4,12},{12,4},... | collective-permute-start | bytes 9224 | tf_op jit(solution)/shard_map/ppermute | solution.py:38
  109.9 16.2 %collective-permute-start.20 = (bf16[3,2,256,1024]{3,2,1,0:T(8,128)(2,1)S(1)}, bf16[3,2,256,1024]{3,2,1,0:T(8,128)(2,1)S(1)}, u32[]{:S(2)}, u32[]{:S(2)}) collective-permute-start(bf16[3,2,256,1024]{3,2,1,0:T(8,128)(2,1)S(1)} %get-tuple-element.88), channel_id=1, source_target_pairs={{0,8},{8,0},{1,9},{9,1},{2,10},{10,2},{3,11},{11,3},{4,12},{12,4},... | collective-permute-start | bytes 9437192 | tf_op jit(solution)/shard_map/ppermute | solution.py:38
  123.5 2.6 %collective-permute-start.19 = (f32[48,128]{1,0:T(8,128)S(1)}, f32[48,128]{1,0:T(8,128)S(1)}, u32[]{:S(2)}, u32[]{:S(2)}) collective-permute-start(f32[48,128]{1,0:T(8,128)S(1)} %span.1.mine_ref), channel_id=1, source_target_pairs={{0,8},{8,0},{1,9},{9,1},{2,10},{10,2},{3,11},{11,3},{4,12},{12,4},... | collective-permute-start | bytes 73736 | tf_op jit(solution)/shard_map/ppermute | solution.py:38
  (9 other events, 106.9 us)
Sparse Core Ops, SparseCore 0:
  33.2 36.2 all-gather.2

commit v3 on v2

--- a/solution.py
+++ b/solution.py
@@ -96,28 +96,32 @@
     return whole(join_kernel, "join", [((4, CN, 3, LOCAL, QUART), jnp.bfloat16)] * 2, blocks)
 
 
-def pick_kernel(z_ref, first_ref, second_ref, out_ref):
-    z = z_ref[0]
+def pick_kernel(z_ref, first_ref, second_ref, out_ref, sem):
     for array, ref in enumerate((first_ref, second_ref)):
 
-        @pl.when(z // 4 == array)
+        @pl.when(lax.rem(z_ref[0], 2) == array)
         def _():
+            copies = []
             for chip in range(XN * YN):
-                start = pl.multiple_of(chip * 2 * ROWS + lax.rem(z, 4) * 128, 128)
-                out_ref[chip] = ref[:, pl.ds(start, 128)]
+                start = pl.multiple_of((2 * chip + z_ref[0] // 2) * ROWS, ROWS)
+                columns = ref.at[:, pl.ds(start, ROWS)]
+                copies.append(pltpu.make_async_copy(columns, out_ref.at[chip], sem.at[chip]))
+                copies[-1].start()
+            for copy in copies:
+                copy.wait()
 
 
 def pick(z, first, second):
-    spec = pl.BlockSpec(memory_space=pltpu.VMEM)
     return pl.pallas_call(
         pick_kernel,
-        in_specs=[pl.BlockSpec(memory_space=pltpu.SMEM), spec, spec],
-        out_specs=spec,
-        out_shape=jax.ShapeDtypeStruct((XN * YN, LOCAL, 128), jnp.bfloat16),
+        in_specs=[pl.BlockSpec(memory_space=pltpu.SMEM)] + [pl.BlockSpec(memory_space=pl.ANY)] * 2,
+        out_specs=pl.BlockSpec(memory_space=pltpu.VMEM),
+        out_shape=pltpu.VMEM((XN * YN, LOCAL, ROWS), jnp.bfloat16),
+        scratch_shapes=[pltpu.SemaphoreType.DMA((XN * YN,))],
         compiler_params=pltpu.CompilerParams(vmem_limit_bytes=VMEM),
         cost_estimate=pl.CostEstimate(flops=0, bytes_accessed=1 << 20, transcendentals=0),
         name="pick",
-    )(z, *here(first, second))
+    )(z, first, second)
 
 
 def start_kernel(*refs):
@@ -199,8 +203,8 @@
     out_ref[...] = BETA * old_ref[...] + (1.0 - BETA) * (total * (1.0 / D) + EPS)
 
 
-def weigh_kernel(rows_ref, mine_ref, other_ref, keep_ref, got_ref, out_ref):
-    out_ref[0, 0:3] = rows_ref[...]
+def weigh_kernel(rows_ref, met_ref, mine_ref, other_ref, keep_ref, got_ref, out_ref):
+    out_ref[0, 0:3] = rows_ref[0] + met_ref[...]
     for m in range(3):
         total = jnp.zeros((ROWS, 128), jnp.float32)
         for ref, span_ref in ((keep_ref, mine_ref), (got_ref, other_ref)):
@@ -279,34 +283,38 @@
     )(core, *operands)
 
 
-def arrange_kernel(place_ref, mine_ref, other_ref, *outs):
-    x, y, core = place_ref[0], place_ref[1], place_ref[2]
+def arrange_kernel(place_ref, *refs):
+    x, y, core, quarter = (place_ref[i] for i in range(4))
+    sources, outs = refs[:4], refs[4:]
     for array in range(2):
         for part in range(4):
-            column = array * 4 + lax.rem(core + part // 2, 2) * 2 + part % 2
+            slot = lax.rem(core + part // 2 + quarter // 2, 2)
+            columns = slice(part % 2 * 128, (part % 2 + 1) * 128)
             rows = slice(part * 128, (part + 1) * 128)
             for route in range(2):
                 for outer in range(4):
                     blocks = []
                     for inner in range(4):
                         dx, dy = (ORDER[outer], ORDER[inner]) if route else (ORDER[inner], ORDER[outer])
-                        source = lax.rem(x + dx, XN) * YN + lax.rem(y + dy, YN)
-                        blocks += [mine_ref[column, source], other_ref[column, source]]
+                        chip = lax.rem(x + dx, XN) * YN + lax.rem(y + dy, YN)
+                        for own, met in (sources[:2], sources[2:]):
+                            mine, theirs = (ref[slot, chip, :, columns] for ref in (own, met))
+                            blocks.append(jnp.where(lax.rem(quarter, 2) == array, mine, theirs))
                     tokens = slice(outer * 256, (outer + 1) * 256)
                     outs[array * 2 + route][rows, tokens] = jnp.concatenate(blocks).T
 
 
-def arrange(place, mine, other):
+def arrange(place, *sources):
     spec = pl.BlockSpec(memory_space=pltpu.VMEM)
     return pl.pallas_call(
         arrange_kernel,
-        in_specs=[pl.BlockSpec(memory_space=pltpu.SMEM), spec, spec],
+        in_specs=[pl.BlockSpec(memory_space=pltpu.SMEM)] + [spec] * 4,
         out_specs=[spec] * 4,
         out_shape=[pltpu.VMEM((2 * ROWS, TOKENS), jnp.bfloat16)] * 4,
         compiler_params=pltpu.CompilerParams(vmem_limit_bytes=VMEM),
         cost_estimate=pl.CostEstimate(flops=0, bytes_accessed=6 << 20, transcendentals=0),
         name="arrange",
-    )(place, *here(mine, other))
+    )(place, *here(*sources))
 
 
 def local(
@@ -324,10 +332,10 @@
 ):
     x, y, c, z = (lax.axis_index(name) for name in ("x", "y", "c", "z"))
     core = c.astype(jnp.int32).reshape(1)
-    level = z.astype(jnp.int32).reshape(1)
-    place = jnp.stack((x, y, c)).astype(jnp.int32)
-    known = (core, level, place, c == 0, gate_pre, up_pre, hidden_grad)
-    core, level, place, first, gate_pre, up_pre, hidden_grad = lax.optimization_barrier(known)
+    quarter = lax.rem(z, 4).astype(jnp.int32).reshape(1)
+    place = jnp.stack((x, y, c, lax.rem(z, 4))).astype(jnp.int32)
+    known = (core, quarter, place, c == 0, gate_pre, up_pre, hidden_grad)
+    core, quarter, place, first, gate_pre, up_pre, hidden_grad = lax.optimization_barrier(known)
     old_span = jnp.stack((col_gate, col_up, row_down)).reshape(3, CN, 16, 128)
     old_span = jnp.where(first, old_span[:, 0], old_span[:, 1]).reshape(48, 128)
     old_width = jnp.stack((row_gate, row_up, col_down))
@@ -340,27 +348,27 @@
     own_a, own_b = own[..., :QUART], own[..., QUART:]
     near = [neighbours(own_a, "x"), neighbours(own_b, "y")]
 
-    chosen = pick(level, layer_input, output_grad)
+    chosen = pick(quarter, layer_input, output_grad)
     chosen = lax.all_to_all(chosen, ("x", "y"), split_axis=0, concat_axis=0, tiled=True)
     near, chosen, old_span, old_width = lax.optimization_barrier((near, chosen, old_span, old_width))
     far = relay(near, ("x", "y"))
-    chosen = lax.all_gather(chosen, "z")
     lines = join([own_a, *near[0], *far[0], own_b, *near[1], *far[1]])
 
     near = [neighbours(line, axis) for line, axis in zip(lines, ("y", "x"))]
     far = relay(near, ("y", "x"))
-    features = arrange(place, chosen, swap(chosen))
+    chosen = jnp.stack((chosen, lax.ppermute(chosen, "z", [(i, i ^ 2) for i in range(ZN)])))
+    met = lax.ppermute(chosen, "z", [(i, i ^ 1) for i in range(ZN)])
+    features = arrange(place, chosen, met, swap(chosen), swap(met))
     parts = [lines[0], *near[0], lines[1], *near[1]]
     keep, send, rows, cols = multiply(features, start(features, parts), [*far[0], *far[1]])
 
-    rows = rows[0] + swap(rows[1])
-    rows, cols, send = lax.optimization_barrier((rows, cols, send))
+    met = swap(rows[1])
     got = swap(send)
 
     parts = collect(cols, ("x", "y"))
     span = whole(span_kernel, "span", [((48, 128), jnp.float32)], (parts, old_span))[0]
     other = swap(span)
-    sums = whole(weigh_kernel, "weigh", [((ZN, 6, ROWS), jnp.float32)], (rows, span, other, keep, got))[0]
+    sums = whole(weigh_kernel, "weigh", [((ZN, 6, ROWS), jnp.float32)], (rows, met, span, other, keep, got))[0]
     parts = collect(sums, ("z",))
     outs = [((3, ROWS), jnp.float32), ((XN * YN * CN, 3, 128), jnp.float32)]
     width, squares = whole(width_kernel, "width", outs, (parts, old_width))

time: 167 us -> 153 us (0.916)
  between operations: 14.3 us -> 1.06 us
  Pallas kernels: 23.2 us -> 17.6 us
  starting transfers between devices: 42.9 us -> 46.2 us
  waiting for transfers between devices: 43.7 us -> 45.4 us
    ppermute x0 -> x2, waiting for transfers between devices: none -> 21.8 us  [the longest x1 11 us: local(): lax.ppermute(chosen, 'z', [(i, i ^ 2) for i in range(ZN)])]
    all_gather x1 -> x0, waiting for transfers between devices: 20.6 us -> none  [local(): chosen = lax.all_gather(chosen, 'z')]
    pallas_call x8, Pallas kernels: 16.4 us -> 10.3 us  [whole(): pl.pallas_call(kernel, in_specs=[spec] * len(operands), out_specs=[spec]...]
    ppermute x0 -> x2, starting transfers between devices: none -> 3.99 us  [the longest x1 2.99 us: local(): lax.ppermute(chosen, 'z', [(i, i ^ 2) for i in range(ZN)])]
    ppermute x21 -> x22, starting transfers between devices: 37.8 us -> 37.2 us  [shift(): lax.ppermute(value, axis, [(i, (i + step) % size) for i in range(size)])]
    ppermute x21 -> x22, waiting for transfers between devices: 22 us -> 21.5 us  [shift(): lax.ppermute(value, axis, [(i, (i + step) % size) for i in range(size)])]
  transfers between devices with their start and end apart: 23 -> 25, of which waited for: 12 -> 11; matrix products, arithmetic and copies ran while one was open for 0% -> 0% of each run, Pallas kernels for 9% -> 5%
where the time goes in v3:
time: 153 us
  starting transfers between devices  46.2 us (30%)
  waiting for transfers between devices  45.4 us (30%)
  blocking collectives  40.7 us (27%)
  Pallas kernels  17.6 us (12%)
  other arithmetic  1.9 us (1%)
    all_to_all x3, blocking collectives, collect(): return lax.all_to_all(copies, axes, split_axis=0, concat_axis=0, tiled=True)  40.7 us
    ppermute x22, starting transfers between devices, shift(): lax.ppermute(value, axis, [(i, (i + step) % size) for i in range(size)])  37.2 us
    ppermute x22, waiting for transfers between devices, shift(): lax.ppermute(value, axis, [(i, (i + step) % size) for i in range(size)])  21.5 us
    ppermute x1, waiting for transfers between devices, local(): lax.ppermute(chosen, 'z', [(i, i ^ 2) for i in range(ZN)])  11 us
    ppermute x1, waiting for transfers between devices, local(): met = lax.ppermute(chosen, 'z', [(i, i ^ 1) for i in range(ZN)])  10.8 us
    pallas_call x8, Pallas kernels, whole(): pl.pallas_call(kernel, in_specs=[spec] * len(operands), out_specs=[spec]...  10.3 us
    all_to_all x1, starting transfers between devices, local(): lax.all_to_all(chosen, ('x', 'y'), split_axis=0, concat_axis=0, tiled=True)  5.03 us
    pallas_call x1, Pallas kernels, finish(): pl.pallas_call(finish_kernel, in_specs=[pl.BlockSpec(memory_space=pltpu.S...  4.41 us
  transfers between devices with their start and end apart: 25, of which 11 were waited for; matrix products, arithmetic and copies ran while one was open for 0% of the time, Pallas kernels for 5%

profile of v3, /device:TPU:1, one launch (start us, length us, event | category | flops | bytes accessed | tf_op | source)
XLA Modules:
  0.0 152.9 jit_solution(10770513788488873758)
XLA Ops:
  2.5 3.3 %collective-permute-start = (bf16[3,32,2048]{2,1,0:T(8,128)(2,1)S(1)}, bf16[3,32,2048]{2,1,0:T(8,128)(2,1)S(1)}, u32[]{:S(2)}, u32[]{:S(2)}) collective-permute-start(bf16[3,32,2048]{2,1,0:T(8,128)(2,1)S(1)} %pad_maximum_fusion.2), channel_id=1, source_target_pairs={{0,8},{8,0},{1,9},{9,1},{2,10},{10,2},{3,11},{11,3},{4,12},{12,4},... | collective-permute-start | bytes 1179656 | tf_op jit(solution)/shard_map/ppermute | solution.py:38
  6.9 5.0 %all-to-all-start = ((bf16[16,32,256]{2,1,0:T(8,128)(2,1)}), bf16[16,32,256]{2,1,0:T(8,128)(2,1)S(1)}, u32[]{:S(2)}, u32[]{:S(2)}) async-start(bf16[16,32,256]{2,1,0:T(8,128)(2,1)} %pick.1), calls=%async_computation | async-start | bytes 524288 | tf_op jit(solution)/shard_map/all_to_all | solution.py:352
  17.6 2.1 %all-to-all-done = bf16[16,32,256]{2,1,0:T(8,128)(2,1)S(1)} async-done(((bf16[16,32,256]{2,1,0:T(8,128)(2,1)}), bf16[16,32,256]{2,1,0:T(8,128)(2,1)S(1)}, u32[]{:S(2)}, u32[]{:S(2)}) %all-to-all-start) | async-done | bytes 262176 | tf_op jit(solution)/shard_map/all_to_all | solution.py:352
  19.8 6.8 %collective-permute-done.1.refs_0_.refs_1_ = bf16[2,3,32,1024]{3,2,1,0:T(8,128)(2,1)S(1)} collective-permute-done((bf16[2,3,32,1024]{3,2,1,0:T(8,128)(2,1)S(1)}, bf16[2,3,32,1024]{3,2,1,0:T(8,128)(2,1)S(1)}, u32[]{:S(2)}, u32[]{:S(2)}) %collective-permute-start.1) | collective-permute-done | bytes 393248 | tf_op jit(solution)/shard_map/ppermute | solution.py:38
  28.6 2.6 %collective-permute-start.10 = (bf16[1,3,32,1024]{3,2,1,0:T(8,128)(2,1)S(1)}, bf16[1,3,32,1024]{3,2,1,0:T(8,128)(2,1)S(1)}, u32[]{:S(2)}, u32[]{:S(2)}) collective-permute-start(bf16[1,3,32,1024]{3,2,1,0:T(8,128)(2,1)S(1)} %get-tuple-element.69), channel_id=1, source_target_pairs={{0,192},{64,0},{128,64},{192,128},{1,193},{65,1},{129,65},{193,129... | collective-permute-start | bytes 589832 | tf_op jit(solution)/shard_map/ppermute | solution.py:38
  31.1 2.7 %collective-permute-start.12 = (bf16[1,3,32,1024]{3,2,1,0:T(8,128)(2,1)S(1)}, bf16[1,3,32,1024]{3,2,1,0:T(8,128)(2,1)S(1)}, u32[]{:S(2)}, u32[]{:S(2)}) collective-permute-start(bf16[1,3,32,1024]{3,2,1,0:T(8,128)(2,1)S(1)} %get-tuple-element.71), channel_id=1, source_target_pairs={{0,48},{16,0},{32,16},{48,32},{1,49},{17,1},{33,17},{49,33},{2,50}... | collective-permute-start | bytes 589832 | tf_op jit(solution)/shard_map/ppermute | solution.py:38
  37.7 2.7 %collective-permute-start.14 = (bf16[4,2,3,32,1024]{4,3,2,1,0:T(8,128)(2,1)S(1)}, bf16[4,2,3,32,1024]{4,3,2,1,0:T(8,128)(2,1)S(1)}, u32[]{:S(2)}, u32[]{:S(2)}) collective-permute-start(bf16[4,2,3,32,1024]{4,3,2,1,0:T(8,128)(2,1)S(1)} %get-tuple-element.72.refs_4_), channel_id=1, source_target_pairs={{0,48},{16,0},{32,16},{48,32},{1,49},{17,1},{33,17},{49,33},{2,50}... | collective-permute-start | bytes 4718600 | tf_op jit(solution)/shard_map/ppermute | solution.py:38
  40.4 2.7 %collective-permute-start.16 = (bf16[4,2,3,32,1024]{4,3,2,1,0:T(8,128)(2,1)S(1)}, bf16[4,2,3,32,1024]{4,3,2,1,0:T(8,128)(2,1)S(1)}, u32[]{:S(2)}, u32[]{:S(2)}) collective-permute-start(bf16[4,2,3,32,1024]{4,3,2,1,0:T(8,128)(2,1)S(1)} %get-tuple-element.73.refs_7_), channel_id=1, source_target_pairs={{0,192},{64,0},{128,64},{192,128},{1,193},{65,1},{129,65},{193,129... | collective-permute-start | bytes 4718600 | tf_op jit(solution)/shard_map/ppermute | solution.py:38
  43.0 3.0 %collective-permute-start.5 = (bf16[16,32,256]{2,1,0:T(8,128)(2,1)S(1)}, bf16[16,32,256]{2,1,0:T(8,128)(2,1)S(1)}, u32[]{:S(2)}, u32[]{:S(2)}) collective-permute-start(bf16[16,32,256]{2,1,0:T(8,128)(2,1)S(1)} %all-to-all-done), channel_id=1, source_target_pairs={{0,2},{1,3},{2,0},{3,1},{4,6},{5,7},{6,4},{7,5},{8,10},{9,11},{10,... | collective-permute-start | bytes 786440 | tf_op jit(solution)/shard_map/ppermute | solution.py:359
  46.0 11.0 %collective-permute-done.5 = bf16[16,32,256]{2,1,0:T(8,128)(2,1)S(1)} collective-permute-done((bf16[16,32,256]{2,1,0:T(8,128)(2,1)S(1)}, bf16[16,32,256]{2,1,0:T(8,128)(2,1)S(1)}, u32[]{:S(2)}, u32[]{:S(2)}) %collective-permute-start.5) | collective-permute-done | bytes 262176 | tf_op jit(solution)/shard_map/ppermute | solution.py:359
  58.1 10.8 %collective-permute-done.6.refs_1_ = bf16[2,16,32,256]{3,2,1,0:T(8,128)(2,1)S(1)} collective-permute-done((bf16[2,16,32,256]{3,2,1,0:T(8,128)(2,1)S(1)}, bf16[2,16,32,256]{3,2,1,0:T(8,128)(2,1)S(1)}, u32[]{:S(2)}, u32[]{:S(2)}) %collective-permute-start.6) | collective-permute-done | bytes 524320 | tf_op jit(solution)/shard_map/ppermute | solution.py:360
  68.8 2.8 %collective-permute-start.7 = (bf16[2,16,32,256]{3,2,1,0:T(8,128)(2,1)S(1)}, bf16[2,16,32,256]{3,2,1,0:T(8,128)(2,1)S(1)}, u32[]{:S(2)}, u32[]{:S(2)}) collective-permute-start(bf16[2,16,32,256]{3,2,1,0:T(8,128)(2,1)S(1)} %pad_maximum_fusion.refs_0_), channel_id=1, source_target_pairs={{0,8},{8,0},{1,9},{9,1},{2,10},{10,2},{3,11},{11,3},{4,12},{12,4},... | collective-permute-start | bytes 1572872 | tf_op jit(solution)/shard_map/ppermute | solution.py:38
  72.5 3.2 %collective-permute-start.8 = (bf16[2,16,32,256]{3,2,1,0:T(8,128)(2,1)S(1)}, bf16[2,16,32,256]{3,2,1,0:T(8,128)(2,1)S(1)}, u32[]{:S(2)}, u32[]{:S(2)}) collective-permute-start(bf16[2,16,32,256]{3,2,1,0:T(8,128)(2,1)S(1)} %collective-permute-done.6.refs_1_), channel_id=1, source_target_pairs={{0,8},{8,0},{1,9},{9,1},{2,10},{10,2},{3,11},{11,3},{4,12},{12,4},... | collective-permute-start | bytes 1572872 | tf_op jit(solution)/shard_map/ppermute | solution.py:38
  76.0 2.7 %collective-permute-start.18 = (bf16[2,2,3,32,1024]{4,3,2,1,0:T(8,128)(2,1)S(1)}, bf16[2,2,3,32,1024]{4,3,2,1,0:T(8,128)(2,1)S(1)}, u32[]{:S(2)}, u32[]{:S(2)}) collective-permute-start(bf16[2,2,3,32,1024]{4,3,2,1,0:T(8,128)(2,1)S(1)} %get-tuple-element.75), channel_id=1, source_target_pairs={{0,48},{16,0},{32,16},{48,32},{1,49},{17,1},{33,17},{49,33},{2,50}... | collective-permute-start | bytes 2359304 | tf_op jit(solution)/shard_map/ppermute | solution.py:38
  78.7 2.7 %collective-permute-start.20 = (bf16[2,2,3,32,1024]{4,3,2,1,0:T(8,128)(2,1)S(1)}, bf16[2,2,3,32,1024]{4,3,2,1,0:T(8,128)(2,1)S(1)}, u32[]{:S(2)}, u32[]{:S(2)}) collective-permute-start(bf16[2,2,3,32,1024]{4,3,2,1,0:T(8,128)(2,1)S(1)} %get-tuple-element.77), channel_id=1, source_target_pairs={{0,192},{64,0},{128,64},{192,128},{1,193},{65,1},{129,65},{193,129... | collective-permute-start | bytes 2359304 | tf_op jit(solution)/shard_map/ppermute | solution.py:38
  83.2 5.1 %start.1.refs_4_ = f32[3,2,512,1024]{3,2,1,0:T(8,128)S(1)} custom-call(bf16[512,1024]{1,0:T(8,128)(2,1)S(1)} %get-tuple-element.60.refs_0_, bf16[512,1024]{1,0:T(8,128)(2,1)S(1)} %get-tuple-element.61.refs_1_, bf16[512,1024]{1,0:T(8,128)(2,1)S(1)} %get-tuple-element.62.refs_2_, bf16[512,1024]{1,0:T(8,128)(2,1)S(1)} %get-tuple-element.63.refs_3_, ...), custom_call_target="tpu_custom_call" | custom-call | flops 4831838208 | bytes 13631488 | tf_op jit(solution)/shard_map/start/pallas_call | solution.py:56
  88.2 5.4 %collective-permute-done.17.refs_5_ = bf16[2,2,3,32,1024]{4,3,2,1,0:T(8,128)(2,1)S(1)} collective-permute-done((bf16[2,2,3,32,1024]{4,3,2,1,0:T(8,128)(2,1)S(1)}, bf16[2,2,3,32,1024]{4,3,2,1,0:T(8,128)(2,1)S(1)}, u32[]{:S(2)}, u32[]{:S(2)}) %collective-permute-start.17) | collective-permute-done | bytes 786464 | tf_op jit(solution)/shard_map/ppermute | solution.py:38
  93.6 2.1 %collective-permute-done.19.refs_7_ = bf16[2,2,3,32,1024]{4,3,2,1,0:T(8,128)(2,1)S(1)} collective-permute-done((bf16[2,2,3,32,1024]{4,3,2,1,0:T(8,128)(2,1)S(1)}, bf16[2,2,3,32,1024]{4,3,2,1,0:T(8,128)(2,1)S(1)}, u32[]{:S(2)}, u32[]{:S(2)}) %collective-permute-start.19) | collective-permute-done | bytes 786464 | tf_op jit(solution)/shard_map/ppermute | solution.py:38
  95.7 3.0 %multiply.1 = (bf16[3,2,256,1024]{3,2,1,0:T(8,128)(2,1)S(1)}, bf16[3,2,256,1024]{3,2,1,0:T(8,128)(2,1)S(1)}, f32[2,3,256]{2,1,0:T(4,128)S(1)}, f32[16,48,128]{2,1,0:T(8,128)S(1)}) custom-call(bf16[512,1024]{1,0:T(8,128)(2,1)S(1)} %get-tuple-element.60.refs_0_, bf16[512,1024]{1,0:T(8,128)(2,1)S(1)} %get-tuple-element.61.refs_1_, ...), custom_call_target="tpu_custom_call" | custom-call | flops 1610612736 | bytes 19922944 | tf_op jit(solution)/shard_map/multiply/pallas_call | solution.py:56
  98.7 4.2 %collective-permute-start.23 = (bf16[3,2,256,1024]{3,2,1,0:T(8,128)(2,1)S(1)}, bf16[3,2,256,1024]{3,2,1,0:T(8,128)(2,1)S(1)}, u32[]{:S(2)}, u32[]{:S(2)}) collective-permute-start(bf16[3,2,256,1024]{3,2,1,0:T(8,128)(2,1)S(1)} %get-tuple-element.82), channel_id=1, source_target_pairs={{0,8},{8,0},{1,9},{9,1},{2,10},{10,2},{3,11},{11,3},{4,12},{12,4},... | collective-permute-start | bytes 9437192 | tf_op jit(solution)/shard_map/ppermute | solution.py:38
  102.9 12.9 %all_to_all.20.parts_ref = f32[16,48,128]{2,1,0:T(8,128)S(1)} all-to-all(f32[16,48,128]{2,1,0:T(8,128)S(1)} %get-tuple-element.79), channel_id=1, replica_groups=mesh['x'=4,'y'=4,'c'=2,'z'=8] {'x','y'}, dimensions={0} | all-to-all | bytes 786432 | tf_op jit(solution)/shard_map/all_to_all | solution.py:82
  120.6 15.1 %all_to_all.21.parts_ref = f32[8,6,256]{2,1,0:T(8,128)S(1)} all-to-all(f32[8,6,256]{2,1,0:T(8,128)S(1)} %weigh.1), channel_id=1, replica_groups=mesh['x'=4,'y'=4,'c'=2,'z'=8] {'z'}, dimensions={0} | all-to-all | bytes 98304 | tf_op jit(solution)/shard_map/all_to_all | solution.py:82
  135.7 12.6 %all_to_all.22.parts_ref = f32[32,3,128]{2,1,0:T(4,128)S(1)} all-to-all(f32[32,3,128]{2,1,0:T(4,128)S(1)} %get-tuple-element.84), channel_id=1, replica_groups=mesh['x'=4,'y'=4,'c'=2,'z'=8] {'x','y','c'}, dimensions={0} | all-to-all | bytes 98304 | tf_op jit(solution)/shard_map/all_to_all | solution.py:82
  148.3 4.4 %finish.1 = (bf16[256,4096]{1,0:T(8,128)(2,1)}, bf16[256,4096]{1,0:T(8,128)(2,1)}, bf16[4096,256]{1,0:T(8,128)(2,1)}, f32[1,256]{1,0:T(1,128)}, f32[1,256]{1,0:T...) custom-call(s32[1]{0:T(128)} %bitcast.core_ref, ...), custom_call_target="tpu_custom_call" | custom-call | flops 12582912 | bytes 12582912 | tf_op jit(solution)/shard_map/finish/pallas_call | solution.py:272
  (66 shorter events, 23.0 us)
Async XLA Ops:
  2.5 9.6 %collective-permute-start = (bf16[3,32,2048]{2,1,0:T(8,128)(2,1)S(1)}, bf16[3,32,2048]{2,1,0:T(8,128)(2,1)S(1)}, u32[]{:S(2)}, u32[]{:S(2)}) collective-permute-start(bf16[3,32,2048]{2,1,0:T(8,128)(2,1)S(1)} %pad_maximum_fusion.2), channel_id=1, source_target_pairs={{0,8},{8,0},{1,9},{9,1},{2,10},{10,2},{3,11},{11,3},{4,12},{12,4},... | collective-permute-start | bytes 1179656 | tf_op jit(solution)/shard_map/ppermute | solution.py:38
  6.9 12.8 %all-to-all-start = ((bf16[16,32,256]{2,1,0:T(8,128)(2,1)}), bf16[16,32,256]{2,1,0:T(8,128)(2,1)S(1)}, u32[]{:S(2)}, u32[]{:S(2)}) async-start(bf16[16,32,256]{2,1,0:T(8,128)(2,1)} %pick.1), calls=%async_computation | async-start | bytes 524288 | tf_op jit(solution)/shard_map/all_to_all | solution.py:352
  12.1 14.4 %collective-permute-start.1 = (bf16[2,3,32,1024]{3,2,1,0:T(8,128)(2,1)S(1)}, bf16[2,3,32,1024]{3,2,1,0:T(8,128)(2,1)S(1)}, u32[]{:S(2)}, u32[]{:S(2)}) collective-permute-start(bf16[2,3,32,1024]{3,2,1,0:T(8,128)(2,1)S(1)} %get-tuple-element.96.refs_0_), channel_id=1, source_target_pairs={{0,64},{64,128},{128,192},{192,0},{1,65},{65,129},{129,193},{193,1... | collective-permute-start | bytes 1179656 | tf_op jit(solution)/shard_map/ppermute | solution.py:38
  13.6 13.0 %collective-permute-start.2 = (bf16[2,3,32,1024]{3,2,1,0:T(8,128)(2,1)S(1)}, bf16[2,3,32,1024]{3,2,1,0:T(8,128)(2,1)S(1)}, u32[]{:S(2)}, u32[]{:S(2)}) collective-permute-start(bf16[2,3,32,1024]{3,2,1,0:T(8,128)(2,1)S(1)} %get-tuple-element.96.refs_0_), channel_id=1, source_target_pairs={{0,192},{64,0},{128,64},{192,128},{1,193},{65,1},{129,65},{193,129... | collective-permute-start | bytes 1179656 | tf_op jit(solution)/shard_map/ppermute | solution.py:38
  14.9 13.5 %collective-permute-start.3 = (bf16[2,3,32,1024]{3,2,1,0:T(8,128)(2,1)S(1)}, bf16[2,3,32,1024]{3,2,1,0:T(8,128)(2,1)S(1)}, u32[]{:S(2)}, u32[]{:S(2)}) collective-permute-start(bf16[2,3,32,1024]{3,2,1,0:T(8,128)(2,1)S(1)} %get-tuple-element.95.refs_5_), channel_id=1, source_target_pairs={{0,16},{16,32},{32,48},{48,0},{1,17},{17,33},{33,49},{49,1},{2,18}... | collective-permute-start | bytes 1179656 | tf_op jit(solution)/shard_map/ppermute | solution.py:38
  16.2 12.1 %collective-permute-start.4 = (bf16[2,3,32,1024]{3,2,1,0:T(8,128)(2,1)S(1)}, bf16[2,3,32,1024]{3,2,1,0:T(8,128)(2,1)S(1)}, u32[]{:S(2)}, u32[]{:S(2)}) collective-permute-start(bf16[2,3,32,1024]{3,2,1,0:T(8,128)(2,1)S(1)} %get-tuple-element.95.refs_5_), channel_id=1, source_target_pairs={{0,48},{16,0},{32,16},{48,32},{1,49},{17,1},{33,17},{49,33},{2,50}... | collective-permute-start | bytes 1179656 | tf_op jit(solution)/shard_map/ppermute | solution.py:38
  28.4 6.9 %collective-permute-start.9 = (bf16[1,3,32,1024]{3,2,1,0:T(8,128)(2,1)S(1)}, bf16[1,3,32,1024]{3,2,1,0:T(8,128)(2,1)S(1)}, u32[]{:S(2)}, u32[]{:S(2)}) collective-permute-start(bf16[1,3,32,1024]{3,2,1,0:T(8,128)(2,1)S(1)} %get-tuple-element.68), channel_id=1, source_target_pairs={{0,64},{64,128},{128,192},{192,0},{1,65},{65,129},{129,193},{193,1... | collective-permute-start | bytes 589832 | tf_op jit(solution)/shard_map/ppermute | solution.py:38
  28.6 6.7 %collective-permute-start.10 = (bf16[1,3,32,1024]{3,2,1,0:T(8,128)(2,1)S(1)}, bf16[1,3,32,1024]{3,2,1,0:T(8,128)(2,1)S(1)}, u32[]{:S(2)}, u32[]{:S(2)}) collective-permute-start(bf16[1,3,32,1024]{3,2,1,0:T(8,128)(2,1)S(1)} %get-tuple-element.69), channel_id=1, source_target_pairs={{0,192},{64,0},{128,64},{192,128},{1,193},{65,1},{129,65},{193,129... | collective-permute-start | bytes 589832 | tf_op jit(solution)/shard_map/ppermute | solution.py:38
  31.1 6.2 %collective-permute-start.11 = (bf16[1,3,32,1024]{3,2,1,0:T(8,128)(2,1)S(1)}, bf16[1,3,32,1024]{3,2,1,0:T(8,128)(2,1)S(1)}, u32[]{:S(2)}, u32[]{:S(2)}) collective-permute-start(bf16[1,3,32,1024]{3,2,1,0:T(8,128)(2,1)S(1)} %get-tuple-element.70), channel_id=1, source_target_pairs={{0,16},{16,32},{32,48},{48,0},{1,17},{17,33},{33,49},{49,1},{2,18}... | collective-permute-start | bytes 589832 | tf_op jit(solution)/shard_map/ppermute | solution.py:38
  31.1 6.2 %collective-permute-start.12 = (bf16[1,3,32,1024]{3,2,1,0:T(8,128)(2,1)S(1)}, bf16[1,3,32,1024]{3,2,1,0:T(8,128)(2,1)S(1)}, u32[]{:S(2)}, u32[]{:S(2)}) collective-permute-start(bf16[1,3,32,1024]{3,2,1,0:T(8,128)(2,1)S(1)} %get-tuple-element.71), channel_id=1, source_target_pairs={{0,48},{16,0},{32,16},{48,32},{1,49},{17,1},{33,17},{49,33},{2,50}... | collective-permute-start | bytes 589832 | tf_op jit(solution)/shard_map/ppermute | solution.py:38
  37.6 34.9 %collective-permute-start.13 = (bf16[4,2,3,32,1024]{4,3,2,1,0:T(8,128)(2,1)S(1)}, bf16[4,2,3,32,1024]{4,3,2,1,0:T(8,128)(2,1)S(1)}, u32[]{:S(2)}, u32[]{:S(2)}) collective-permute-start(bf16[4,2,3,32,1024]{4,3,2,1,0:T(8,128)(2,1)S(1)} %get-tuple-element.72.refs_4_), channel_id=1, source_target_pairs={{0,16},{16,32},{32,48},{48,0},{1,17},{17,33},{33,49},{49,1},{2,18}... | collective-permute-start | bytes 4718600 | tf_op jit(solution)/shard_map/ppermute | solution.py:38
  37.7 38.0 %collective-permute-start.14 = (bf16[4,2,3,32,1024]{4,3,2,1,0:T(8,128)(2,1)S(1)}, bf16[4,2,3,32,1024]{4,3,2,1,0:T(8,128)(2,1)S(1)}, u32[]{:S(2)}, u32[]{:S(2)}) collective-permute-start(bf16[4,2,3,32,1024]{4,3,2,1,0:T(8,128)(2,1)S(1)} %get-tuple-element.72.refs_4_), channel_id=1, source_target_pairs={{0,48},{16,0},{32,16},{48,32},{1,49},{17,1},{33,17},{49,33},{2,50}... | collective-permute-start | bytes 4718600 | tf_op jit(solution)/shard_map/ppermute | solution.py:38
  40.4 35.3 %collective-permute-start.15 = (bf16[4,2,3,32,1024]{4,3,2,1,0:T(8,128)(2,1)S(1)}, bf16[4,2,3,32,1024]{4,3,2,1,0:T(8,128)(2,1)S(1)}, u32[]{:S(2)}, u32[]{:S(2)}) collective-permute-start(bf16[4,2,3,32,1024]{4,3,2,1,0:T(8,128)(2,1)S(1)} %get-tuple-element.73.refs_7_), channel_id=1, source_target_pairs={{0,64},{64,128},{128,192},{192,0},{1,65},{65,129},{129,193},{193,1... | collective-permute-start | bytes 4718600 | tf_op jit(solution)/shard_map/ppermute | solution.py:38
  40.4 35.3 %collective-permute-start.16 = (bf16[4,2,3,32,1024]{4,3,2,1,0:T(8,128)(2,1)S(1)}, bf16[4,2,3,32,1024]{4,3,2,1,0:T(8,128)(2,1)S(1)}, u32[]{:S(2)}, u32[]{:S(2)}) collective-permute-start(bf16[4,2,3,32,1024]{4,3,2,1,0:T(8,128)(2,1)S(1)} %get-tuple-element.73.refs_7_), channel_id=1, source_target_pairs={{0,192},{64,0},{128,64},{192,128},{1,193},{65,1},{129,65},{193,129... | collective-permute-start | bytes 4718600 | tf_op jit(solution)/shard_map/ppermute | solution.py:38
  43.0 14.0 %collective-permute-start.5 = (bf16[16,32,256]{2,1,0:T(8,128)(2,1)S(1)}, bf16[16,32,256]{2,1,0:T(8,128)(2,1)S(1)}, u32[]{:S(2)}, u32[]{:S(2)}) collective-permute-start(bf16[16,32,256]{2,1,0:T(8,128)(2,1)S(1)} %all-to-all-done), channel_id=1, source_target_pairs={{0,2},{1,3},{2,0},{3,1},{4,6},{5,7},{6,4},{7,5},{8,10},{9,11},{10,... | collective-permute-start | bytes 786440 | tf_op jit(solution)/shard_map/ppermute | solution.py:359
  57.1 11.8 %collective-permute-start.6 = (bf16[2,16,32,256]{3,2,1,0:T(8,128)(2,1)S(1)}, bf16[2,16,32,256]{3,2,1,0:T(8,128)(2,1)S(1)}, u32[]{:S(2)}, u32[]{:S(2)}) collective-permute-start(bf16[2,16,32,256]{3,2,1,0:T(8,128)(2,1)S(1)} %pad_maximum_fusion.refs_0_), channel_id=1, source_target_pairs={{0,1},{1,0},{2,3},{3,2},{4,5},{5,4},{6,7},{7,6},{8,9},{9,8},{10,11... | collective-permute-start | bytes 1572872 | tf_op jit(solution)/shard_map/ppermute | solution.py:360
  68.8 9.8 %collective-permute-start.7 = (bf16[2,16,32,256]{3,2,1,0:T(8,128)(2,1)S(1)}, bf16[2,16,32,256]{3,2,1,0:T(8,128)(2,1)S(1)}, u32[]{:S(2)}, u32[]{:S(2)}) collective-permute-start(bf16[2,16,32,256]{3,2,1,0:T(8,128)(2,1)S(1)} %pad_maximum_fusion.refs_0_), channel_id=1, source_target_pairs={{0,8},{8,0},{1,9},{9,1},{2,10},{10,2},{3,11},{11,3},{4,12},{12,4},... | collective-permute-start | bytes 1572872 | tf_op jit(solution)/shard_map/ppermute | solution.py:38
  72.5 8.9 %collective-permute-start.8 = (bf16[2,16,32,256]{3,2,1,0:T(8,128)(2,1)S(1)}, bf16[2,16,32,256]{3,2,1,0:T(8,128)(2,1)S(1)}, u32[]{:S(2)}, u32[]{:S(2)}) collective-permute-start(bf16[2,16,32,256]{3,2,1,0:T(8,128)(2,1)S(1)} %collective-permute-done.6.refs_1_), channel_id=1, source_target_pairs={{0,8},{8,0},{1,9},{9,1},{2,10},{10,2},{3,11},{11,3},{4,12},{12,4},... | collective-permute-start | bytes 1572872 | tf_op jit(solution)/shard_map/ppermute | solution.py:38
  75.9 17.7 %collective-permute-start.17 = (bf16[2,2,3,32,1024]{4,3,2,1,0:T(8,128)(2,1)S(1)}, bf16[2,2,3,32,1024]{4,3,2,1,0:T(8,128)(2,1)S(1)}, u32[]{:S(2)}, u32[]{:S(2)}) collective-permute-start(bf16[2,2,3,32,1024]{4,3,2,1,0:T(8,128)(2,1)S(1)} %get-tuple-element.74), channel_id=1, source_target_pairs={{0,16},{16,32},{32,48},{48,0},{1,17},{17,33},{33,49},{49,1},{2,18}... | collective-permute-start | bytes 2359304 | tf_op jit(solution)/shard_map/ppermute | solution.py:38
  76.0 17.6 %collective-permute-start.18 = (bf16[2,2,3,32,1024]{4,3,2,1,0:T(8,128)(2,1)S(1)}, bf16[2,2,3,32,1024]{4,3,2,1,0:T(8,128)(2,1)S(1)}, u32[]{:S(2)}, u32[]{:S(2)}) collective-permute-start(bf16[2,2,3,32,1024]{4,3,2,1,0:T(8,128)(2,1)S(1)} %get-tuple-element.75), channel_id=1, source_target_pairs={{0,48},{16,0},{32,16},{48,32},{1,49},{17,1},{33,17},{49,33},{2,50}... | collective-permute-start | bytes 2359304 | tf_op jit(solution)/shard_map/ppermute | solution.py:38
  78.7 17.0 %collective-permute-start.19 = (bf16[2,2,3,32,1024]{4,3,2,1,0:T(8,128)(2,1)S(1)}, bf16[2,2,3,32,1024]{4,3,2,1,0:T(8,128)(2,1)S(1)}, u32[]{:S(2)}, u32[]{:S(2)}) collective-permute-start(bf16[2,2,3,32,1024]{4,3,2,1,0:T(8,128)(2,1)S(1)} %get-tuple-element.76), channel_id=1, source_target_pairs={{0,64},{64,128},{128,192},{192,0},{1,65},{65,129},{129,193},{193,1... | collective-permute-start | bytes 2359304 | tf_op jit(solution)/shard_map/ppermute | solution.py:38
  78.7 17.0 %collective-permute-start.20 = (bf16[2,2,3,32,1024]{4,3,2,1,0:T(8,128)(2,1)S(1)}, bf16[2,2,3,32,1024]{4,3,2,1,0:T(8,128)(2,1)S(1)}, u32[]{:S(2)}, u32[]{:S(2)}) collective-permute-start(bf16[2,2,3,32,1024]{4,3,2,1,0:T(8,128)(2,1)S(1)} %get-tuple-element.77), channel_id=1, source_target_pairs={{0,192},{64,0},{128,64},{192,128},{1,193},{65,1},{129,65},{193,129... | collective-permute-start | bytes 2359304 | tf_op jit(solution)/shard_map/ppermute | solution.py:38
  98.7 20.1 %collective-permute-start.23 = (bf16[3,2,256,1024]{3,2,1,0:T(8,128)(2,1)S(1)}, bf16[3,2,256,1024]{3,2,1,0:T(8,128)(2,1)S(1)}, u32[]{:S(2)}, u32[]{:S(2)}) collective-permute-start(bf16[3,2,256,1024]{3,2,1,0:T(8,128)(2,1)S(1)} %get-tuple-element.82), channel_id=1, source_target_pairs={{0,8},{8,0},{1,9},{9,1},{2,10},{10,2},{3,11},{11,3},{4,12},{12,4},... | collective-permute-start | bytes 9437192 | tf_op jit(solution)/shard_map/ppermute | solution.py:38
  115.9 2.9 %collective-permute-start.22 = (f32[48,128]{1,0:T(8,128)S(1)}, f32[48,128]{1,0:T(8,128)S(1)}, u32[]{:S(2)}, u32[]{:S(2)}) collective-permute-start(f32[48,128]{1,0:T(8,128)S(1)} %span.1.mine_ref), channel_id=1, source_target_pairs={{0,8},{8,0},{1,9},{9,1},{2,10},{10,2},{3,11},{11,3},{4,12},{12,4},... | collective-permute-start | bytes 73736 | tf_op jit(solution)/shard_map/ppermute | solution.py:38
  (9 other events, 102.2 us)

commit v4 on v3

--- a/solution.py
+++ b/solution.py
@@ -346,9 +346,9 @@
     got = swap(halves(1 - c))
     own = jnp.stack((halves(c), got))
     own_a, own_b = own[..., :QUART], own[..., QUART:]
+    chosen = pick(quarter, layer_input, output_grad)
+    own_a, own_b, chosen = lax.optimization_barrier((own_a, own_b, chosen))
     near = [neighbours(own_a, "x"), neighbours(own_b, "y")]
-
-    chosen = pick(quarter, layer_input, output_grad)
     chosen = lax.all_to_all(chosen, ("x", "y"), split_axis=0, concat_axis=0, tiled=True)
     near, chosen, old_span, old_width = lax.optimization_barrier((near, chosen, old_span, old_width))
     far = relay(near, ("x", "y"))

time: 153 us -> 147 us (0.961)
  waiting for transfers between devices: 45.4 us -> 39 us
    ppermute x22, waiting for transfers between devices: 21.5 us -> 14.2 us  [shift(): lax.ppermute(value, axis, [(i, (i + step) % size) for i in range(size)])]
    all_to_all x1, waiting for transfers between devices: 2.13 us -> 7.25 us  [local(): lax.all_to_all(chosen, ('x', 'y'), split_axis=0, concat_axis=0, tiled=True)]
    ppermute x22, starting transfers between devices: 37.2 us -> 41.6 us  [shift(): lax.ppermute(value, axis, [(i, (i + step) % size) for i in range(size)])]
    ppermute x1, waiting for transfers between devices: 11 us -> 7.16 us  [local(): lax.ppermute(chosen, 'z', [(i, i ^ 2) for i in range(ZN)])]
  transfers between devices with their start and end apart: 25 -> 25, of which waited for: 11 -> 10; matrix products, arithmetic and copies ran while one was open for 0% -> 0% of each run, Pallas kernels for 5% -> 6%
where the time goes in v4:
time: 147 us
  starting transfers between devices  47.6 us (32%)
  blocking collectives  39.8 us (27%)
  waiting for transfers between devices  39 us (27%)
  Pallas kernels  17.6 us (12%)
  other arithmetic  1.9 us (1%)
    ppermute x22, starting transfers between devices, shift(): lax.ppermute(value, axis, [(i, (i + step) % size) for i in range(size)])  41.6 us
    all_to_all x3, blocking collectives, collect(): return lax.all_to_all(copies, axes, split_axis=0, concat_axis=0, tiled=True)  39.8 us
    ppermute x22, waiting for transfers between devices, shift(): lax.ppermute(value, axis, [(i, (i + step) % size) for i in range(size)])  14.2 us
    ppermute x1, waiting for transfers between devices, local(): met = lax.ppermute(chosen, 'z', [(i, i ^ 1) for i in range(ZN)])  10.3 us
    pallas_call x8, Pallas kernels, whole(): pl.pallas_call(kernel, in_specs=[spec] * len(operands), out_specs=[spec]...  10.3 us
    all_to_all x1, waiting for transfers between devices, local(): lax.all_to_all(chosen, ('x', 'y'), split_axis=0, concat_axis=0, tiled=True)  7.25 us
    ppermute x1, waiting for transfers between devices, local(): lax.ppermute(chosen, 'z', [(i, i ^ 2) for i in range(ZN)])  7.16 us
    pallas_call x1, Pallas kernels, finish(): pl.pallas_call(finish_kernel, in_specs=[pl.BlockSpec(memory_space=pltpu.S...  4.41 us
  transfers between devices with their start and end apart: 25, of which 10 were waited for; matrix products, arithmetic and copies ran while one was open for 0% of the time, Pallas kernels for 6%

profile of v4, /device:TPU:1, one launch (start us, length us, event | category | flops | bytes accessed | tf_op | source)
XLA Modules:
  0.0 147.0 jit_solution(16288730679100802299)
XLA Ops:
  2.5 3.3 %collective-permute-start = (bf16[3,32,2048]{2,1,0:T(8,128)(2,1)S(1)}, bf16[3,32,2048]{2,1,0:T(8,128)(2,1)S(1)}, u32[]{:S(2)}, u32[]{:S(2)}) collective-permute-start(bf16[3,32,2048]{2,1,0:T(8,128)(2,1)S(1)} %pad_maximum_fusion.2), channel_id=1, source_target_pairs={{0,8},{8,0},{1,9},{9,1},{2,10},{10,2},{3,11},{11,3},{4,12},{12,4},... | collective-permute-start | bytes 1179656 | tf_op jit(solution)/shard_map/ppermute | solution.py:38
  7.3 2.7 %collective-permute-start.2 = (bf16[2,3,32,1024]{3,2,1,0:T(8,128)(2,1)S(1)}, bf16[2,3,32,1024]{3,2,1,0:T(8,128)(2,1)S(1)}, u32[]{:S(2)}, u32[]{:S(2)}) collective-permute-start(bf16[2,3,32,1024]{3,2,1,0:T(8,128)(2,1)S(1)} %get-tuple-element.61.refs_0_), channel_id=1, source_target_pairs={{0,192},{64,0},{128,64},{192,128},{1,193},{65,1},{129,65},{193,129... | collective-permute-start | bytes 1179656 | tf_op jit(solution)/shard_map/ppermute | solution.py:38
  10.0 2.7 %collective-permute-start.4 = (bf16[2,3,32,1024]{3,2,1,0:T(8,128)(2,1)S(1)}, bf16[2,3,32,1024]{3,2,1,0:T(8,128)(2,1)S(1)}, u32[]{:S(2)}, u32[]{:S(2)}) collective-permute-start(bf16[2,3,32,1024]{3,2,1,0:T(8,128)(2,1)S(1)} %get-tuple-element.62.refs_5_), channel_id=1, source_target_pairs={{0,48},{16,0},{32,16},{48,32},{1,49},{17,1},{33,17},{49,33},{2,50}... | collective-permute-start | bytes 1179656 | tf_op jit(solution)/shard_map/ppermute | solution.py:38
  12.7 3.5 %all-to-all-start = ((bf16[16,32,256]{2,1,0:T(8,128)(2,1)}), bf16[16,32,256]{2,1,0:T(8,128)(2,1)S(1)}, u32[]{:S(2)}, u32[]{:S(2)}) async-start(bf16[16,32,256]{2,1,0:T(8,128)(2,1)} %pick.1), calls=%async_computation | async-start | bytes 524288 | tf_op jit(solution)/shard_map/all_to_all | solution.py:352
  16.3 7.3 %all-to-all-done = bf16[16,32,256]{2,1,0:T(8,128)(2,1)S(1)} async-done(((bf16[16,32,256]{2,1,0:T(8,128)(2,1)}), bf16[16,32,256]{2,1,0:T(8,128)(2,1)S(1)}, u32[]{:S(2)}, u32[]{:S(2)}) %all-to-all-start) | async-done | bytes 262176 | tf_op jit(solution)/shard_map/all_to_all | solution.py:352
  23.8 2.6 %collective-permute-start.10 = (bf16[1,3,32,1024]{3,2,1,0:T(8,128)(2,1)S(1)}, bf16[1,3,32,1024]{3,2,1,0:T(8,128)(2,1)S(1)}, u32[]{:S(2)}, u32[]{:S(2)}) collective-permute-start(bf16[1,3,32,1024]{3,2,1,0:T(8,128)(2,1)S(1)} %get-tuple-element.75), channel_id=1, source_target_pairs={{0,192},{64,0},{128,64},{192,128},{1,193},{65,1},{129,65},{193,129... | collective-permute-start | bytes 589832 | tf_op jit(solution)/shard_map/ppermute | solution.py:38
  26.5 2.5 %collective-permute-start.12 = (bf16[1,3,32,1024]{3,2,1,0:T(8,128)(2,1)S(1)}, bf16[1,3,32,1024]{3,2,1,0:T(8,128)(2,1)S(1)}, u32[]{:S(2)}, u32[]{:S(2)}) collective-permute-start(bf16[1,3,32,1024]{3,2,1,0:T(8,128)(2,1)S(1)} %get-tuple-element.77), channel_id=1, source_target_pairs={{0,48},{16,0},{32,16},{48,32},{1,49},{17,1},{33,17},{49,33},{2,50}... | collective-permute-start | bytes 589832 | tf_op jit(solution)/shard_map/ppermute | solution.py:38
  29.4 3.0 %collective-permute-done.11.refs_8_ = bf16[1,3,32,1024]{3,2,1,0:T(8,128)(2,1)S(1)} collective-permute-done((bf16[1,3,32,1024]{3,2,1,0:T(8,128)(2,1)S(1)}, bf16[1,3,32,1024]{3,2,1,0:T(8,128)(2,1)S(1)}, u32[]{:S(2)}, u32[]{:S(2)}) %collective-permute-start.11) | collective-permute-done | bytes 196640 | tf_op jit(solution)/shard_map/ppermute | solution.py:38
  32.7 2.7 %collective-permute-start.14 = (bf16[4,2,3,32,1024]{4,3,2,1,0:T(8,128)(2,1)S(1)}, bf16[4,2,3,32,1024]{4,3,2,1,0:T(8,128)(2,1)S(1)}, u32[]{:S(2)}, u32[]{:S(2)}) collective-permute-start(bf16[4,2,3,32,1024]{4,3,2,1,0:T(8,128)(2,1)S(1)} %get-tuple-element.78.refs_4_), channel_id=1, source_target_pairs={{0,48},{16,0},{32,16},{48,32},{1,49},{17,1},{33,17},{49,33},{2,50}... | collective-permute-start | bytes 4718600 | tf_op jit(solution)/shard_map/ppermute | solution.py:38
  35.4 2.7 %collective-permute-start.16 = (bf16[4,2,3,32,1024]{4,3,2,1,0:T(8,128)(2,1)S(1)}, bf16[4,2,3,32,1024]{4,3,2,1,0:T(8,128)(2,1)S(1)}, u32[]{:S(2)}, u32[]{:S(2)}) collective-permute-start(bf16[4,2,3,32,1024]{4,3,2,1,0:T(8,128)(2,1)S(1)} %get-tuple-element.79.refs_7_), channel_id=1, source_target_pairs={{0,192},{64,0},{128,64},{192,128},{1,193},{65,1},{129,65},{193,129... | collective-permute-start | bytes 4718600 | tf_op jit(solution)/shard_map/ppermute | solution.py:38
  40.1 7.2 %collective-permute-done.5 = bf16[16,32,256]{2,1,0:T(8,128)(2,1)S(1)} collective-permute-done((bf16[16,32,256]{2,1,0:T(8,128)(2,1)S(1)}, bf16[16,32,256]{2,1,0:T(8,128)(2,1)S(1)}, u32[]{:S(2)}, u32[]{:S(2)}) %collective-permute-start.5) | collective-permute-done | bytes 262176 | tf_op jit(solution)/shard_map/ppermute | solution.py:359
  47.7 10.3 %collective-permute-done.6.refs_1_ = bf16[2,16,32,256]{3,2,1,0:T(8,128)(2,1)S(1)} collective-permute-done((bf16[2,16,32,256]{3,2,1,0:T(8,128)(2,1)S(1)}, bf16[2,16,32,256]{3,2,1,0:T(8,128)(2,1)S(1)}, u32[]{:S(2)}, u32[]{:S(2)}) %collective-permute-start.6) | collective-permute-done | bytes 524320 | tf_op jit(solution)/shard_map/ppermute | solution.py:360
  58.1 5.5 %collective-permute-start.7 = (bf16[2,16,32,256]{3,2,1,0:T(8,128)(2,1)S(1)}, bf16[2,16,32,256]{3,2,1,0:T(8,128)(2,1)S(1)}, u32[]{:S(2)}, u32[]{:S(2)}) collective-permute-start(bf16[2,16,32,256]{3,2,1,0:T(8,128)(2,1)S(1)} %pad_maximum_fusion.refs_0_), channel_id=1, source_target_pairs={{0,8},{8,0},{1,9},{9,1},{2,10},{10,2},{3,11},{11,3},{4,12},{12,4},... | collective-permute-start | bytes 1572872 | tf_op jit(solution)/shard_map/ppermute | solution.py:38
  65.7 5.0 %collective-permute-start.8 = (bf16[2,16,32,256]{3,2,1,0:T(8,128)(2,1)S(1)}, bf16[2,16,32,256]{3,2,1,0:T(8,128)(2,1)S(1)}, u32[]{:S(2)}, u32[]{:S(2)}) collective-permute-start(bf16[2,16,32,256]{3,2,1,0:T(8,128)(2,1)S(1)} %collective-permute-done.6.refs_1_), channel_id=1, source_target_pairs={{0,8},{8,0},{1,9},{9,1},{2,10},{10,2},{3,11},{11,3},{4,12},{12,4},... | collective-permute-start | bytes 1572872 | tf_op jit(solution)/shard_map/ppermute | solution.py:38
  71.0 2.7 %collective-permute-start.18 = (bf16[2,2,3,32,1024]{4,3,2,1,0:T(8,128)(2,1)S(1)}, bf16[2,2,3,32,1024]{4,3,2,1,0:T(8,128)(2,1)S(1)}, u32[]{:S(2)}, u32[]{:S(2)}) collective-permute-start(bf16[2,2,3,32,1024]{4,3,2,1,0:T(8,128)(2,1)S(1)} %get-tuple-element.81), channel_id=1, source_target_pairs={{0,48},{16,0},{32,16},{48,32},{1,49},{17,1},{33,17},{49,33},{2,50}... | collective-permute-start | bytes 2359304 | tf_op jit(solution)/shard_map/ppermute | solution.py:38
  73.7 2.7 %collective-permute-start.20 = (bf16[2,2,3,32,1024]{4,3,2,1,0:T(8,128)(2,1)S(1)}, bf16[2,2,3,32,1024]{4,3,2,1,0:T(8,128)(2,1)S(1)}, u32[]{:S(2)}, u32[]{:S(2)}) collective-permute-start(bf16[2,2,3,32,1024]{4,3,2,1,0:T(8,128)(2,1)S(1)} %get-tuple-element.83), channel_id=1, source_target_pairs={{0,192},{64,0},{128,64},{192,128},{1,193},{65,1},{129,65},{193,129... | collective-permute-start | bytes 2359304 | tf_op jit(solution)/shard_map/ppermute | solution.py:38
  78.2 5.1 %start.1.refs_4_ = f32[3,2,512,1024]{3,2,1,0:T(8,128)S(1)} custom-call(bf16[512,1024]{1,0:T(8,128)(2,1)S(1)} %get-tuple-element.66.refs_0_, bf16[512,1024]{1,0:T(8,128)(2,1)S(1)} %get-tuple-element.67.refs_1_, bf16[512,1024]{1,0:T(8,128)(2,1)S(1)} %get-tuple-element.68.refs_2_, bf16[512,1024]{1,0:T(8,128)(2,1)S(1)} %get-tuple-element.69.refs_3_, ...), custom_call_target="tpu_custom_call" | custom-call | flops 4831838208 | bytes 13631488 | tf_op jit(solution)/shard_map/start/pallas_call | solution.py:56
  83.2 5.4 %collective-permute-done.17.refs_5_ = bf16[2,2,3,32,1024]{4,3,2,1,0:T(8,128)(2,1)S(1)} collective-permute-done((bf16[2,2,3,32,1024]{4,3,2,1,0:T(8,128)(2,1)S(1)}, bf16[2,2,3,32,1024]{4,3,2,1,0:T(8,128)(2,1)S(1)}, u32[]{:S(2)}, u32[]{:S(2)}) %collective-permute-start.17) | collective-permute-done | bytes 786464 | tf_op jit(solution)/shard_map/ppermute | solution.py:38
  90.7 3.0 %multiply.1 = (bf16[3,2,256,1024]{3,2,1,0:T(8,128)(2,1)S(1)}, bf16[3,2,256,1024]{3,2,1,0:T(8,128)(2,1)S(1)}, f32[2,3,256]{2,1,0:T(4,128)S(1)}, f32[16,48,128]{2,1,0:T(8,128)S(1)}) custom-call(bf16[512,1024]{1,0:T(8,128)(2,1)S(1)} %get-tuple-element.66.refs_0_, bf16[512,1024]{1,0:T(8,128)(2,1)S(1)} %get-tuple-element.67.refs_1_, ...), custom_call_target="tpu_custom_call" | custom-call | flops 1610612736 | bytes 19922944 | tf_op jit(solution)/shard_map/multiply/pallas_call | solution.py:56
  93.7 4.2 %collective-permute-start.23 = (bf16[3,2,256,1024]{3,2,1,0:T(8,128)(2,1)S(1)}, bf16[3,2,256,1024]{3,2,1,0:T(8,128)(2,1)S(1)}, u32[]{:S(2)}, u32[]{:S(2)}) collective-permute-start(bf16[3,2,256,1024]{3,2,1,0:T(8,128)(2,1)S(1)} %get-tuple-element.88), channel_id=1, source_target_pairs={{0,8},{8,0},{1,9},{9,1},{2,10},{10,2},{3,11},{11,3},{4,12},{12,4},... | collective-permute-start | bytes 9437192 | tf_op jit(solution)/shard_map/ppermute | solution.py:38
  98.0 13.0 %all_to_all.20.parts_ref = f32[16,48,128]{2,1,0:T(8,128)S(1)} all-to-all(f32[16,48,128]{2,1,0:T(8,128)S(1)} %get-tuple-element.85), channel_id=1, replica_groups=mesh['x'=4,'y'=4,'c'=2,'z'=8] {'x','y'}, dimensions={0} | all-to-all | bytes 786432 | tf_op jit(solution)/shard_map/all_to_all | solution.py:82
  115.6 14.2 %all_to_all.21.parts_ref = f32[8,6,256]{2,1,0:T(8,128)S(1)} all-to-all(f32[8,6,256]{2,1,0:T(8,128)S(1)} %weigh.1), channel_id=1, replica_groups=mesh['x'=4,'y'=4,'c'=2,'z'=8] {'z'}, dimensions={0} | all-to-all | bytes 98304 | tf_op jit(solution)/shard_map/all_to_all | solution.py:82
  129.8 12.6 %all_to_all.22.parts_ref = f32[32,3,128]{2,1,0:T(4,128)S(1)} all-to-all(f32[32,3,128]{2,1,0:T(4,128)S(1)} %get-tuple-element.90), channel_id=1, replica_groups=mesh['x'=4,'y'=4,'c'=2,'z'=8] {'x','y','c'}, dimensions={0} | all-to-all | bytes 98304 | tf_op jit(solution)/shard_map/all_to_all | solution.py:82
  142.4 4.4 %finish.1 = (bf16[256,4096]{1,0:T(8,128)(2,1)}, bf16[256,4096]{1,0:T(8,128)(2,1)}, bf16[4096,256]{1,0:T(8,128)(2,1)}, f32[1,256]{1,0:T(1,128)}, f32[1,256]{1,0:T...) custom-call(s32[1]{0:T(128)} %bitcast.core_ref, ...), custom_call_target="tpu_custom_call" | custom-call | flops 12582912 | bytes 12582912 | tf_op jit(solution)/shard_map/finish/pallas_call | solution.py:272
  (66 shorter events, 18.0 us)
Async XLA Ops:
  2.5 4.7 %collective-permute-start = (bf16[3,32,2048]{2,1,0:T(8,128)(2,1)S(1)}, bf16[3,32,2048]{2,1,0:T(8,128)(2,1)S(1)}, u32[]{:S(2)}, u32[]{:S(2)}) collective-permute-start(bf16[3,32,2048]{2,1,0:T(8,128)(2,1)S(1)} %pad_maximum_fusion.2), channel_id=1, source_target_pairs={{0,8},{8,0},{1,9},{9,1},{2,10},{10,2},{3,11},{11,3},{4,12},{12,4},... | collective-permute-start | bytes 1179656 | tf_op jit(solution)/shard_map/ppermute | solution.py:38
  7.2 16.3 %collective-permute-start.1 = (bf16[2,3,32,1024]{3,2,1,0:T(8,128)(2,1)S(1)}, bf16[2,3,32,1024]{3,2,1,0:T(8,128)(2,1)S(1)}, u32[]{:S(2)}, u32[]{:S(2)}) collective-permute-start(bf16[2,3,32,1024]{3,2,1,0:T(8,128)(2,1)S(1)} %get-tuple-element.61.refs_0_), channel_id=1, source_target_pairs={{0,64},{64,128},{128,192},{192,0},{1,65},{65,129},{129,193},{193,1... | collective-permute-start | bytes 1179656 | tf_op jit(solution)/shard_map/ppermute | solution.py:38
  7.3 16.2 %collective-permute-start.2 = (bf16[2,3,32,1024]{3,2,1,0:T(8,128)(2,1)S(1)}, bf16[2,3,32,1024]{3,2,1,0:T(8,128)(2,1)S(1)}, u32[]{:S(2)}, u32[]{:S(2)}) collective-permute-start(bf16[2,3,32,1024]{3,2,1,0:T(8,128)(2,1)S(1)} %get-tuple-element.61.refs_0_), channel_id=1, source_target_pairs={{0,192},{64,0},{128,64},{192,128},{1,193},{65,1},{129,65},{193,129... | collective-permute-start | bytes 1179656 | tf_op jit(solution)/shard_map/ppermute | solution.py:38
  10.0 13.6 %collective-permute-start.3 = (bf16[2,3,32,1024]{3,2,1,0:T(8,128)(2,1)S(1)}, bf16[2,3,32,1024]{3,2,1,0:T(8,128)(2,1)S(1)}, u32[]{:S(2)}, u32[]{:S(2)}) collective-permute-start(bf16[2,3,32,1024]{3,2,1,0:T(8,128)(2,1)S(1)} %get-tuple-element.62.refs_5_), channel_id=1, source_target_pairs={{0,16},{16,32},{32,48},{48,0},{1,17},{17,33},{33,49},{49,1},{2,18}... | collective-permute-start | bytes 1179656 | tf_op jit(solution)/shard_map/ppermute | solution.py:38
  10.0 13.6 %collective-permute-start.4 = (bf16[2,3,32,1024]{3,2,1,0:T(8,128)(2,1)S(1)}, bf16[2,3,32,1024]{3,2,1,0:T(8,128)(2,1)S(1)}, u32[]{:S(2)}, u32[]{:S(2)}) collective-permute-start(bf16[2,3,32,1024]{3,2,1,0:T(8,128)(2,1)S(1)} %get-tuple-element.62.refs_5_), channel_id=1, source_target_pairs={{0,48},{16,0},{32,16},{48,32},{1,49},{17,1},{33,17},{49,33},{2,50}... | collective-permute-start | bytes 1179656 | tf_op jit(solution)/shard_map/ppermute | solution.py:38
  12.7 10.9 %all-to-all-start = ((bf16[16,32,256]{2,1,0:T(8,128)(2,1)}), bf16[16,32,256]{2,1,0:T(8,128)(2,1)S(1)}, u32[]{:S(2)}, u32[]{:S(2)}) async-start(bf16[16,32,256]{2,1,0:T(8,128)(2,1)} %pick.1), calls=%async_computation | async-start | bytes 524288 | tf_op jit(solution)/shard_map/all_to_all | solution.py:352
  23.6 5.8 %collective-permute-start.9 = (bf16[1,3,32,1024]{3,2,1,0:T(8,128)(2,1)S(1)}, bf16[1,3,32,1024]{3,2,1,0:T(8,128)(2,1)S(1)}, u32[]{:S(2)}, u32[]{:S(2)}) collective-permute-start(bf16[1,3,32,1024]{3,2,1,0:T(8,128)(2,1)S(1)} %get-tuple-element.74), channel_id=1, source_target_pairs={{0,64},{64,128},{128,192},{192,0},{1,65},{65,129},{129,193},{193,1... | collective-permute-start | bytes 589832 | tf_op jit(solution)/shard_map/ppermute | solution.py:38
  23.8 5.6 %collective-permute-start.10 = (bf16[1,3,32,1024]{3,2,1,0:T(8,128)(2,1)S(1)}, bf16[1,3,32,1024]{3,2,1,0:T(8,128)(2,1)S(1)}, u32[]{:S(2)}, u32[]{:S(2)}) collective-permute-start(bf16[1,3,32,1024]{3,2,1,0:T(8,128)(2,1)S(1)} %get-tuple-element.75), channel_id=1, source_target_pairs={{0,192},{64,0},{128,64},{192,128},{1,193},{65,1},{129,65},{193,129... | collective-permute-start | bytes 589832 | tf_op jit(solution)/shard_map/ppermute | solution.py:38
  26.4 6.0 %collective-permute-start.11 = (bf16[1,3,32,1024]{3,2,1,0:T(8,128)(2,1)S(1)}, bf16[1,3,32,1024]{3,2,1,0:T(8,128)(2,1)S(1)}, u32[]{:S(2)}, u32[]{:S(2)}) collective-permute-start(bf16[1,3,32,1024]{3,2,1,0:T(8,128)(2,1)S(1)} %get-tuple-element.76), channel_id=1, source_target_pairs={{0,16},{16,32},{32,48},{48,0},{1,17},{17,33},{33,49},{49,1},{2,18}... | collective-permute-start | bytes 589832 | tf_op jit(solution)/shard_map/ppermute | solution.py:38
  26.5 5.9 %collective-permute-start.12 = (bf16[1,3,32,1024]{3,2,1,0:T(8,128)(2,1)S(1)}, bf16[1,3,32,1024]{3,2,1,0:T(8,128)(2,1)S(1)}, u32[]{:S(2)}, u32[]{:S(2)}) collective-permute-start(bf16[1,3,32,1024]{3,2,1,0:T(8,128)(2,1)S(1)} %get-tuple-element.77), channel_id=1, source_target_pairs={{0,48},{16,0},{32,16},{48,32},{1,49},{17,1},{33,17},{49,33},{2,50}... | collective-permute-start | bytes 589832 | tf_op jit(solution)/shard_map/ppermute | solution.py:38
  32.6 33.1 %collective-permute-start.13 = (bf16[4,2,3,32,1024]{4,3,2,1,0:T(8,128)(2,1)S(1)}, bf16[4,2,3,32,1024]{4,3,2,1,0:T(8,128)(2,1)S(1)}, u32[]{:S(2)}, u32[]{:S(2)}) collective-permute-start(bf16[4,2,3,32,1024]{4,3,2,1,0:T(8,128)(2,1)S(1)} %get-tuple-element.78.refs_4_), channel_id=1, source_target_pairs={{0,16},{16,32},{32,48},{48,0},{1,17},{17,33},{33,49},{49,1},{2,18}... | collective-permute-start | bytes 4718600 | tf_op jit(solution)/shard_map/ppermute | solution.py:38
  32.7 38.0 %collective-permute-start.14 = (bf16[4,2,3,32,1024]{4,3,2,1,0:T(8,128)(2,1)S(1)}, bf16[4,2,3,32,1024]{4,3,2,1,0:T(8,128)(2,1)S(1)}, u32[]{:S(2)}, u32[]{:S(2)}) collective-permute-start(bf16[4,2,3,32,1024]{4,3,2,1,0:T(8,128)(2,1)S(1)} %get-tuple-element.78.refs_4_), channel_id=1, source_target_pairs={{0,48},{16,0},{32,16},{48,32},{1,49},{17,1},{33,17},{49,33},{2,50}... | collective-permute-start | bytes 4718600 | tf_op jit(solution)/shard_map/ppermute | solution.py:38
  35.4 35.3 %collective-permute-start.15 = (bf16[4,2,3,32,1024]{4,3,2,1,0:T(8,128)(2,1)S(1)}, bf16[4,2,3,32,1024]{4,3,2,1,0:T(8,128)(2,1)S(1)}, u32[]{:S(2)}, u32[]{:S(2)}) collective-permute-start(bf16[4,2,3,32,1024]{4,3,2,1,0:T(8,128)(2,1)S(1)} %get-tuple-element.79.refs_7_), channel_id=1, source_target_pairs={{0,64},{64,128},{128,192},{192,0},{1,65},{65,129},{129,193},{193,1... | collective-permute-start | bytes 4718600 | tf_op jit(solution)/shard_map/ppermute | solution.py:38
  35.4 35.3 %collective-permute-start.16 = (bf16[4,2,3,32,1024]{4,3,2,1,0:T(8,128)(2,1)S(1)}, bf16[4,2,3,32,1024]{4,3,2,1,0:T(8,128)(2,1)S(1)}, u32[]{:S(2)}, u32[]{:S(2)}) collective-permute-start(bf16[4,2,3,32,1024]{4,3,2,1,0:T(8,128)(2,1)S(1)} %get-tuple-element.79.refs_7_), channel_id=1, source_target_pairs={{0,192},{64,0},{128,64},{192,128},{1,193},{65,1},{129,65},{193,129... | collective-permute-start | bytes 4718600 | tf_op jit(solution)/shard_map/ppermute | solution.py:38
  38.1 9.2 %collective-permute-start.5 = (bf16[16,32,256]{2,1,0:T(8,128)(2,1)S(1)}, bf16[16,32,256]{2,1,0:T(8,128)(2,1)S(1)}, u32[]{:S(2)}, u32[]{:S(2)}) collective-permute-start(bf16[16,32,256]{2,1,0:T(8,128)(2,1)S(1)} %all-to-all-done), channel_id=1, source_target_pairs={{0,2},{1,3},{2,0},{3,1},{4,6},{5,7},{6,4},{7,5},{8,10},{9,11},{10,... | collective-permute-start | bytes 786440 | tf_op jit(solution)/shard_map/ppermute | solution.py:359
  47.3 10.8 %collective-permute-start.6 = (bf16[2,16,32,256]{3,2,1,0:T(8,128)(2,1)S(1)}, bf16[2,16,32,256]{3,2,1,0:T(8,128)(2,1)S(1)}, u32[]{:S(2)}, u32[]{:S(2)}) collective-permute-start(bf16[2,16,32,256]{3,2,1,0:T(8,128)(2,1)S(1)} %pad_maximum_fusion.refs_0_), channel_id=1, source_target_pairs={{0,1},{1,0},{2,3},{3,2},{4,5},{5,4},{6,7},{7,6},{8,9},{9,8},{10,11... | collective-permute-start | bytes 1572872 | tf_op jit(solution)/shard_map/ppermute | solution.py:360
  58.1 15.6 %collective-permute-start.7 = (bf16[2,16,32,256]{3,2,1,0:T(8,128)(2,1)S(1)}, bf16[2,16,32,256]{3,2,1,0:T(8,128)(2,1)S(1)}, u32[]{:S(2)}, u32[]{:S(2)}) collective-permute-start(bf16[2,16,32,256]{3,2,1,0:T(8,128)(2,1)S(1)} %pad_maximum_fusion.refs_0_), channel_id=1, source_target_pairs={{0,8},{8,0},{1,9},{9,1},{2,10},{10,2},{3,11},{11,3},{4,12},{12,4},... | collective-permute-start | bytes 1572872 | tf_op jit(solution)/shard_map/ppermute | solution.py:38
  65.7 10.6 %collective-permute-start.8 = (bf16[2,16,32,256]{3,2,1,0:T(8,128)(2,1)S(1)}, bf16[2,16,32,256]{3,2,1,0:T(8,128)(2,1)S(1)}, u32[]{:S(2)}, u32[]{:S(2)}) collective-permute-start(bf16[2,16,32,256]{3,2,1,0:T(8,128)(2,1)S(1)} %collective-permute-done.6.refs_1_), channel_id=1, source_target_pairs={{0,8},{8,0},{1,9},{9,1},{2,10},{10,2},{3,11},{11,3},{4,12},{12,4},... | collective-permute-start | bytes 1572872 | tf_op jit(solution)/shard_map/ppermute | solution.py:38
  70.9 17.7 %collective-permute-start.17 = (bf16[2,2,3,32,1024]{4,3,2,1,0:T(8,128)(2,1)S(1)}, bf16[2,2,3,32,1024]{4,3,2,1,0:T(8,128)(2,1)S(1)}, u32[]{:S(2)}, u32[]{:S(2)}) collective-permute-start(bf16[2,2,3,32,1024]{4,3,2,1,0:T(8,128)(2,1)S(1)} %get-tuple-element.80), channel_id=1, source_target_pairs={{0,16},{16,32},{32,48},{48,0},{1,17},{17,33},{33,49},{49,1},{2,18}... | collective-permute-start | bytes 2359304 | tf_op jit(solution)/shard_map/ppermute | solution.py:38
  71.0 17.6 %collective-permute-start.18 = (bf16[2,2,3,32,1024]{4,3,2,1,0:T(8,128)(2,1)S(1)}, bf16[2,2,3,32,1024]{4,3,2,1,0:T(8,128)(2,1)S(1)}, u32[]{:S(2)}, u32[]{:S(2)}) collective-permute-start(bf16[2,2,3,32,1024]{4,3,2,1,0:T(8,128)(2,1)S(1)} %get-tuple-element.81), channel_id=1, source_target_pairs={{0,48},{16,0},{32,16},{48,32},{1,49},{17,1},{33,17},{49,33},{2,50}... | collective-permute-start | bytes 2359304 | tf_op jit(solution)/shard_map/ppermute | solution.py:38
  73.7 17.0 %collective-permute-start.19 = (bf16[2,2,3,32,1024]{4,3,2,1,0:T(8,128)(2,1)S(1)}, bf16[2,2,3,32,1024]{4,3,2,1,0:T(8,128)(2,1)S(1)}, u32[]{:S(2)}, u32[]{:S(2)}) collective-permute-start(bf16[2,2,3,32,1024]{4,3,2,1,0:T(8,128)(2,1)S(1)} %get-tuple-element.82), channel_id=1, source_target_pairs={{0,64},{64,128},{128,192},{192,0},{1,65},{65,129},{129,193},{193,1... | collective-permute-start | bytes 2359304 | tf_op jit(solution)/shard_map/ppermute | solution.py:38
  73.7 17.0 %collective-permute-start.20 = (bf16[2,2,3,32,1024]{4,3,2,1,0:T(8,128)(2,1)S(1)}, bf16[2,2,3,32,1024]{4,3,2,1,0:T(8,128)(2,1)S(1)}, u32[]{:S(2)}, u32[]{:S(2)}) collective-permute-start(bf16[2,2,3,32,1024]{4,3,2,1,0:T(8,128)(2,1)S(1)} %get-tuple-element.83), channel_id=1, source_target_pairs={{0,192},{64,0},{128,64},{192,128},{1,193},{65,1},{129,65},{193,129... | collective-permute-start | bytes 2359304 | tf_op jit(solution)/shard_map/ppermute | solution.py:38
  93.7 20.1 %collective-permute-start.23 = (bf16[3,2,256,1024]{3,2,1,0:T(8,128)(2,1)S(1)}, bf16[3,2,256,1024]{3,2,1,0:T(8,128)(2,1)S(1)}, u32[]{:S(2)}, u32[]{:S(2)}) collective-permute-start(bf16[3,2,256,1024]{3,2,1,0:T(8,128)(2,1)S(1)} %get-tuple-element.88), channel_id=1, source_target_pairs={{0,8},{8,0},{1,9},{9,1},{2,10},{10,2},{3,11},{11,3},{4,12},{12,4},... | collective-permute-start | bytes 9437192 | tf_op jit(solution)/shard_map/ppermute | solution.py:38
  110.9 2.9 %collective-permute-start.22 = (f32[48,128]{1,0:T(8,128)S(1)}, f32[48,128]{1,0:T(8,128)S(1)}, u32[]{:S(2)}, u32[]{:S(2)}) collective-permute-start(f32[48,128]{1,0:T(8,128)S(1)} %span.1.mine_ref), channel_id=1, source_target_pairs={{0,8},{8,0},{1,9},{9,1},{2,10},{10,2},{3,11},{11,3},{4,12},{12,4},... | collective-permute-start | bytes 73736 | tf_op jit(solution)/shard_map/ppermute | solution.py:38
  (9 other events, 83.7 us)

commit v5 on v4

--- a/solution.py
+++ b/solution.py
@@ -350,8 +350,9 @@
     own_a, own_b, chosen = lax.optimization_barrier((own_a, own_b, chosen))
     near = [neighbours(own_a, "x"), neighbours(own_b, "y")]
     chosen = lax.all_to_all(chosen, ("x", "y"), split_axis=0, concat_axis=0, tiled=True)
-    near, chosen, old_span, old_width = lax.optimization_barrier((near, chosen, old_span, old_width))
+    near, old_span, old_width = lax.optimization_barrier((near, old_span, old_width))
     far = relay(near, ("x", "y"))
+    far, chosen = lax.optimization_barrier((far, chosen))
     lines = join([own_a, *near[0], *far[0], own_b, *near[1], *far[1]])
 
     near = [neighbours(line, axis) for line, axis in zip(lines, ("y", "x"))]

time: 147 us -> 146 us (level)
  waiting for transfers between devices: 39 us -> 35.8 us
    all_to_all x1, waiting for transfers between devices: 7.25 us -> 0.01 us  [local(): lax.all_to_all(chosen, ('x', 'y'), split_axis=0, concat_axis=0, tiled=True)]
    ppermute x22, waiting for transfers between devices: 14.2 us -> 16.8 us  [shift(): lax.ppermute(value, axis, [(i, (i + step) % size) for i in range(size)])]
  transfers between devices with their start and end apart: 25 -> 25, of which waited for: 10 -> 10; matrix products, arithmetic and copies ran while one was open for 0% -> 1% of each run, Pallas kernels for 6% -> 6%
where the time goes in v5:
time: 146 us
  starting transfers between devices  48.3 us (33%)
  blocking collectives  39.3 us (27%)
  waiting for transfers between devices  35.8 us (25%)
  Pallas kernels  18.4 us (13%)
  other arithmetic  2.84 us (2%)
    ppermute x22, starting transfers between devices, shift(): lax.ppermute(value, axis, [(i, (i + step) % size) for i in range(size)])  42.8 us
    all_to_all x3, blocking collectives, collect(): return lax.all_to_all(copies, axes, split_axis=0, concat_axis=0, tiled=True)  39.3 us
    ppermute x22, waiting for transfers between devices, shift(): lax.ppermute(value, axis, [(i, (i + step) % size) for i in range(size)])  16.8 us
    pallas_call x8, Pallas kernels, whole(): pl.pallas_call(kernel, in_specs=[spec] * len(operands), out_specs=[spec]...  11.1 us
    ppermute x1, waiting for transfers between devices, local(): met = lax.ppermute(chosen, 'z', [(i, i ^ 1) for i in range(ZN)])  10.6 us
    ppermute x1, waiting for transfers between devices, local(): lax.ppermute(chosen, 'z', [(i, i ^ 2) for i in range(ZN)])  8.43 us
    pallas_call x1, Pallas kernels, finish(): pl.pallas_call(finish_kernel, in_specs=[pl.BlockSpec(memory_space=pltpu.S...  4.41 us
    all_to_all x1, starting transfers between devices, local(): lax.all_to_all(chosen, ('x', 'y'), split_axis=0, concat_axis=0, tiled=True)  4.21 us
  transfers between devices with their start and end apart: 25, of which 10 were waited for; matrix products, arithmetic and copies ran while one was open for 1% of the time, Pallas kernels for 6%

profile of v5, /device:TPU:1, one launch (start us, length us, event | category | flops | bytes accessed | tf_op | source)
XLA Modules:
  0.0 145.8 jit_solution(16929347627469512228)
XLA Ops:
  2.5 3.3 %collective-permute-start = (bf16[3,32,2048]{2,1,0:T(8,128)(2,1)S(1)}, bf16[3,32,2048]{2,1,0:T(8,128)(2,1)S(1)}, u32[]{:S(2)}, u32[]{:S(2)}) collective-permute-start(bf16[3,32,2048]{2,1,0:T(8,128)(2,1)S(1)} %pad_maximum_fusion.2), channel_id=1, source_target_pairs={{0,8},{8,0},{1,9},{9,1},{2,10},{10,2},{3,11},{11,3},{4,12},{12,4},... | collective-permute-start | bytes 1179656 | tf_op jit(solution)/shard_map/ppermute | solution.py:38
  7.3 2.7 %collective-permute-start.2 = (bf16[2,3,32,1024]{3,2,1,0:T(8,128)(2,1)S(1)}, bf16[2,3,32,1024]{3,2,1,0:T(8,128)(2,1)S(1)}, u32[]{:S(2)}, u32[]{:S(2)}) collective-permute-start(bf16[2,3,32,1024]{3,2,1,0:T(8,128)(2,1)S(1)} %get-tuple-element.65.refs_0_), channel_id=1, source_target_pairs={{0,192},{64,0},{128,64},{192,128},{1,193},{65,1},{129,65},{193,129... | collective-permute-start | bytes 1179656 | tf_op jit(solution)/shard_map/ppermute | solution.py:38
  10.0 2.7 %collective-permute-start.4 = (bf16[2,3,32,1024]{3,2,1,0:T(8,128)(2,1)S(1)}, bf16[2,3,32,1024]{3,2,1,0:T(8,128)(2,1)S(1)}, u32[]{:S(2)}, u32[]{:S(2)}) collective-permute-start(bf16[2,3,32,1024]{3,2,1,0:T(8,128)(2,1)S(1)} %get-tuple-element.66.refs_5_), channel_id=1, source_target_pairs={{0,48},{16,0},{32,16},{48,32},{1,49},{17,1},{33,17},{49,33},{2,50}... | collective-permute-start | bytes 1179656 | tf_op jit(solution)/shard_map/ppermute | solution.py:38
  12.7 4.2 %all-to-all-start = ((bf16[16,32,256]{2,1,0:T(8,128)(2,1)}), bf16[16,32,256]{2,1,0:T(8,128)(2,1)}, u32[]{:S(2)}, u32[]{:S(2)}) async-start(bf16[16,32,256]{2,1,0:T(8,128)(2,1)} %pick.1), calls=%async_computation | async-start | bytes 524288 | tf_op jit(solution)/shard_map/all_to_all | solution.py:352
  21.7 2.7 %collective-permute-start.6 = (bf16[1,3,32,1024]{3,2,1,0:T(8,128)(2,1)}, bf16[1,3,32,1024]{3,2,1,0:T(8,128)(2,1)S(1)}, u32[]{:S(2)}, u32[]{:S(2)}) collective-permute-start(bf16[1,3,32,1024]{3,2,1,0:T(8,128)(2,1)} %get-tuple-element.73), channel_id=1, source_target_pairs={{0,192},{64,0},{128,64},{192,128},{1,193},{65,1},{129,65},{193,129... | collective-permute-start | bytes 589832 | tf_op jit(solution)/shard_map/ppermute | solution.py:38
  24.4 3.1 %collective-permute-start.8 = (bf16[1,3,32,1024]{3,2,1,0:T(8,128)(2,1)S(1)}, bf16[1,3,32,1024]{3,2,1,0:T(8,128)(2,1)S(1)}, u32[]{:S(2)}, u32[]{:S(2)}) collective-permute-start(bf16[1,3,32,1024]{3,2,1,0:T(8,128)(2,1)S(1)} %get-tuple-element.75), channel_id=1, source_target_pairs={{0,48},{16,0},{32,16},{48,32},{1,49},{17,1},{33,17},{49,33},{2,50}... | collective-permute-start | bytes 589832 | tf_op jit(solution)/shard_map/ppermute | solution.py:38
  27.7 3.4 %collective-permute-done.7.refs_8_ = bf16[1,3,32,1024]{3,2,1,0:T(8,128)(2,1)S(1)} collective-permute-done((bf16[1,3,32,1024]{3,2,1,0:T(8,128)(2,1)}, bf16[1,3,32,1024]{3,2,1,0:T(8,128)(2,1)S(1)}, u32[]{:S(2)}, u32[]{:S(2)}) %collective-permute-start.7) | collective-permute-done | bytes 196640 | tf_op jit(solution)/shard_map/ppermute | solution.py:38
  31.7 2.3 %collective-permute-start.14 = (bf16[4,2,3,32,1024]{4,3,2,1,0:T(8,128)(2,1)S(1)}, bf16[4,2,3,32,1024]{4,3,2,1,0:T(8,128)(2,1)S(1)}, u32[]{:S(2)}, u32[]{:S(2)}) collective-permute-start(bf16[4,2,3,32,1024]{4,3,2,1,0:T(8,128)(2,1)S(1)} %get-tuple-element.86.refs_4_), channel_id=1, source_target_pairs={{0,48},{16,0},{32,16},{48,32},{1,49},{17,1},{33,17},{49,33},{2,50}... | collective-permute-start | bytes 4718600 | tf_op jit(solution)/shard_map/ppermute | solution.py:38
  34.0 2.7 %collective-permute-start.16 = (bf16[4,2,3,32,1024]{4,3,2,1,0:T(8,128)(2,1)S(1)}, bf16[4,2,3,32,1024]{4,3,2,1,0:T(8,128)(2,1)S(1)}, u32[]{:S(2)}, u32[]{:S(2)}) collective-permute-start(bf16[4,2,3,32,1024]{4,3,2,1,0:T(8,128)(2,1)S(1)} %get-tuple-element.87.refs_7_), channel_id=1, source_target_pairs={{0,192},{64,0},{128,64},{192,128},{1,193},{65,1},{129,65},{193,129... | collective-permute-start | bytes 4718600 | tf_op jit(solution)/shard_map/ppermute | solution.py:38
  37.7 8.4 %collective-permute-done.9 = bf16[16,32,256]{2,1,0:T(8,128)(2,1)S(1)} collective-permute-done((bf16[16,32,256]{2,1,0:T(8,128)(2,1)}, bf16[16,32,256]{2,1,0:T(8,128)(2,1)S(1)}, u32[]{:S(2)}, u32[]{:S(2)}) %collective-permute-start.9) | collective-permute-done | bytes 262176 | tf_op jit(solution)/shard_map/ppermute | solution.py:360
  47.4 10.6 %collective-permute-done.10.refs_1_ = bf16[2,16,32,256]{3,2,1,0:T(8,128)(2,1)S(1)} collective-permute-done((bf16[2,16,32,256]{3,2,1,0:T(8,128)(2,1)S(1)}, bf16[2,16,32,256]{3,2,1,0:T(8,128)(2,1)S(1)}, u32[]{:S(2)}, u32[]{:S(2)}) %collective-permute-start.10) | collective-permute-done | bytes 524320 | tf_op jit(solution)/shard_map/ppermute | solution.py:361
  58.0 6.4 %collective-permute-start.11 = (bf16[2,16,32,256]{3,2,1,0:T(8,128)(2,1)S(1)}, bf16[2,16,32,256]{3,2,1,0:T(8,128)(2,1)S(1)}, u32[]{:S(2)}, u32[]{:S(2)}) collective-permute-start(bf16[2,16,32,256]{3,2,1,0:T(8,128)(2,1)S(1)} %pad_maximum_fusion.refs_0_), channel_id=1, source_target_pairs={{0,8},{8,0},{1,9},{9,1},{2,10},{10,2},{3,11},{11,3},{4,12},{12,4},... | collective-permute-start | bytes 1572872 | tf_op jit(solution)/shard_map/ppermute | solution.py:38
  64.4 5.6 %collective-permute-start.12 = (bf16[2,16,32,256]{3,2,1,0:T(8,128)(2,1)S(1)}, bf16[2,16,32,256]{3,2,1,0:T(8,128)(2,1)S(1)}, u32[]{:S(2)}, u32[]{:S(2)}) collective-permute-start(bf16[2,16,32,256]{3,2,1,0:T(8,128)(2,1)S(1)} %collective-permute-done.10.refs_1_), channel_id=1, source_target_pairs={{0,8},{8,0},{1,9},{9,1},{2,10},{10,2},{3,11},{11,3},{4,12},{12,4},... | collective-permute-start | bytes 1572872 | tf_op jit(solution)/shard_map/ppermute | solution.py:38
  70.3 2.7 %collective-permute-start.18 = (bf16[2,2,3,32,1024]{4,3,2,1,0:T(8,128)(2,1)S(1)}, bf16[2,2,3,32,1024]{4,3,2,1,0:T(8,128)(2,1)S(1)}, u32[]{:S(2)}, u32[]{:S(2)}) collective-permute-start(bf16[2,2,3,32,1024]{4,3,2,1,0:T(8,128)(2,1)S(1)} %get-tuple-element.89), channel_id=1, source_target_pairs={{0,48},{16,0},{32,16},{48,32},{1,49},{17,1},{33,17},{49,33},{2,50}... | collective-permute-start | bytes 2359304 | tf_op jit(solution)/shard_map/ppermute | solution.py:38
  73.0 2.7 %collective-permute-start.20 = (bf16[2,2,3,32,1024]{4,3,2,1,0:T(8,128)(2,1)S(1)}, bf16[2,2,3,32,1024]{4,3,2,1,0:T(8,128)(2,1)S(1)}, u32[]{:S(2)}, u32[]{:S(2)}) collective-permute-start(bf16[2,2,3,32,1024]{4,3,2,1,0:T(8,128)(2,1)S(1)} %get-tuple-element.91), channel_id=1, source_target_pairs={{0,192},{64,0},{128,64},{192,128},{1,193},{65,1},{129,65},{193,129... | collective-permute-start | bytes 2359304 | tf_op jit(solution)/shard_map/ppermute | solution.py:38
  77.4 5.1 %start.1.refs_4_ = f32[3,2,512,1024]{3,2,1,0:T(8,128)S(1)} custom-call(bf16[512,1024]{1,0:T(8,128)(2,1)S(1)} %get-tuple-element.78.refs_0_, bf16[512,1024]{1,0:T(8,128)(2,1)S(1)} %get-tuple-element.79.refs_1_, bf16[512,1024]{1,0:T(8,128)(2,1)S(1)} %get-tuple-element.80.refs_2_, bf16[512,1024]{1,0:T(8,128)(2,1)S(1)} %get-tuple-element.81.refs_3_, ...), custom_call_target="tpu_custom_call" | custom-call | flops 4831838208 | bytes 13631488 | tf_op jit(solution)/shard_map/start/pallas_call | solution.py:56
  82.5 6.0 %collective-permute-done.17.refs_5_ = bf16[2,2,3,32,1024]{4,3,2,1,0:T(8,128)(2,1)S(1)} collective-permute-done((bf16[2,2,3,32,1024]{4,3,2,1,0:T(8,128)(2,1)S(1)}, bf16[2,2,3,32,1024]{4,3,2,1,0:T(8,128)(2,1)S(1)}, u32[]{:S(2)}, u32[]{:S(2)}) %collective-permute-start.17) | collective-permute-done | bytes 786464 | tf_op jit(solution)/shard_map/ppermute | solution.py:38
  88.5 2.1 %collective-permute-done.19.refs_7_ = bf16[2,2,3,32,1024]{4,3,2,1,0:T(8,128)(2,1)S(1)} collective-permute-done((bf16[2,2,3,32,1024]{4,3,2,1,0:T(8,128)(2,1)S(1)}, bf16[2,2,3,32,1024]{4,3,2,1,0:T(8,128)(2,1)S(1)}, u32[]{:S(2)}, u32[]{:S(2)}) %collective-permute-start.19) | collective-permute-done | bytes 786464 | tf_op jit(solution)/shard_map/ppermute | solution.py:38
  90.6 3.0 %multiply.1 = (bf16[3,2,256,1024]{3,2,1,0:T(8,128)(2,1)S(1)}, bf16[3,2,256,1024]{3,2,1,0:T(8,128)(2,1)S(1)}, f32[2,3,256]{2,1,0:T(4,128)S(1)}, f32[16,48,128]{2,1,0:T(8,128)S(1)}) custom-call(bf16[512,1024]{1,0:T(8,128)(2,1)S(1)} %get-tuple-element.78.refs_0_, bf16[512,1024]{1,0:T(8,128)(2,1)S(1)} %get-tuple-element.79.refs_1_, ...), custom_call_target="tpu_custom_call" | custom-call | flops 1610612736 | bytes 19922944 | tf_op jit(solution)/shard_map/multiply/pallas_call | solution.py:56
  93.6 3.6 %collective-permute-start.23 = (bf16[3,2,256,1024]{3,2,1,0:T(8,128)(2,1)S(1)}, bf16[3,2,256,1024]{3,2,1,0:T(8,128)(2,1)S(1)}, u32[]{:S(2)}, u32[]{:S(2)}) collective-permute-start(bf16[3,2,256,1024]{3,2,1,0:T(8,128)(2,1)S(1)} %get-tuple-element.96), channel_id=1, source_target_pairs={{0,8},{8,0},{1,9},{9,1},{2,10},{10,2},{3,11},{11,3},{4,12},{12,4},... | collective-permute-start | bytes 9437192 | tf_op jit(solution)/shard_map/ppermute | solution.py:38
  97.2 13.2 %all_to_all.20.parts_ref = f32[16,48,128]{2,1,0:T(8,128)S(1)} all-to-all(f32[16,48,128]{2,1,0:T(8,128)S(1)} %get-tuple-element.93), channel_id=1, replica_groups=mesh['x'=4,'y'=4,'c'=2,'z'=8] {'x','y'}, dimensions={0} | all-to-all | bytes 786432 | tf_op jit(solution)/shard_map/all_to_all | solution.py:82
  115.1 13.5 %all_to_all.21.parts_ref = f32[8,6,256]{2,1,0:T(8,128)S(1)} all-to-all(f32[8,6,256]{2,1,0:T(8,128)S(1)} %weigh.1), channel_id=1, replica_groups=mesh['x'=4,'y'=4,'c'=2,'z'=8] {'z'}, dimensions={0} | all-to-all | bytes 98304 | tf_op jit(solution)/shard_map/all_to_all | solution.py:82
  128.6 12.6 %all_to_all.22.parts_ref = f32[32,3,128]{2,1,0:T(4,128)S(1)} all-to-all(f32[32,3,128]{2,1,0:T(4,128)S(1)} %get-tuple-element.98), channel_id=1, replica_groups=mesh['x'=4,'y'=4,'c'=2,'z'=8] {'x','y','c'}, dimensions={0} | all-to-all | bytes 98304 | tf_op jit(solution)/shard_map/all_to_all | solution.py:82
  141.2 4.4 %finish.1 = (bf16[256,4096]{1,0:T(8,128)(2,1)}, bf16[256,4096]{1,0:T(8,128)(2,1)}, bf16[4096,256]{1,0:T(8,128)(2,1)}, f32[1,256]{1,0:T(1,128)}, f32[1,256]{1,0:T...) custom-call(s32[1]{0:T(128)} %bitcast.core_ref, ...), custom_call_target="tpu_custom_call" | custom-call | flops 12582912 | bytes 12582912 | tf_op jit(solution)/shard_map/finish/pallas_call | solution.py:272
  (66 shorter events, 17.9 us)
Async XLA Ops:
  2.5 4.7 %collective-permute-start = (bf16[3,32,2048]{2,1,0:T(8,128)(2,1)S(1)}, bf16[3,32,2048]{2,1,0:T(8,128)(2,1)S(1)}, u32[]{:S(2)}, u32[]{:S(2)}) collective-permute-start(bf16[3,32,2048]{2,1,0:T(8,128)(2,1)S(1)} %pad_maximum_fusion.2), channel_id=1, source_target_pairs={{0,8},{8,0},{1,9},{9,1},{2,10},{10,2},{3,11},{11,3},{4,12},{12,4},... | collective-permute-start | bytes 1179656 | tf_op jit(solution)/shard_map/ppermute | solution.py:38
  7.2 11.6 %collective-permute-start.1 = (bf16[2,3,32,1024]{3,2,1,0:T(8,128)(2,1)S(1)}, bf16[2,3,32,1024]{3,2,1,0:T(8,128)(2,1)S(1)}, u32[]{:S(2)}, u32[]{:S(2)}) collective-permute-start(bf16[2,3,32,1024]{3,2,1,0:T(8,128)(2,1)S(1)} %get-tuple-element.65.refs_0_), channel_id=1, source_target_pairs={{0,64},{64,128},{128,192},{192,0},{1,65},{65,129},{129,193},{193,1... | collective-permute-start | bytes 1179656 | tf_op jit(solution)/shard_map/ppermute | solution.py:38
  7.3 11.5 %collective-permute-start.2 = (bf16[2,3,32,1024]{3,2,1,0:T(8,128)(2,1)S(1)}, bf16[2,3,32,1024]{3,2,1,0:T(8,128)(2,1)S(1)}, u32[]{:S(2)}, u32[]{:S(2)}) collective-permute-start(bf16[2,3,32,1024]{3,2,1,0:T(8,128)(2,1)S(1)} %get-tuple-element.65.refs_0_), channel_id=1, source_target_pairs={{0,192},{64,0},{128,64},{192,128},{1,193},{65,1},{129,65},{193,129... | collective-permute-start | bytes 1179656 | tf_op jit(solution)/shard_map/ppermute | solution.py:38
  10.0 10.9 %collective-permute-start.3 = (bf16[2,3,32,1024]{3,2,1,0:T(8,128)(2,1)S(1)}, bf16[2,3,32,1024]{3,2,1,0:T(8,128)(2,1)S(1)}, u32[]{:S(2)}, u32[]{:S(2)}) collective-permute-start(bf16[2,3,32,1024]{3,2,1,0:T(8,128)(2,1)S(1)} %get-tuple-element.66.refs_5_), channel_id=1, source_target_pairs={{0,16},{16,32},{32,48},{48,0},{1,17},{17,33},{33,49},{49,1},{2,18}... | collective-permute-start | bytes 1179656 | tf_op jit(solution)/shard_map/ppermute | solution.py:38
  10.0 10.9 %collective-permute-start.4 = (bf16[2,3,32,1024]{3,2,1,0:T(8,128)(2,1)S(1)}, bf16[2,3,32,1024]{3,2,1,0:T(8,128)(2,1)S(1)}, u32[]{:S(2)}, u32[]{:S(2)}) collective-permute-start(bf16[2,3,32,1024]{3,2,1,0:T(8,128)(2,1)S(1)} %get-tuple-element.66.refs_5_), channel_id=1, source_target_pairs={{0,48},{16,0},{32,16},{48,32},{1,49},{17,1},{33,17},{49,33},{2,50}... | collective-permute-start | bytes 1179656 | tf_op jit(solution)/shard_map/ppermute | solution.py:38
  12.7 14.8 %all-to-all-start = ((bf16[16,32,256]{2,1,0:T(8,128)(2,1)}), bf16[16,32,256]{2,1,0:T(8,128)(2,1)}, u32[]{:S(2)}, u32[]{:S(2)}) async-start(bf16[16,32,256]{2,1,0:T(8,128)(2,1)} %pick.1), calls=%async_computation | async-start | bytes 524288 | tf_op jit(solution)/shard_map/all_to_all | solution.py:352
  21.7 5.9 %collective-permute-start.5 = (bf16[1,3,32,1024]{3,2,1,0:T(8,128)(2,1)}, bf16[1,3,32,1024]{3,2,1,0:T(8,128)(2,1)S(1)}, u32[]{:S(2)}, u32[]{:S(2)}) collective-permute-start(bf16[1,3,32,1024]{3,2,1,0:T(8,128)(2,1)} %get-tuple-element.72), channel_id=1, source_target_pairs={{0,64},{64,128},{128,192},{192,0},{1,65},{65,129},{129,193},{193,1... | collective-permute-start | bytes 589832 | tf_op jit(solution)/shard_map/ppermute | solution.py:38
  21.7 5.9 %collective-permute-start.6 = (bf16[1,3,32,1024]{3,2,1,0:T(8,128)(2,1)}, bf16[1,3,32,1024]{3,2,1,0:T(8,128)(2,1)S(1)}, u32[]{:S(2)}, u32[]{:S(2)}) collective-permute-start(bf16[1,3,32,1024]{3,2,1,0:T(8,128)(2,1)} %get-tuple-element.73), channel_id=1, source_target_pairs={{0,192},{64,0},{128,64},{192,128},{1,193},{65,1},{129,65},{193,129... | collective-permute-start | bytes 589832 | tf_op jit(solution)/shard_map/ppermute | solution.py:38
  24.4 6.6 %collective-permute-start.7 = (bf16[1,3,32,1024]{3,2,1,0:T(8,128)(2,1)}, bf16[1,3,32,1024]{3,2,1,0:T(8,128)(2,1)S(1)}, u32[]{:S(2)}, u32[]{:S(2)}) collective-permute-start(bf16[1,3,32,1024]{3,2,1,0:T(8,128)(2,1)} %get-tuple-element.74), channel_id=1, source_target_pairs={{0,16},{16,32},{32,48},{48,0},{1,17},{17,33},{33,49},{49,1},{2,18}... | collective-permute-start | bytes 589832 | tf_op jit(solution)/shard_map/ppermute | solution.py:38
  24.4 6.6 %collective-permute-start.8 = (bf16[1,3,32,1024]{3,2,1,0:T(8,128)(2,1)S(1)}, bf16[1,3,32,1024]{3,2,1,0:T(8,128)(2,1)S(1)}, u32[]{:S(2)}, u32[]{:S(2)}) collective-permute-start(bf16[1,3,32,1024]{3,2,1,0:T(8,128)(2,1)S(1)} %get-tuple-element.75), channel_id=1, source_target_pairs={{0,48},{16,0},{32,16},{48,32},{1,49},{17,1},{33,17},{49,33},{2,50}... | collective-permute-start | bytes 589832 | tf_op jit(solution)/shard_map/ppermute | solution.py:38
  31.3 33.1 %collective-permute-start.13 = (bf16[4,2,3,32,1024]{4,3,2,1,0:T(8,128)(2,1)S(1)}, bf16[4,2,3,32,1024]{4,3,2,1,0:T(8,128)(2,1)S(1)}, u32[]{:S(2)}, u32[]{:S(2)}) collective-permute-start(bf16[4,2,3,32,1024]{4,3,2,1,0:T(8,128)(2,1)S(1)} %get-tuple-element.86.refs_4_), channel_id=1, source_target_pairs={{0,16},{16,32},{32,48},{48,0},{1,17},{17,33},{33,49},{49,1},{2,18}... | collective-permute-start | bytes 4718600 | tf_op jit(solution)/shard_map/ppermute | solution.py:38
  31.7 38.3 %collective-permute-start.14 = (bf16[4,2,3,32,1024]{4,3,2,1,0:T(8,128)(2,1)S(1)}, bf16[4,2,3,32,1024]{4,3,2,1,0:T(8,128)(2,1)S(1)}, u32[]{:S(2)}, u32[]{:S(2)}) collective-permute-start(bf16[4,2,3,32,1024]{4,3,2,1,0:T(8,128)(2,1)S(1)} %get-tuple-element.86.refs_4_), channel_id=1, source_target_pairs={{0,48},{16,0},{32,16},{48,32},{1,49},{17,1},{33,17},{49,33},{2,50}... | collective-permute-start | bytes 4718600 | tf_op jit(solution)/shard_map/ppermute | solution.py:38
  34.0 36.0 %collective-permute-start.15 = (bf16[4,2,3,32,1024]{4,3,2,1,0:T(8,128)(2,1)S(1)}, bf16[4,2,3,32,1024]{4,3,2,1,0:T(8,128)(2,1)S(1)}, u32[]{:S(2)}, u32[]{:S(2)}) collective-permute-start(bf16[4,2,3,32,1024]{4,3,2,1,0:T(8,128)(2,1)S(1)} %get-tuple-element.87.refs_7_), channel_id=1, source_target_pairs={{0,64},{64,128},{128,192},{192,0},{1,65},{65,129},{129,193},{193,1... | collective-permute-start | bytes 4718600 | tf_op jit(solution)/shard_map/ppermute | solution.py:38
  34.0 36.0 %collective-permute-start.16 = (bf16[4,2,3,32,1024]{4,3,2,1,0:T(8,128)(2,1)S(1)}, bf16[4,2,3,32,1024]{4,3,2,1,0:T(8,128)(2,1)S(1)}, u32[]{:S(2)}, u32[]{:S(2)}) collective-permute-start(bf16[4,2,3,32,1024]{4,3,2,1,0:T(8,128)(2,1)S(1)} %get-tuple-element.87.refs_7_), channel_id=1, source_target_pairs={{0,192},{64,0},{128,64},{192,128},{1,193},{65,1},{129,65},{193,129... | collective-permute-start | bytes 4718600 | tf_op jit(solution)/shard_map/ppermute | solution.py:38
  36.7 9.4 %collective-permute-start.9 = (bf16[16,32,256]{2,1,0:T(8,128)(2,1)}, bf16[16,32,256]{2,1,0:T(8,128)(2,1)S(1)}, u32[]{:S(2)}, u32[]{:S(2)}) collective-permute-start(bf16[16,32,256]{2,1,0:T(8,128)(2,1)} %all-to-all-done), channel_id=1, source_target_pairs={{0,2},{1,3},{2,0},{3,1},{4,6},{5,7},{6,4},{7,5},{8,10},{9,11},{10,... | collective-permute-start | bytes 786440 | tf_op jit(solution)/shard_map/ppermute | solution.py:360
  47.1 10.9 %collective-permute-start.10 = (bf16[2,16,32,256]{3,2,1,0:T(8,128)(2,1)S(1)}, bf16[2,16,32,256]{3,2,1,0:T(8,128)(2,1)S(1)}, u32[]{:S(2)}, u32[]{:S(2)}) collective-permute-start(bf16[2,16,32,256]{3,2,1,0:T(8,128)(2,1)S(1)} %pad_maximum_fusion.refs_0_), channel_id=1, source_target_pairs={{0,1},{1,0},{2,3},{3,2},{4,5},{5,4},{6,7},{7,6},{8,9},{9,8},{10,11... | collective-permute-start | bytes 1572872 | tf_op jit(solution)/shard_map/ppermute | solution.py:361
  58.0 15.0 %collective-permute-start.11 = (bf16[2,16,32,256]{3,2,1,0:T(8,128)(2,1)S(1)}, bf16[2,16,32,256]{3,2,1,0:T(8,128)(2,1)S(1)}, u32[]{:S(2)}, u32[]{:S(2)}) collective-permute-start(bf16[2,16,32,256]{3,2,1,0:T(8,128)(2,1)S(1)} %pad_maximum_fusion.refs_0_), channel_id=1, source_target_pairs={{0,8},{8,0},{1,9},{9,1},{2,10},{10,2},{3,11},{11,3},{4,12},{12,4},... | collective-permute-start | bytes 1572872 | tf_op jit(solution)/shard_map/ppermute | solution.py:38
  64.4 11.2 %collective-permute-start.12 = (bf16[2,16,32,256]{3,2,1,0:T(8,128)(2,1)S(1)}, bf16[2,16,32,256]{3,2,1,0:T(8,128)(2,1)S(1)}, u32[]{:S(2)}, u32[]{:S(2)}) collective-permute-start(bf16[2,16,32,256]{3,2,1,0:T(8,128)(2,1)S(1)} %collective-permute-done.10.refs_1_), channel_id=1, source_target_pairs={{0,8},{8,0},{1,9},{9,1},{2,10},{10,2},{3,11},{11,3},{4,12},{12,4},... | collective-permute-start | bytes 1572872 | tf_op jit(solution)/shard_map/ppermute | solution.py:38
  70.2 18.3 %collective-permute-start.17 = (bf16[2,2,3,32,1024]{4,3,2,1,0:T(8,128)(2,1)S(1)}, bf16[2,2,3,32,1024]{4,3,2,1,0:T(8,128)(2,1)S(1)}, u32[]{:S(2)}, u32[]{:S(2)}) collective-permute-start(bf16[2,2,3,32,1024]{4,3,2,1,0:T(8,128)(2,1)S(1)} %get-tuple-element.88), channel_id=1, source_target_pairs={{0,16},{16,32},{32,48},{48,0},{1,17},{17,33},{33,49},{49,1},{2,18}... | collective-permute-start | bytes 2359304 | tf_op jit(solution)/shard_map/ppermute | solution.py:38
  70.3 18.2 %collective-permute-start.18 = (bf16[2,2,3,32,1024]{4,3,2,1,0:T(8,128)(2,1)S(1)}, bf16[2,2,3,32,1024]{4,3,2,1,0:T(8,128)(2,1)S(1)}, u32[]{:S(2)}, u32[]{:S(2)}) collective-permute-start(bf16[2,2,3,32,1024]{4,3,2,1,0:T(8,128)(2,1)S(1)} %get-tuple-element.89), channel_id=1, source_target_pairs={{0,48},{16,0},{32,16},{48,32},{1,49},{17,1},{33,17},{49,33},{2,50}... | collective-permute-start | bytes 2359304 | tf_op jit(solution)/shard_map/ppermute | solution.py:38
  72.9 17.6 %collective-permute-start.19 = (bf16[2,2,3,32,1024]{4,3,2,1,0:T(8,128)(2,1)S(1)}, bf16[2,2,3,32,1024]{4,3,2,1,0:T(8,128)(2,1)S(1)}, u32[]{:S(2)}, u32[]{:S(2)}) collective-permute-start(bf16[2,2,3,32,1024]{4,3,2,1,0:T(8,128)(2,1)S(1)} %get-tuple-element.90), channel_id=1, source_target_pairs={{0,64},{64,128},{128,192},{192,0},{1,65},{65,129},{129,193},{193,1... | collective-permute-start | bytes 2359304 | tf_op jit(solution)/shard_map/ppermute | solution.py:38
  73.0 17.6 %collective-permute-start.20 = (bf16[2,2,3,32,1024]{4,3,2,1,0:T(8,128)(2,1)S(1)}, bf16[2,2,3,32,1024]{4,3,2,1,0:T(8,128)(2,1)S(1)}, u32[]{:S(2)}, u32[]{:S(2)}) collective-permute-start(bf16[2,2,3,32,1024]{4,3,2,1,0:T(8,128)(2,1)S(1)} %get-tuple-element.91), channel_id=1, source_target_pairs={{0,192},{64,0},{128,64},{192,128},{1,193},{65,1},{129,65},{193,129... | collective-permute-start | bytes 2359304 | tf_op jit(solution)/shard_map/ppermute | solution.py:38
  93.6 19.8 %collective-permute-start.23 = (bf16[3,2,256,1024]{3,2,1,0:T(8,128)(2,1)S(1)}, bf16[3,2,256,1024]{3,2,1,0:T(8,128)(2,1)S(1)}, u32[]{:S(2)}, u32[]{:S(2)}) collective-permute-start(bf16[3,2,256,1024]{3,2,1,0:T(8,128)(2,1)S(1)} %get-tuple-element.96), channel_id=1, source_target_pairs={{0,8},{8,0},{1,9},{9,1},{2,10},{10,2},{3,11},{11,3},{4,12},{12,4},... | collective-permute-start | bytes 9437192 | tf_op jit(solution)/shard_map/ppermute | solution.py:38
  110.4 2.9 %collective-permute-start.22 = (f32[48,128]{1,0:T(8,128)S(1)}, f32[48,128]{1,0:T(8,128)S(1)}, u32[]{:S(2)}, u32[]{:S(2)}) collective-permute-start(f32[48,128]{1,0:T(8,128)S(1)} %span.1.mine_ref), channel_id=1, source_target_pairs={{0,8},{8,0},{1,9},{9,1},{2,10},{10,2},{3,11},{11,3},{4,12},{12,4},... | collective-permute-start | bytes 73736 | tf_op jit(solution)/shard_map/ppermute | solution.py:38
  (9 other events, 85.8 us)

commit v6 on v5

--- a/solution.py
+++ b/solution.py
@@ -152,11 +152,10 @@
 
 def multiply_kernel(*refs):
     features, total_ref, parts = refs[:4], refs[4], refs[5:9]
-    keep_ref, send_ref, rows_ref, cols_ref, line = refs[9:]
+    keep_ref, send_ref, cols_ref, line = refs[9:]
     depth = line.shape[1]
     tile = line.shape[2]
     for m in range(3):
-        across = [jnp.zeros((ROWS, 128), jnp.float32) for _ in range(2)]
         for step in range(QUART // tile):
             units = slice(step * tile, (step + 1) * tile)
             for route in range(2):
@@ -172,14 +171,10 @@
                     out_ref[m, route, :, units] = grad.astype(jnp.bfloat16)
                     square = grad * grad
                     down += jnp.sum(square, axis=0, keepdims=True)
-                    for k in range(tile // 128):
-                        across[i] += square[:, k * 128 : (k + 1) * 128]
                 for k in range(tile // 128):
                     row = step * (tile // 128) + k
                     row += (m * 2 + route) * 8
                     cols_ref[0, row : row + 1] = down[:, k * 128 : (k + 1) * 128] * SCALE
-        for i, total in enumerate(across):
-            rows_ref[i, m : m + 1] = jnp.sum(total.T, axis=0, keepdims=True) * SCALE
     for i in range(1, XN * YN):
         cols_ref[i] = cols_ref[0]
 
@@ -188,7 +183,6 @@
     outs = [
         ((3, 2, ROWS, QUART), jnp.bfloat16),
         ((3, 2, ROWS, QUART), jnp.bfloat16),
-        ((2, 3, ROWS), jnp.float32),
         ((XN * YN, 48, 128), jnp.float32),
     ]
     depth = TOKENS // 4
@@ -203,17 +197,20 @@
     out_ref[...] = BETA * old_ref[...] + (1.0 - BETA) * (total * (1.0 / D) + EPS)
 
 
-def weigh_kernel(rows_ref, met_ref, mine_ref, other_ref, keep_ref, got_ref, out_ref):
-    out_ref[0, 0:3] = rows_ref[0] + met_ref[...]
+def weigh_kernel(mine_ref, other_ref, keep_ref, got_ref, out_ref):
     for m in range(3):
         total = jnp.zeros((ROWS, 128), jnp.float32)
+        plain = jnp.zeros((ROWS, 128), jnp.float32)
         for ref, span_ref in ((keep_ref, mine_ref), (got_ref, other_ref)):
             for route in range(2):
                 at = (m * 2 + route) * 8
                 inverse = 1.0 / span_ref[at : at + 8]
                 for k in range(8):
                     grad = ref[m, route, :, k * 128 : (k + 1) * 128].astype(jnp.float32)
-                    total += grad * grad * inverse[k : k + 1]
+                    square = grad * grad
+                    plain += square
+                    total += square * inverse[k : k + 1]
+        out_ref[0, m : m + 1] = jnp.sum(plain.T, axis=0, keepdims=True) * SCALE
         out_ref[0, 3 + m : 4 + m] = jnp.sum(total.T, axis=0, keepdims=True) * SCALE
     for i in range(1, ZN):
         out_ref[i] = out_ref[0]
@@ -361,15 +358,14 @@
     met = lax.ppermute(chosen, "z", [(i, i ^ 1) for i in range(ZN)])
     features = arrange(place, chosen, met, swap(chosen), swap(met))
     parts = [lines[0], *near[0], lines[1], *near[1]]
-    keep, send, rows, cols = multiply(features, start(features, parts), [*far[0], *far[1]])
-
-    met = swap(rows[1])
+    keep, send, cols = multiply(features, start(features, parts), [*far[0], *far[1]])
+
     got = swap(send)
 
     parts = collect(cols, ("x", "y"))
     span = whole(span_kernel, "span", [((48, 128), jnp.float32)], (parts, old_span))[0]
     other = swap(span)
-    sums = whole(weigh_kernel, "weigh", [((ZN, 6, ROWS), jnp.float32)], (rows, met, span, other, keep, got))[0]
+    sums = whole(weigh_kernel, "weigh", [((ZN, 6, ROWS), jnp.float32)], (span, other, keep, got))[0]
     parts = collect(sums, ("z",))
     outs = [((3, ROWS), jnp.float32), ((XN * YN * CN, 3, 128), jnp.float32)]
     width, squares = whole(width_kernel, "width", outs, (parts, old_width))

time: 146 us -> 146 us (level)
    ppermute x22 -> x21, waiting for transfers between devices: 16.8 us -> 16.6 us  [shift(): lax.ppermute(value, axis, [(i, (i + step) % size) for i in range(size)])]
    ppermute x22 -> x21, starting transfers between devices: 42.8 us -> 42.9 us  [shift(): lax.ppermute(value, axis, [(i, (i + step) % size) for i in range(size)])]
  transfers between devices with their start and end apart: 25 -> 24, of which waited for: 10 -> 10; matrix products, arithmetic and copies ran while one was open for 1% -> 1% of each run, Pallas kernels for 6% -> 6%
where the time goes in v6:
time: 146 us
  starting transfers between devices  48.4 us (33%)
  blocking collectives  39.4 us (27%)
  waiting for transfers between devices  35.6 us (24%)
  Pallas kernels  18.1 us (12%)
  other arithmetic  2.84 us (2%)
    ppermute x21, starting transfers between devices, shift(): lax.ppermute(value, axis, [(i, (i + step) % size) for i in range(size)])  42.9 us
    all_to_all x3, blocking collectives, collect(): return lax.all_to_all(copies, axes, split_axis=0, concat_axis=0, tiled=True)  39.4 us
    ppermute x21, waiting for transfers between devices, shift(): lax.ppermute(value, axis, [(i, (i + step) % size) for i in range(size)])  16.6 us
    pallas_call x8, Pallas kernels, whole(): pl.pallas_call(kernel, in_specs=[spec] * len(operands), out_specs=[spec]...  10.8 us
    ppermute x1, waiting for transfers between devices, local(): met = lax.ppermute(chosen, 'z', [(i, i ^ 1) for i in range(ZN)])  10.6 us
    ppermute x1, waiting for transfers between devices, local(): lax.ppermute(chosen, 'z', [(i, i ^ 2) for i in range(ZN)])  8.43 us
    pallas_call x1, Pallas kernels, finish(): pl.pallas_call(finish_kernel, in_specs=[pl.BlockSpec(memory_space=pltpu.S...  4.41 us
    all_to_all x1, starting transfers between devices, local(): lax.all_to_all(chosen, ('x', 'y'), split_axis=0, concat_axis=0, tiled=True)  4.2 us
  transfers between devices with their start and end apart: 24, of which 10 were waited for; matrix products, arithmetic and copies ran while one was open for 1% of the time, Pallas kernels for 6%

profile of v6, /device:TPU:1, one launch (start us, length us, event | category | flops | bytes accessed | tf_op | source)
XLA Modules:
  0.0 145.6 jit_solution(12164518298686643379)
XLA Ops:
  2.5 3.3 %collective-permute-start = (bf16[3,32,2048]{2,1,0:T(8,128)(2,1)S(1)}, bf16[3,32,2048]{2,1,0:T(8,128)(2,1)S(1)}, u32[]{:S(2)}, u32[]{:S(2)}) collective-permute-start(bf16[3,32,2048]{2,1,0:T(8,128)(2,1)S(1)} %pad_maximum_fusion.2), channel_id=1, source_target_pairs={{0,8},{8,0},{1,9},{9,1},{2,10},{10,2},{3,11},{11,3},{4,12},{12,4},... | collective-permute-start | bytes 1179656 | tf_op jit(solution)/shard_map/ppermute | solution.py:38
  7.3 2.7 %collective-permute-start.2 = (bf16[2,3,32,1024]{3,2,1,0:T(8,128)(2,1)S(1)}, bf16[2,3,32,1024]{3,2,1,0:T(8,128)(2,1)S(1)}, u32[]{:S(2)}, u32[]{:S(2)}) collective-permute-start(bf16[2,3,32,1024]{3,2,1,0:T(8,128)(2,1)S(1)} %get-tuple-element.64.refs_0_), channel_id=1, source_target_pairs={{0,192},{64,0},{128,64},{192,128},{1,193},{65,1},{129,65},{193,129... | collective-permute-start | bytes 1179656 | tf_op jit(solution)/shard_map/ppermute | solution.py:38
  10.0 2.7 %collective-permute-start.4 = (bf16[2,3,32,1024]{3,2,1,0:T(8,128)(2,1)S(1)}, bf16[2,3,32,1024]{3,2,1,0:T(8,128)(2,1)S(1)}, u32[]{:S(2)}, u32[]{:S(2)}) collective-permute-start(bf16[2,3,32,1024]{3,2,1,0:T(8,128)(2,1)S(1)} %get-tuple-element.65.refs_5_), channel_id=1, source_target_pairs={{0,48},{16,0},{32,16},{48,32},{1,49},{17,1},{33,17},{49,33},{2,50}... | collective-permute-start | bytes 1179656 | tf_op jit(solution)/shard_map/ppermute | solution.py:38
  12.7 4.2 %all-to-all-start = ((bf16[16,32,256]{2,1,0:T(8,128)(2,1)}), bf16[16,32,256]{2,1,0:T(8,128)(2,1)}, u32[]{:S(2)}, u32[]{:S(2)}) async-start(bf16[16,32,256]{2,1,0:T(8,128)(2,1)} %pick.1), calls=%async_computation | async-start | bytes 524288 | tf_op jit(solution)/shard_map/all_to_all | solution.py:349
  21.7 2.7 %collective-permute-start.6 = (bf16[1,3,32,1024]{3,2,1,0:T(8,128)(2,1)}, bf16[1,3,32,1024]{3,2,1,0:T(8,128)(2,1)S(1)}, u32[]{:S(2)}, u32[]{:S(2)}) collective-permute-start(bf16[1,3,32,1024]{3,2,1,0:T(8,128)(2,1)} %get-tuple-element.72), channel_id=1, source_target_pairs={{0,192},{64,0},{128,64},{192,128},{1,193},{65,1},{129,65},{193,129... | collective-permute-start | bytes 589832 | tf_op jit(solution)/shard_map/ppermute | solution.py:38
  24.4 3.1 %collective-permute-start.8 = (bf16[1,3,32,1024]{3,2,1,0:T(8,128)(2,1)S(1)}, bf16[1,3,32,1024]{3,2,1,0:T(8,128)(2,1)S(1)}, u32[]{:S(2)}, u32[]{:S(2)}) collective-permute-start(bf16[1,3,32,1024]{3,2,1,0:T(8,128)(2,1)S(1)} %get-tuple-element.74), channel_id=1, source_target_pairs={{0,48},{16,0},{32,16},{48,32},{1,49},{17,1},{33,17},{49,33},{2,50}... | collective-permute-start | bytes 589832 | tf_op jit(solution)/shard_map/ppermute | solution.py:38
  27.7 3.4 %collective-permute-done.7.refs_8_ = bf16[1,3,32,1024]{3,2,1,0:T(8,128)(2,1)S(1)} collective-permute-done((bf16[1,3,32,1024]{3,2,1,0:T(8,128)(2,1)}, bf16[1,3,32,1024]{3,2,1,0:T(8,128)(2,1)S(1)}, u32[]{:S(2)}, u32[]{:S(2)}) %collective-permute-start.7) | collective-permute-done | bytes 196640 | tf_op jit(solution)/shard_map/ppermute | solution.py:38
  31.7 2.3 %collective-permute-start.14 = (bf16[4,2,3,32,1024]{4,3,2,1,0:T(8,128)(2,1)S(1)}, bf16[4,2,3,32,1024]{4,3,2,1,0:T(8,128)(2,1)S(1)}, u32[]{:S(2)}, u32[]{:S(2)}) collective-permute-start(bf16[4,2,3,32,1024]{4,3,2,1,0:T(8,128)(2,1)S(1)} %get-tuple-element.85.refs_4_), channel_id=1, source_target_pairs={{0,48},{16,0},{32,16},{48,32},{1,49},{17,1},{33,17},{49,33},{2,50}... | collective-permute-start | bytes 4718600 | tf_op jit(solution)/shard_map/ppermute | solution.py:38
  34.0 2.7 %collective-permute-start.16 = (bf16[4,2,3,32,1024]{4,3,2,1,0:T(8,128)(2,1)S(1)}, bf16[4,2,3,32,1024]{4,3,2,1,0:T(8,128)(2,1)S(1)}, u32[]{:S(2)}, u32[]{:S(2)}) collective-permute-start(bf16[4,2,3,32,1024]{4,3,2,1,0:T(8,128)(2,1)S(1)} %get-tuple-element.86.refs_7_), channel_id=1, source_target_pairs={{0,192},{64,0},{128,64},{192,128},{1,193},{65,1},{129,65},{193,129... | collective-permute-start | bytes 4718600 | tf_op jit(solution)/shard_map/ppermute | solution.py:38
  37.7 8.4 %collective-permute-done.9 = bf16[16,32,256]{2,1,0:T(8,128)(2,1)S(1)} collective-permute-done((bf16[16,32,256]{2,1,0:T(8,128)(2,1)}, bf16[16,32,256]{2,1,0:T(8,128)(2,1)S(1)}, u32[]{:S(2)}, u32[]{:S(2)}) %collective-permute-start.9) | collective-permute-done | bytes 262176 | tf_op jit(solution)/shard_map/ppermute | solution.py:357
  47.4 10.6 %collective-permute-done.10.refs_1_ = bf16[2,16,32,256]{3,2,1,0:T(8,128)(2,1)S(1)} collective-permute-done((bf16[2,16,32,256]{3,2,1,0:T(8,128)(2,1)S(1)}, bf16[2,16,32,256]{3,2,1,0:T(8,128)(2,1)S(1)}, u32[]{:S(2)}, u32[]{:S(2)}) %collective-permute-start.10) | collective-permute-done | bytes 524320 | tf_op jit(solution)/shard_map/ppermute | solution.py:358
  58.0 6.4 %collective-permute-start.11 = (bf16[2,16,32,256]{3,2,1,0:T(8,128)(2,1)S(1)}, bf16[2,16,32,256]{3,2,1,0:T(8,128)(2,1)S(1)}, u32[]{:S(2)}, u32[]{:S(2)}) collective-permute-start(bf16[2,16,32,256]{3,2,1,0:T(8,128)(2,1)S(1)} %pad_maximum_fusion.refs_0_), channel_id=1, source_target_pairs={{0,8},{8,0},{1,9},{9,1},{2,10},{10,2},{3,11},{11,3},{4,12},{12,4},... | collective-permute-start | bytes 1572872 | tf_op jit(solution)/shard_map/ppermute | solution.py:38
  64.4 5.6 %collective-permute-start.12 = (bf16[2,16,32,256]{3,2,1,0:T(8,128)(2,1)S(1)}, bf16[2,16,32,256]{3,2,1,0:T(8,128)(2,1)S(1)}, u32[]{:S(2)}, u32[]{:S(2)}) collective-permute-start(bf16[2,16,32,256]{3,2,1,0:T(8,128)(2,1)S(1)} %collective-permute-done.10.refs_1_), channel_id=1, source_target_pairs={{0,8},{8,0},{1,9},{9,1},{2,10},{10,2},{3,11},{11,3},{4,12},{12,4},... | collective-permute-start | bytes 1572872 | tf_op jit(solution)/shard_map/ppermute | solution.py:38
  70.3 2.7 %collective-permute-start.18 = (bf16[2,2,3,32,1024]{4,3,2,1,0:T(8,128)(2,1)S(1)}, bf16[2,2,3,32,1024]{4,3,2,1,0:T(8,128)(2,1)S(1)}, u32[]{:S(2)}, u32[]{:S(2)}) collective-permute-start(bf16[2,2,3,32,1024]{4,3,2,1,0:T(8,128)(2,1)S(1)} %get-tuple-element.88), channel_id=1, source_target_pairs={{0,48},{16,0},{32,16},{48,32},{1,49},{17,1},{33,17},{49,33},{2,50}... | collective-permute-start | bytes 2359304 | tf_op jit(solution)/shard_map/ppermute | solution.py:38
  73.0 2.7 %collective-permute-start.20 = (bf16[2,2,3,32,1024]{4,3,2,1,0:T(8,128)(2,1)S(1)}, bf16[2,2,3,32,1024]{4,3,2,1,0:T(8,128)(2,1)S(1)}, u32[]{:S(2)}, u32[]{:S(2)}) collective-permute-start(bf16[2,2,3,32,1024]{4,3,2,1,0:T(8,128)(2,1)S(1)} %get-tuple-element.90), channel_id=1, source_target_pairs={{0,192},{64,0},{128,64},{192,128},{1,193},{65,1},{129,65},{193,129... | collective-permute-start | bytes 2359304 | tf_op jit(solution)/shard_map/ppermute | solution.py:38
  77.4 5.1 %start.1.refs_4_ = f32[3,2,512,1024]{3,2,1,0:T(8,128)S(1)} custom-call(bf16[512,1024]{1,0:T(8,128)(2,1)S(1)} %get-tuple-element.77.refs_0_, bf16[512,1024]{1,0:T(8,128)(2,1)S(1)} %get-tuple-element.78.refs_1_, bf16[512,1024]{1,0:T(8,128)(2,1)S(1)} %get-tuple-element.79.refs_2_, bf16[512,1024]{1,0:T(8,128)(2,1)S(1)} %get-tuple-element.80.refs_3_, ...), custom_call_target="tpu_custom_call" | custom-call | flops 4831838208 | bytes 13631488 | tf_op jit(solution)/shard_map/start/pallas_call | solution.py:56
  82.5 6.0 %collective-permute-done.17.refs_5_ = bf16[2,2,3,32,1024]{4,3,2,1,0:T(8,128)(2,1)S(1)} collective-permute-done((bf16[2,2,3,32,1024]{4,3,2,1,0:T(8,128)(2,1)S(1)}, bf16[2,2,3,32,1024]{4,3,2,1,0:T(8,128)(2,1)S(1)}, u32[]{:S(2)}, u32[]{:S(2)}) %collective-permute-start.17) | collective-permute-done | bytes 786464 | tf_op jit(solution)/shard_map/ppermute | solution.py:38
  90.6 2.2 %multiply.1 = (bf16[3,2,256,1024]{3,2,1,0:T(8,128)(2,1)S(1)}, bf16[3,2,256,1024]{3,2,1,0:T(8,128)(2,1)S(1)}, f32[16,48,128]{2,1,0:T(8,128)S(1)}) custom-call(bf16[512,1024]{1,0:T(8,128)(2,1)S(1)} %get-tuple-element.77.refs_0_, bf16[512,1024]{1,0:T(8,128)(2,1)S(1)} %get-tuple-element.78.refs_1_, bf16[512,1024]{1,0:T(8,128)(2,1)S(1)} %get-tuple-element.79.refs_2_, ...), custom_call_target="tpu_custom_call" | custom-call | flops 1610612736 | bytes 19922944 | tf_op jit(solution)/shard_map/multiply/pallas_call | solution.py:56
  92.7 3.9 %collective-permute-start.22 = (bf16[3,2,256,1024]{3,2,1,0:T(8,128)(2,1)S(1)}, bf16[3,2,256,1024]{3,2,1,0:T(8,128)(2,1)S(1)}, u32[]{:S(2)}, u32[]{:S(2)}) collective-permute-start(bf16[3,2,256,1024]{3,2,1,0:T(8,128)(2,1)S(1)} %get-tuple-element.94), channel_id=1, source_target_pairs={{0,8},{8,0},{1,9},{9,1},{2,10},{10,2},{3,11},{11,3},{4,12},{12,4},... | collective-permute-start | bytes 9437192 | tf_op jit(solution)/shard_map/ppermute | solution.py:38
  96.6 13.2 %all_to_all.20.parts_ref = f32[16,48,128]{2,1,0:T(8,128)S(1)} all-to-all(f32[16,48,128]{2,1,0:T(8,128)S(1)} %get-tuple-element.91), channel_id=1, replica_groups=mesh['x'=4,'y'=4,'c'=2,'z'=8] {'x','y'}, dimensions={0} | all-to-all | bytes 786432 | tf_op jit(solution)/shard_map/all_to_all | solution.py:82
  112.4 2.3 %weigh.1 = f32[8,6,256]{2,1,0:T(8,128)S(1)} custom-call(f32[48,128]{1,0:T(8,128)S(1)} %span.1.mine_ref, f32[48,128]{1,0:T(8,128)S(1)} %collective-permute-done.21.other_ref, bf16[3,2,256,1024]{3,2,1,0:T(8,128)(2,1)S(1)} %get-tuple-element.93.keep_ref, bf16[3,2,256,1024]{3,2,1,0:T(8,128)(2,1)S(1)} %collective-permute-done.22.got_ref), custom_call_target="tpu_custom_call" | custom-call | bytes 6340608 | tf_op jit(solution)/shard_map/weigh/pallas_call | solution.py:56
  114.7 13.5 %all_to_all.21.parts_ref = f32[8,6,256]{2,1,0:T(8,128)S(1)} all-to-all(f32[8,6,256]{2,1,0:T(8,128)S(1)} %weigh.1), channel_id=1, replica_groups=mesh['x'=4,'y'=4,'c'=2,'z'=8] {'z'}, dimensions={0} | all-to-all | bytes 98304 | tf_op jit(solution)/shard_map/all_to_all | solution.py:82
  128.3 12.7 %all_to_all.22.parts_ref = f32[32,3,128]{2,1,0:T(4,128)S(1)} all-to-all(f32[32,3,128]{2,1,0:T(4,128)S(1)} %get-tuple-element.96), channel_id=1, replica_groups=mesh['x'=4,'y'=4,'c'=2,'z'=8] {'x','y','c'}, dimensions={0} | all-to-all | bytes 98304 | tf_op jit(solution)/shard_map/all_to_all | solution.py:82
  141.0 4.4 %finish.1 = (bf16[256,4096]{1,0:T(8,128)(2,1)}, bf16[256,4096]{1,0:T(8,128)(2,1)}, bf16[4096,256]{1,0:T(8,128)(2,1)}, f32[1,256]{1,0:T(1,128)}, f32[1,256]{1,0:T...) custom-call(s32[1]{0:T(128)} %bitcast.core_ref, ...), custom_call_target="tpu_custom_call" | custom-call | flops 12582912 | bytes 12582912 | tf_op jit(solution)/shard_map/finish/pallas_call | solution.py:269
  (63 shorter events, 18.0 us)
Async XLA Ops:
  2.5 4.7 %collective-permute-start = (bf16[3,32,2048]{2,1,0:T(8,128)(2,1)S(1)}, bf16[3,32,2048]{2,1,0:T(8,128)(2,1)S(1)}, u32[]{:S(2)}, u32[]{:S(2)}) collective-permute-start(bf16[3,32,2048]{2,1,0:T(8,128)(2,1)S(1)} %pad_maximum_fusion.2), channel_id=1, source_target_pairs={{0,8},{8,0},{1,9},{9,1},{2,10},{10,2},{3,11},{11,3},{4,12},{12,4},... | collective-permute-start | bytes 1179656 | tf_op jit(solution)/shard_map/ppermute | solution.py:38
  7.2 11.6 %collective-permute-start.1 = (bf16[2,3,32,1024]{3,2,1,0:T(8,128)(2,1)S(1)}, bf16[2,3,32,1024]{3,2,1,0:T(8,128)(2,1)S(1)}, u32[]{:S(2)}, u32[]{:S(2)}) collective-permute-start(bf16[2,3,32,1024]{3,2,1,0:T(8,128)(2,1)S(1)} %get-tuple-element.64.refs_0_), channel_id=1, source_target_pairs={{0,64},{64,128},{128,192},{192,0},{1,65},{65,129},{129,193},{193,1... | collective-permute-start | bytes 1179656 | tf_op jit(solution)/shard_map/ppermute | solution.py:38
  7.3 11.5 %collective-permute-start.2 = (bf16[2,3,32,1024]{3,2,1,0:T(8,128)(2,1)S(1)}, bf16[2,3,32,1024]{3,2,1,0:T(8,128)(2,1)S(1)}, u32[]{:S(2)}, u32[]{:S(2)}) collective-permute-start(bf16[2,3,32,1024]{3,2,1,0:T(8,128)(2,1)S(1)} %get-tuple-element.64.refs_0_), channel_id=1, source_target_pairs={{0,192},{64,0},{128,64},{192,128},{1,193},{65,1},{129,65},{193,129... | collective-permute-start | bytes 1179656 | tf_op jit(solution)/shard_map/ppermute | solution.py:38
  10.0 10.9 %collective-permute-start.3 = (bf16[2,3,32,1024]{3,2,1,0:T(8,128)(2,1)S(1)}, bf16[2,3,32,1024]{3,2,1,0:T(8,128)(2,1)S(1)}, u32[]{:S(2)}, u32[]{:S(2)}) collective-permute-start(bf16[2,3,32,1024]{3,2,1,0:T(8,128)(2,1)S(1)} %get-tuple-element.65.refs_5_), channel_id=1, source_target_pairs={{0,16},{16,32},{32,48},{48,0},{1,17},{17,33},{33,49},{49,1},{2,18}... | collective-permute-start | bytes 1179656 | tf_op jit(solution)/shard_map/ppermute | solution.py:38
  10.0 10.9 %collective-permute-start.4 = (bf16[2,3,32,1024]{3,2,1,0:T(8,128)(2,1)S(1)}, bf16[2,3,32,1024]{3,2,1,0:T(8,128)(2,1)S(1)}, u32[]{:S(2)}, u32[]{:S(2)}) collective-permute-start(bf16[2,3,32,1024]{3,2,1,0:T(8,128)(2,1)S(1)} %get-tuple-element.65.refs_5_), channel_id=1, source_target_pairs={{0,48},{16,0},{32,16},{48,32},{1,49},{17,1},{33,17},{49,33},{2,50}... | collective-permute-start | bytes 1179656 | tf_op jit(solution)/shard_map/ppermute | solution.py:38
  12.7 14.8 %all-to-all-start = ((bf16[16,32,256]{2,1,0:T(8,128)(2,1)}), bf16[16,32,256]{2,1,0:T(8,128)(2,1)}, u32[]{:S(2)}, u32[]{:S(2)}) async-start(bf16[16,32,256]{2,1,0:T(8,128)(2,1)} %pick.1), calls=%async_computation | async-start | bytes 524288 | tf_op jit(solution)/shard_map/all_to_all | solution.py:349
  21.7 5.9 %collective-permute-start.5 = (bf16[1,3,32,1024]{3,2,1,0:T(8,128)(2,1)}, bf16[1,3,32,1024]{3,2,1,0:T(8,128)(2,1)S(1)}, u32[]{:S(2)}, u32[]{:S(2)}) collective-permute-start(bf16[1,3,32,1024]{3,2,1,0:T(8,128)(2,1)} %get-tuple-element.71), channel_id=1, source_target_pairs={{0,64},{64,128},{128,192},{192,0},{1,65},{65,129},{129,193},{193,1... | collective-permute-start | bytes 589832 | tf_op jit(solution)/shard_map/ppermute | solution.py:38
  21.7 5.9 %collective-permute-start.6 = (bf16[1,3,32,1024]{3,2,1,0:T(8,128)(2,1)}, bf16[1,3,32,1024]{3,2,1,0:T(8,128)(2,1)S(1)}, u32[]{:S(2)}, u32[]{:S(2)}) collective-permute-start(bf16[1,3,32,1024]{3,2,1,0:T(8,128)(2,1)} %get-tuple-element.72), channel_id=1, source_target_pairs={{0,192},{64,0},{128,64},{192,128},{1,193},{65,1},{129,65},{193,129... | collective-permute-start | bytes 589832 | tf_op jit(solution)/shard_map/ppermute | solution.py:38
  24.4 6.6 %collective-permute-start.7 = (bf16[1,3,32,1024]{3,2,1,0:T(8,128)(2,1)}, bf16[1,3,32,1024]{3,2,1,0:T(8,128)(2,1)S(1)}, u32[]{:S(2)}, u32[]{:S(2)}) collective-permute-start(bf16[1,3,32,1024]{3,2,1,0:T(8,128)(2,1)} %get-tuple-element.73), channel_id=1, source_target_pairs={{0,16},{16,32},{32,48},{48,0},{1,17},{17,33},{33,49},{49,1},{2,18}... | collective-permute-start | bytes 589832 | tf_op jit(solution)/shard_map/ppermute | solution.py:38
  24.4 6.6 %collective-permute-start.8 = (bf16[1,3,32,1024]{3,2,1,0:T(8,128)(2,1)S(1)}, bf16[1,3,32,1024]{3,2,1,0:T(8,128)(2,1)S(1)}, u32[]{:S(2)}, u32[]{:S(2)}) collective-permute-start(bf16[1,3,32,1024]{3,2,1,0:T(8,128)(2,1)S(1)} %get-tuple-element.74), channel_id=1, source_target_pairs={{0,48},{16,0},{32,16},{48,32},{1,49},{17,1},{33,17},{49,33},{2,50}... | collective-permute-start | bytes 589832 | tf_op jit(solution)/shard_map/ppermute | solution.py:38
  31.3 33.1 %collective-permute-start.13 = (bf16[4,2,3,32,1024]{4,3,2,1,0:T(8,128)(2,1)S(1)}, bf16[4,2,3,32,1024]{4,3,2,1,0:T(8,128)(2,1)S(1)}, u32[]{:S(2)}, u32[]{:S(2)}) collective-permute-start(bf16[4,2,3,32,1024]{4,3,2,1,0:T(8,128)(2,1)S(1)} %get-tuple-element.85.refs_4_), channel_id=1, source_target_pairs={{0,16},{16,32},{32,48},{48,0},{1,17},{17,33},{33,49},{49,1},{2,18}... | collective-permute-start | bytes 4718600 | tf_op jit(solution)/shard_map/ppermute | solution.py:38
  31.7 38.3 %collective-permute-start.14 = (bf16[4,2,3,32,1024]{4,3,2,1,0:T(8,128)(2,1)S(1)}, bf16[4,2,3,32,1024]{4,3,2,1,0:T(8,128)(2,1)S(1)}, u32[]{:S(2)}, u32[]{:S(2)}) collective-permute-start(bf16[4,2,3,32,1024]{4,3,2,1,0:T(8,128)(2,1)S(1)} %get-tuple-element.85.refs_4_), channel_id=1, source_target_pairs={{0,48},{16,0},{32,16},{48,32},{1,49},{17,1},{33,17},{49,33},{2,50}... | collective-permute-start | bytes 4718600 | tf_op jit(solution)/shard_map/ppermute | solution.py:38
  34.0 36.0 %collective-permute-start.15 = (bf16[4,2,3,32,1024]{4,3,2,1,0:T(8,128)(2,1)S(1)}, bf16[4,2,3,32,1024]{4,3,2,1,0:T(8,128)(2,1)S(1)}, u32[]{:S(2)}, u32[]{:S(2)}) collective-permute-start(bf16[4,2,3,32,1024]{4,3,2,1,0:T(8,128)(2,1)S(1)} %get-tuple-element.86.refs_7_), channel_id=1, source_target_pairs={{0,64},{64,128},{128,192},{192,0},{1,65},{65,129},{129,193},{193,1... | collective-permute-start | bytes 4718600 | tf_op jit(solution)/shard_map/ppermute | solution.py:38
  34.0 36.0 %collective-permute-start.16 = (bf16[4,2,3,32,1024]{4,3,2,1,0:T(8,128)(2,1)S(1)}, bf16[4,2,3,32,1024]{4,3,2,1,0:T(8,128)(2,1)S(1)}, u32[]{:S(2)}, u32[]{:S(2)}) collective-permute-start(bf16[4,2,3,32,1024]{4,3,2,1,0:T(8,128)(2,1)S(1)} %get-tuple-element.86.refs_7_), channel_id=1, source_target_pairs={{0,192},{64,0},{128,64},{192,128},{1,193},{65,1},{129,65},{193,129... | collective-permute-start | bytes 4718600 | tf_op jit(solution)/shard_map/ppermute | solution.py:38
  36.7 9.4 %collective-permute-start.9 = (bf16[16,32,256]{2,1,0:T(8,128)(2,1)}, bf16[16,32,256]{2,1,0:T(8,128)(2,1)S(1)}, u32[]{:S(2)}, u32[]{:S(2)}) collective-permute-start(bf16[16,32,256]{2,1,0:T(8,128)(2,1)} %all-to-all-done), channel_id=1, source_target_pairs={{0,2},{1,3},{2,0},{3,1},{4,6},{5,7},{6,4},{7,5},{8,10},{9,11},{10,... | collective-permute-start | bytes 786440 | tf_op jit(solution)/shard_map/ppermute | solution.py:357
  47.1 10.9 %collective-permute-start.10 = (bf16[2,16,32,256]{3,2,1,0:T(8,128)(2,1)S(1)}, bf16[2,16,32,256]{3,2,1,0:T(8,128)(2,1)S(1)}, u32[]{:S(2)}, u32[]{:S(2)}) collective-permute-start(bf16[2,16,32,256]{3,2,1,0:T(8,128)(2,1)S(1)} %pad_maximum_fusion.refs_0_), channel_id=1, source_target_pairs={{0,1},{1,0},{2,3},{3,2},{4,5},{5,4},{6,7},{7,6},{8,9},{9,8},{10,11... | collective-permute-start | bytes 1572872 | tf_op jit(solution)/shard_map/ppermute | solution.py:358
  58.0 15.0 %collective-permute-start.11 = (bf16[2,16,32,256]{3,2,1,0:T(8,128)(2,1)S(1)}, bf16[2,16,32,256]{3,2,1,0:T(8,128)(2,1)S(1)}, u32[]{:S(2)}, u32[]{:S(2)}) collective-permute-start(bf16[2,16,32,256]{3,2,1,0:T(8,128)(2,1)S(1)} %pad_maximum_fusion.refs_0_), channel_id=1, source_target_pairs={{0,8},{8,0},{1,9},{9,1},{2,10},{10,2},{3,11},{11,3},{4,12},{12,4},... | collective-permute-start | bytes 1572872 | tf_op jit(solution)/shard_map/ppermute | solution.py:38
  64.4 11.2 %collective-permute-start.12 = (bf16[2,16,32,256]{3,2,1,0:T(8,128)(2,1)S(1)}, bf16[2,16,32,256]{3,2,1,0:T(8,128)(2,1)S(1)}, u32[]{:S(2)}, u32[]{:S(2)}) collective-permute-start(bf16[2,16,32,256]{3,2,1,0:T(8,128)(2,1)S(1)} %collective-permute-done.10.refs_1_), channel_id=1, source_target_pairs={{0,8},{8,0},{1,9},{9,1},{2,10},{10,2},{3,11},{11,3},{4,12},{12,4},... | collective-permute-start | bytes 1572872 | tf_op jit(solution)/shard_map/ppermute | solution.py:38
  70.2 18.3 %collective-permute-start.17 = (bf16[2,2,3,32,1024]{4,3,2,1,0:T(8,128)(2,1)S(1)}, bf16[2,2,3,32,1024]{4,3,2,1,0:T(8,128)(2,1)S(1)}, u32[]{:S(2)}, u32[]{:S(2)}) collective-permute-start(bf16[2,2,3,32,1024]{4,3,2,1,0:T(8,128)(2,1)S(1)} %get-tuple-element.87), channel_id=1, source_target_pairs={{0,16},{16,32},{32,48},{48,0},{1,17},{17,33},{33,49},{49,1},{2,18}... | collective-permute-start | bytes 2359304 | tf_op jit(solution)/shard_map/ppermute | solution.py:38
  70.3 18.2 %collective-permute-start.18 = (bf16[2,2,3,32,1024]{4,3,2,1,0:T(8,128)(2,1)S(1)}, bf16[2,2,3,32,1024]{4,3,2,1,0:T(8,128)(2,1)S(1)}, u32[]{:S(2)}, u32[]{:S(2)}) collective-permute-start(bf16[2,2,3,32,1024]{4,3,2,1,0:T(8,128)(2,1)S(1)} %get-tuple-element.88), channel_id=1, source_target_pairs={{0,48},{16,0},{32,16},{48,32},{1,49},{17,1},{33,17},{49,33},{2,50}... | collective-permute-start | bytes 2359304 | tf_op jit(solution)/shard_map/ppermute | solution.py:38
  72.9 17.6 %collective-permute-start.19 = (bf16[2,2,3,32,1024]{4,3,2,1,0:T(8,128)(2,1)S(1)}, bf16[2,2,3,32,1024]{4,3,2,1,0:T(8,128)(2,1)S(1)}, u32[]{:S(2)}, u32[]{:S(2)}) collective-permute-start(bf16[2,2,3,32,1024]{4,3,2,1,0:T(8,128)(2,1)S(1)} %get-tuple-element.89), channel_id=1, source_target_pairs={{0,64},{64,128},{128,192},{192,0},{1,65},{65,129},{129,193},{193,1... | collective-permute-start | bytes 2359304 | tf_op jit(solution)/shard_map/ppermute | solution.py:38
  73.0 17.6 %collective-permute-start.20 = (bf16[2,2,3,32,1024]{4,3,2,1,0:T(8,128)(2,1)S(1)}, bf16[2,2,3,32,1024]{4,3,2,1,0:T(8,128)(2,1)S(1)}, u32[]{:S(2)}, u32[]{:S(2)}) collective-permute-start(bf16[2,2,3,32,1024]{4,3,2,1,0:T(8,128)(2,1)S(1)} %get-tuple-element.90), channel_id=1, source_target_pairs={{0,192},{64,0},{128,64},{192,128},{1,193},{65,1},{129,65},{193,129... | collective-permute-start | bytes 2359304 | tf_op jit(solution)/shard_map/ppermute | solution.py:38
  92.7 19.7 %collective-permute-start.22 = (bf16[3,2,256,1024]{3,2,1,0:T(8,128)(2,1)S(1)}, bf16[3,2,256,1024]{3,2,1,0:T(8,128)(2,1)S(1)}, u32[]{:S(2)}, u32[]{:S(2)}) collective-permute-start(bf16[3,2,256,1024]{3,2,1,0:T(8,128)(2,1)S(1)} %get-tuple-element.94), channel_id=1, source_target_pairs={{0,8},{8,0},{1,9},{9,1},{2,10},{10,2},{3,11},{11,3},{4,12},{12,4},... | collective-permute-start | bytes 9437192 | tf_op jit(solution)/shard_map/ppermute | solution.py:38
  109.8 2.6 %collective-permute-start.21 = (f32[48,128]{1,0:T(8,128)S(1)}, f32[48,128]{1,0:T(8,128)S(1)}, u32[]{:S(2)}, u32[]{:S(2)}) collective-permute-start(f32[48,128]{1,0:T(8,128)S(1)} %span.1.mine_ref), channel_id=1, source_target_pairs={{0,8},{8,0},{1,9},{9,1},{2,10},{10,2},{3,11},{11,3},{4,12},{12,4},... | collective-permute-start | bytes 73736 | tf_op jit(solution)/shard_map/ppermute | solution.py:38
  (8 other events, 84.6 us)
